TPU v7x, 32 devices: a whole 2x2x4 slice. The times are simulated.
32 devices in a mesh: shard: 4 (over z), ctx: 4 (over x, core), tp: 2 (over y).
Axes of the slice: x: 2, y: 2, z: 4, core: 2. Of those that a mesh axis runs over, the one named last changes fastest.
Arguments:
- tokens: bfloat16 [2048, 768], P(('shard', 'ctx')), may hold values from -6 to 6
- timesteps: int32 [4, 9], P('shard'), may hold values from 0 to 999
- cont_lengths: int32 [4, 8], P('shard'), may hold values from 1 to 128, 256 in all within a row
- table: bfloat16 [1000, 768], P(None, ('shard', 'ctx')), may hold values from -3 to 3
- w_qkv: bfloat16 [2, 768, 3, 768], P(None, ('shard', 'ctx'), None, 'tp'), may hold values from -0.21875 to 0.21875
- w_out: bfloat16 [2, 768, 768], P(None, ('shard', 'ctx'), 'tp'), may hold values from -2.5 to 2.5
- w_up: bfloat16 [2, 768, 3072], P(None, ('shard', 'ctx'), 'tp'), may hold values from -0.21875 to 0.21875
- w_down: bfloat16 [2, 768, 3072], P(None, ('shard', 'ctx'), 'tp'), may hold values from -0.109375 to 0.109375
- norms: bfloat16 [2, 768, 2], P(None, ('shard', 'ctx')), may hold values from 0.099609375 to 1.8984375
- query_bias: bfloat16 [2, 768], P(None, 'tp'), may hold values from -3 to 3
- value_bias: bfloat16 [2, 768], P(None, 'tp'), may hold values from -0.1796875 to 0.1796875
- up_bias: bfloat16 [2, 3072], P(None, 'tp'), may hold values from -3 to 3
- out_biases: bfloat16 [2, 768, 2], P(None, ('shard', 'ctx')), may hold values from -3 to 3
- cotangent: bfloat16 [2048, 768], P(('shard', 'ctx')), may hold values from -6 to 6
Outputs:
- activations: bfloat16 [2048, 768], P(('shard', 'ctx'))
- grad_tokens: float32 [2048, 768], P(('shard', 'ctx'))
- grad_qkv: float32 [2, 768, 3, 768], P(None, ('shard', 'ctx'), None, 'tp')
- grad_out: float32 [2, 768, 768], P(None, ('shard', 'ctx'), 'tp')
- grad_up: float32 [2, 768, 3072], P(None, ('shard', 'ctx'), 'tp')
- grad_down: float32 [2, 768, 3072], P(None, ('shard', 'ctx'), 'tp')
- grad_norms: float32 [2, 768, 2], P(None, ('shard', 'ctx'))
- grad_table: float32 [1000, 768], P(None, ('shard', 'ctx'))
- grad_query_bias: float32 [2, 768], P(None, 'tp')
- grad_value_bias: float32 [2, 768], P(None, 'tp')
- grad_up_bias: float32 [2, 3072], P(None, 'tp')
- grad_out_biases: float32 [2, 768, 2], P(None, ('shard', 'ctx'))
Inputs may be any that keep to these rules, and one draw needn't show every extreme that they name: `cont_lengths`: the lengths of each group sum to half of 512, and the largest of each group is exactly 128.
All inputs are finite; a program needn't handle non-finite values.
Results may differ from a plain program's by a relative error of at most 0.014.
Values may be sent and summed in bfloat16 or wider, within the bound.
No kernel may reach another device: no remote copies, remote signals or barrier semaphores. Data moves between devices by JAX's collectives and lax.ppermute only.
A program may use at most 192 MiB of HBM per device.

v0:
```python
import math

import jax
import jax.numpy as jnp
from jax import lax
from jax.sharding import PartitionSpec as P

HEAD_DIM = 64


EPSILON = 1e-05
PRECISE = lax.Precision.HIGHEST
NEGATIVE = -1e30


def split_up(array, dim, devices):
    before, after = (array.shape[:dim], array.shape[dim + 1 :])
    return jnp.moveaxis(array.reshape(*before, devices, -1, *after), dim, 0)


def sum_at_owner(array, axis, dim):
    devices = lax.axis_size(axis)
    tiles = lax.all_to_all(split_up(array, dim, devices), axis, 0, 0, tiled=True)
    return jnp.sum(tiles.astype(jnp.float32), axis=0)


def layer_norm(values, gain_vec):
    row_mean = jnp.mean(values, axis=-1, keepdims=True)
    centered = values - row_mean
    row_var = jnp.mean(centered * centered, axis=-1, keepdims=True)
    return centered * lax.rsqrt(row_var + EPSILON) * gain_vec


def gelu_exact(values):
    return jax.nn.gelu(values, approximate=False)


def group_segments(lengths, group_len, prompt_len):
    seq_ends = jnp.cumsum(lengths)
    position = jnp.arange(group_len, dtype=jnp.int32) - prompt_len
    passed = (position[:, None] >= seq_ends[None, :]).astype(jnp.int32)
    seg_ids = 1 + jnp.sum(passed, axis=1)
    return jnp.where(position < 0, 0, seg_ids)


def key_mask(seg_queries, seg_keys):
    return (seg_keys[None, :] == 0) | (seg_keys[None, :] == seg_queries[:, None])


def head_split(flat_rows, row_span, heads_here, head_dim):
    return flat_rows.reshape(row_span, heads_here, head_dim).transpose(1, 0, 2)


def head_merge(split_rows):
    return split_rows.transpose(1, 0, 2).reshape(
        split_rows.shape[1], split_rows.shape[0] * split_rows.shape[2]
    )


def stack_part(entries, position):
    return jnp.stack([entry[position] for entry in entries])


def per_device(
    tokens,
    timesteps,
    cont_lengths,
    table,
    w_qkv,
    w_out,
    w_up,
    w_down,
    norms,
    query_bias,
    value_bias,
    up_bias,
    out_biases,
    cotangent,
):
    row_count = tokens.shape[0]
    layer_count = w_qkv.shape[0]
    local_width = w_qkv.shape[3]
    head_dim = HEAD_DIM
    heads_here = local_width // head_dim
    score_scale = 1.0 / math.sqrt(head_dim)
    group_len = row_count * lax.axis_size("ctx")
    seg_all = group_segments(cont_lengths[0], group_len, group_len // 2)
    seg_here = lax.dynamic_slice_in_dim(seg_all, lax.axis_index("ctx") * row_count, row_count)
    mask_here = key_mask(seg_here, seg_all)
    seq_count = cont_lengths.shape[1] + 1
    member = (seg_here[:, None] == jnp.arange(seq_count, dtype=jnp.int32)[None, :]).astype(
        jnp.float32
    )
    step_rows = timesteps[0][:, None] == jnp.arange(table.shape[0], dtype=jnp.int32)[None, :]
    full_table = lax.all_gather(table, ("shard", "ctx"), axis=1, tiled=True)
    seq_embed = jnp.dot(
        step_rows.astype(jnp.bfloat16), full_table, preferred_element_type=jnp.float32
    )
    x_now = tokens.astype(jnp.float32) + jnp.dot(member, seq_embed, precision=PRECISE)

    def layer_weights(layer_index):
        return (
            lax.all_gather(w_qkv[layer_index], ("shard", "ctx"), axis=0, tiled=True),
            lax.all_gather(w_out[layer_index], ("shard", "ctx"), axis=0, tiled=True),
            lax.all_gather(w_up[layer_index], ("shard", "ctx"), axis=0, tiled=True),
            lax.all_gather(w_down[layer_index], ("shard", "ctx"), axis=0, tiled=True),
            lax.all_gather(norms[layer_index], ("shard", "ctx"), axis=0, tiled=True),
            lax.all_gather(out_biases[layer_index], ("shard", "ctx"), axis=0, tiled=True),
        )

    def tensor_sum(term_value):
        return lax.psum(term_value.astype(jnp.bfloat16), "tp").astype(jnp.float32)

    def probs_and_grads(q_one, k_one, v_one, d_one, total_one, allowed):
        scores = (
            jnp.einsum("qd,kd->qk", q_one, k_one, preferred_element_type=jnp.float32) * score_scale
        )
        attn_prob = jnp.where(allowed, jnp.exp(scores - total_one[:, None]), 0.0)
        prob_grad = jnp.einsum("qd,kd->qk", d_one, v_one, preferred_element_type=jnp.float32)
        return (attn_prob, prob_grad)

    def attend(query_b, kv_all):
        q_heads = head_split(query_b, row_count, heads_here, head_dim)
        k_heads = head_split(kv_all[0], group_len, heads_here, head_dim)
        v_heads = head_split(kv_all[1], group_len, heads_here, head_dim)

        def per_head(bundle):
            q_one, k_one, v_one = bundle
            scores = (
                jnp.einsum("qd,kd->qk", q_one, k_one, preferred_element_type=jnp.float32)
                * score_scale
            )
            scores = jnp.where(mask_here, scores, NEGATIVE)
            row_top = jnp.max(scores, axis=1, keepdims=True)
            weights_exp = jnp.exp(scores - row_top)
            row_total = jnp.sum(weights_exp, axis=1, keepdims=True)
            prob_b = (weights_exp / row_total).astype(jnp.bfloat16)
            head_out = jnp.dot(prob_b, v_one, preferred_element_type=jnp.float32)
            return (head_out, row_top[:, 0] + jnp.log(row_total[:, 0]))

        head_outs, log_total = lax.map(per_head, (q_heads, k_heads, v_heads))
        return (head_merge(head_outs).astype(jnp.bfloat16), log_total)

    def run_layer(x_in, weights, layer_index):
        qkv_w, out_w, up_w, down_w, gain_pair, bias_pair = weights
        gains_f = gain_pair.astype(jnp.float32)
        biases_f = bias_pair.astype(jnp.float32)
        q_bias = query_bias[layer_index].astype(jnp.float32)
        bias_rows = jnp.stack(
            [q_bias, jnp.zeros_like(q_bias), value_bias[layer_index].astype(jnp.float32)]
        )
        normed = layer_norm(x_in, gains_f[:, 0]).astype(jnp.bfloat16)
        qkv_f = jnp.einsum("td,dcn->ctn", normed, qkv_w, preferred_element_type=jnp.float32)
        qkv_b = (qkv_f + bias_rows[:, None, :]).astype(jnp.bfloat16)
        kv_all = lax.all_gather(qkv_b[1:], "ctx", axis=1, tiled=True)
        attn_b, log_total = attend(qkv_b[0], kv_all)
        x_mid = (
            x_in
            + tensor_sum(jnp.einsum("tn,dn->td", attn_b, out_w, preferred_element_type=jnp.float32))
            + biases_f[:, 0]
        )
        second = layer_norm(x_mid, gains_f[:, 1]).astype(jnp.bfloat16)
        hidden = jnp.dot(second, up_w, preferred_element_type=jnp.float32) + up_bias[
            layer_index
        ].astype(jnp.float32)
        gelu_b = gelu_exact(hidden).astype(jnp.bfloat16)
        x_out = (
            x_mid
            + tensor_sum(
                jnp.einsum("tf,df->td", gelu_b, down_w, preferred_element_type=jnp.float32)
            )
            + biases_f[:, 1]
        )
        return (x_out, (normed, qkv_b, kv_all, attn_b, log_total, x_mid, second, hidden, gelu_b))

    layer_inputs = []
    for layer_index in range(layer_count):
        weights = layer_weights(layer_index)
        layer_inputs.append(x_now)
        x_now, unused = run_layer(x_now, weights, layer_index)
    activations = x_now.astype(jnp.bfloat16)
    gradient = cotangent.astype(jnp.float32)
    reduced = [0] * layer_count
    local_bias = [0] * layer_count
    for layer_index in reversed(range(layer_count)):
        weights = layer_weights(layer_index)
        unused, saved_state = run_layer(layer_inputs[layer_index], weights, layer_index)
        layer_qkv_w, layer_out_w, layer_up_w, layer_down_w, layer_gain_pair, layer_bias_pair = (
            weights
        )
        layer_gains_f = layer_gain_pair.astype(jnp.float32)
        (
            layer_normed,
            layer_qkv_b,
            layer_kv_all,
            layer_attn_b,
            layer_log_total,
            layer_x_mid,
            layer_second,
            layer_hidden,
            layer_gelu_b,
        ) = saved_state
        down_bias_grad = jnp.sum(gradient, axis=0)
        down_b = gradient.astype(jnp.bfloat16)
        grad_down = jnp.einsum(
            "td,tf->df", down_b, layer_gelu_b, preferred_element_type=jnp.float32
        )
        gelu_value, gelu_back = jax.vjp(gelu_exact, layer_hidden)
        hidden_grad = gelu_back(jnp.dot(down_b, layer_down_w, preferred_element_type=jnp.float32))[
            0
        ].astype(jnp.bfloat16)
        up_bias_grad = jnp.sum(hidden_grad.astype(jnp.float32), axis=0)
        grad_up = jnp.einsum(
            "td,tf->df", layer_second, hidden_grad, preferred_element_type=jnp.float32
        )
        second_grad = tensor_sum(
            jnp.einsum("tf,df->td", hidden_grad, layer_up_w, preferred_element_type=jnp.float32)
        )
        norm_value, norm_back = jax.vjp(layer_norm, layer_x_mid, layer_gains_f[:, 1])
        mid_from_norm, gain_second = norm_back(second_grad)
        grad_mid = gradient + mid_from_norm
        mid_bias_grad = jnp.sum(grad_mid, axis=0)
        mid_b = grad_mid.astype(jnp.bfloat16)
        grad_outw = jnp.einsum("td,tn->dn", mid_b, layer_attn_b, preferred_element_type=jnp.float32)
        attn_grad = jnp.dot(mid_b, layer_out_w, preferred_element_type=jnp.float32).astype(
            jnp.bfloat16
        )
        layer_q_heads = head_split(layer_qkv_b[0], row_count, heads_here, head_dim)
        layer_k_heads = head_split(layer_kv_all[0], group_len, heads_here, head_dim)
        layer_v_heads = head_split(layer_kv_all[1], group_len, heads_here, head_dim)
        d_heads = head_split(attn_grad, row_count, heads_here, head_dim)

        def query_full(bundle):
            q_one, k_one, v_one, d_one, total_one = bundle
            attn_prob, prob_grad = probs_and_grads(q_one, k_one, v_one, d_one, total_one, mask_here)
            row_delta = jnp.sum(attn_prob * prob_grad, axis=1)
            score_grad = (attn_prob * (prob_grad - row_delta[:, None])).astype(jnp.bfloat16)
            q_grad_one = (
                jnp.dot(score_grad, k_one, preferred_element_type=jnp.float32) * score_scale
            )
            k_term = (
                jnp.einsum("qk,qd->kd", score_grad, q_one, preferred_element_type=jnp.float32)
                * score_scale
            )
            v_term = jnp.einsum(
                "qk,qd->kd",
                attn_prob.astype(jnp.bfloat16),
                d_one,
                preferred_element_type=jnp.float32,
            )
            return (q_grad_one, row_delta, k_term, v_term)

        q_grad, deltas, k_terms, v_terms = lax.map(
            query_full, (layer_q_heads, layer_k_heads, layer_v_heads, d_heads, layer_log_total)
        )
        key_rows = jnp.stack([head_merge(k_terms), head_merge(v_terms)], axis=1)
        kv_grad = lax.psum_scatter(
            key_rows.astype(jnp.bfloat16), "ctx", scatter_dimension=0, tiled=True
        )
        q_grad_b = head_merge(q_grad).astype(jnp.bfloat16)
        qkv_grad = jnp.concatenate([q_grad_b[:, None], kv_grad], axis=1)
        column_sums = jnp.sum(qkv_grad.astype(jnp.float32), axis=0)
        grad_qkv = jnp.einsum(
            "td,tcn->dcn", layer_normed, qkv_grad, preferred_element_type=jnp.float32
        )
        first_grad = tensor_sum(
            jnp.einsum("tcn,dcn->td", qkv_grad, layer_qkv_w, preferred_element_type=jnp.float32)
        )
        first_value, first_back = jax.vjp(
            layer_norm, layer_inputs[layer_index], layer_gains_f[:, 0]
        )
        in_from_norm, gain_first = first_back(first_grad)
        gain_grads = jnp.stack([gain_first, gain_second], axis=1)
        bias_grads = jnp.stack([mid_bias_grad, down_bias_grad], axis=1)
        gradient = grad_mid + in_from_norm
        layer_grads = (grad_qkv, grad_outw, grad_up, grad_down, gain_grads, bias_grads)
        bias_parts = (column_sums[0], column_sums[2], up_bias_grad)
        local_bias[layer_index] = bias_parts
        reduced[layer_index] = layer_grads
    bias_totals = lax.psum(
        (stack_part(local_bias, 0), stack_part(local_bias, 1), stack_part(local_bias, 2)),
        ("shard", "ctx"),
    )
    seq_grad = jnp.einsum("ts,td->sd", member, gradient, precision=PRECISE)
    table_grad = jnp.einsum("sr,sd->rd", step_rows.astype(jnp.float32), seq_grad, precision=PRECISE)
    table_total = sum_at_owner(table_grad.astype(jnp.bfloat16), ("shard", "ctx"), 1)
    stacked_qkv = stack_part(reduced, 0)
    stacked_out = stack_part(reduced, 1)
    stacked_up = stack_part(reduced, 2)
    stacked_down = stack_part(reduced, 3)
    stacked_norms = stack_part(reduced, 4)
    stacked_bias = stack_part(reduced, 5)
    totals = (
        lax.psum_scatter(stacked_qkv, ("shard", "ctx"), scatter_dimension=1, tiled=True),
        lax.psum_scatter(stacked_out, ("shard", "ctx"), scatter_dimension=1, tiled=True),
        lax.psum_scatter(stacked_up, ("shard", "ctx"), scatter_dimension=1, tiled=True),
        lax.psum_scatter(stacked_down, ("shard", "ctx"), scatter_dimension=1, tiled=True),
        lax.psum_scatter(stacked_norms, ("shard", "ctx"), scatter_dimension=1, tiled=True),
        lax.psum_scatter(stacked_bias, ("shard", "ctx"), scatter_dimension=1, tiled=True),
    )
    return (
        activations,
        gradient,
        totals[0],
        totals[1],
        totals[2],
        totals[3],
        totals[4],
        table_total,
        bias_totals[0],
        bias_totals[1],
        bias_totals[2],
        totals[5],
    )


def solution(mesh):
    placed = (
        P(("shard", "ctx"), None),
        P("shard", None),
        P("shard", None),
        P(None, ("shard", "ctx")),
        P(None, ("shard", "ctx"), None, "tp"),
        P(None, ("shard", "ctx"), "tp"),
        P(None, ("shard", "ctx"), "tp"),
        P(None, ("shard", "ctx"), "tp"),
        P(None, ("shard", "ctx"), None),
        P(None, "tp"),
        P(None, "tp"),
        P(None, "tp"),
        P(None, ("shard", "ctx"), None),
        P(("shard", "ctx"), None),
    )
    return jax.shard_map(
        per_device,
        mesh=mesh,
        in_specs=placed,
        out_specs=(
            P(("shard", "ctx"), None),
            P(("shard", "ctx"), None),
            P(None, ("shard", "ctx"), None, "tp"),
            P(None, ("shard", "ctx"), "tp"),
            P(None, ("shard", "ctx"), "tp"),
            P(None, ("shard", "ctx"), "tp"),
            P(None, ("shard", "ctx"), None),
            P(None, ("shard", "ctx")),
            P(None, "tp"),
            P(None, "tp"),
            P(None, "tp"),
            P(None, ("shard", "ctx"), None),
        ),
        check_vma=False,
    )
```

profile of v0, /device:TPU:0, one launch (start us, length us, event | category | flops | bytes accessed | tf_op | source)
XLA Modules:
  0.0 1233.5 jit_solution(6214926940190025999)
XLA Ops:
  11.1 24.4 %all-gather = bf16[1,768,2]{2,0,1:T(2,128)(2,1)S(1)} all-gather(bf16[1,48,2]{2,0,1:T(2,128)(2,1)S(1)} %copy.218), channel_id=2, replica_groups=mesh['shard'=4,'ctx'=4,'tp'=2] {'shard','ctx'}, dimensions={1}, use_global_device_ids=true | all-gather | bytes 3264 | tf_op jit(solution)/shard_map/all_gather | solution.py:107
  39.2 19.9 %all-gather.2 = bf16[1,768,384]{2,1,0:T(8,128)(2,1)S(1)} all-gather(bf16[1,48,384]{2,1,0:T(8,128)(2,1)S(1)} %get-tuple-element.831), channel_id=4, replica_groups=mesh['shard'=4,'ctx'=4,'tp'=2] {'shard','ctx'}, dimensions={1}, use_global_device_ids=true | all-gather | bytes 626688 | tf_op jit(solution)/shard_map/all_gather | solution.py:104
  61.9 35.4 %all-gather.22.cloned.1.call-done = bf16[1,768,3,384]{3,1,2,0:T(8,128)(2,1)} async-done(((bf16[1,48,3,384]{3,1,2,0:T(8,128)(2,1)}), bf16[1,768,3,384]{3,1,2,0:T(8,128)(2,1)}) %all-gather.22.cloned.1.call-update) | async-done | bytes 1769488 | tf_op jit(solution)/shard_map/all_gather | solution.py:103
  122.6 20.4 %all-gather.3 = bf16[1,768,2]{2,0,1:T(2,128)(2,1)S(1)} all-gather(bf16[1,48,2]{2,0,1:T(2,128)(2,1)S(1)} %copy.219), channel_id=5, replica_groups=mesh['shard'=4,'ctx'=4,'tp'=2] {'shard','ctx'}, dimensions={1}, use_global_device_ids=true | all-gather | bytes 3264 | tf_op jit(solution)/shard_map/all_gather | solution.py:108
  146.7 39.2 %all-gather.26.cloned.1.call-done = bf16[1,768,1536]{2,1,0:T(8,128)(2,1)} async-done(((bf16[1,48,1536]{2,1,0:T(8,128)(2,1)}), bf16[1,768,1536]{2,1,0:T(8,128)(2,1)}) %all-gather.26.cloned.1.call-update) | async-done | bytes 2359312 | tf_op jit(solution)/shard_map/all_gather | solution.py:106
  185.9 43.8 %all-gather.24.cloned.1.call-done = bf16[1,768,1536]{2,1,0:T(8,128)(2,1)} async-done(((bf16[1,48,1536]{2,1,0:T(8,128)(2,1)}), bf16[1,768,1536]{2,1,0:T(8,128)(2,1)}) %all-gather.24.cloned.1.call-update) | async-done | bytes 2359312 | tf_op jit(solution)/shard_map/all_gather | solution.py:105
  236.6 20.3 %all-gather.6 = bf16[1,768,2]{2,0,1:T(2,128)(2,1)S(1)} all-gather(bf16[1,48,2]{2,0,1:T(2,128)(2,1)S(1)} %copy.220), channel_id=8, replica_groups=mesh['shard'=4,'ctx'=4,'tp'=2] {'shard','ctx'}, dimensions={1}, use_global_device_ids=true | all-gather | bytes 3264 | tf_op jit(solution)/shard_map/all_gather | solution.py:107
  257.7 20.6 %all-gather.8 = bf16[1,768,384]{2,1,0:T(8,128)(2,1)S(1)} all-gather(bf16[1,48,384]{2,1,0:T(8,128)(2,1)S(1)} %copy-done.46), channel_id=10, replica_groups=mesh['shard'=4,'ctx'=4,'tp'=2] {'shard','ctx'}, dimensions={1}, use_global_device_ids=true | all-gather | bytes 626688 | tf_op jit(solution)/shard_map/all_gather | solution.py:104
  279.9 21.1 %all-gather.28.cloned.1.call-done = bf16[1,768,3,384]{3,1,2,0:T(8,128)(2,1)} async-done(((bf16[1,48,3,384]{3,1,2,0:T(8,128)(2,1)}), bf16[1,768,3,384]{3,1,2,0:T(8,128)(2,1)}) %all-gather.28.cloned.1.call-update) | async-done | bytes 1769488 | tf_op jit(solution)/shard_map/all_gather | solution.py:103
  335.8 20.4 %all-gather.9 = bf16[1,768,2]{2,0,1:T(2,128)(2,1)S(1)} all-gather(bf16[1,48,2]{2,0,1:T(2,128)(2,1)S(1)} %copy.221), channel_id=11, replica_groups=mesh['shard'=4,'ctx'=4,'tp'=2] {'shard','ctx'}, dimensions={1}, use_global_device_ids=true | all-gather | bytes 3264 | tf_op jit(solution)/shard_map/all_gather | solution.py:108
  369.5 30.8 %all-gather.30.cloned.1.call-done = bf16[1,768,1536]{2,1,0:T(8,128)(2,1)} async-done(((bf16[1,48,1536]{2,1,0:T(8,128)(2,1)}), bf16[1,768,1536]{2,1,0:T(8,128)(2,1)}) %all-gather.30.cloned.1.call-update) | async-done | bytes 2359312 | tf_op jit(solution)/shard_map/all_gather | solution.py:105
  403.4 40.7 %all-gather.32.cloned.1.call-done = bf16[1,768,1536]{2,1,0:T(8,128)(2,1)} async-done(((bf16[1,48,1536]{2,1,0:T(8,128)(2,1)}), bf16[1,768,1536]{2,1,0:T(8,128)(2,1)}) %all-gather.32.cloned.1.call-update) | async-done | bytes 2359312 | tf_op jit(solution)/shard_map/all_gather | solution.py:106
  479.0 32.7 %while.81 = (s32[]{:T(128)}, bf16[6,128,64]{1,2,0:T(8,128)(2,1)S(1)}, bf16[6,512,64]{1,2,0:T(8,128)(2,1)S(1)}, bf16[6,512,64]{1,2,0:T(8,128)(2,1)S(1)}, bf16[6,1...) while((s32[]{:T(128)}, ...), condition=%wide.region_34.35_spmd.clone, body=%wide.region_32.34_spmd.clone.sunk | while | flops 42704768 | bytes 2763401 | solution.py:253
  514.4 19.1 %while.79 = (s32[]{:T(128)}, bf16[6,128,64]{1,2,0:T(8,128)(2,1)}, bf16[6,128,64]{2,1,0:T(8,128)(2,1)}, bf16[6,512,64]{2,1,0:T(8,128)(2,1)}, bf16[6,512,64]{2,1,0...) while((s32[]{:T(128)}, bf16[6,128,64]{1,2,0:T(8,128)(2,1)}, ...), condition=%wide.region_17.18_spmd.clone, body=%wide.region_14.17_spmd.clone.sunk | while | flops 17432320 | bytes 1121893 | solution.py:141
  539.7 31.1 %all-reduce.23.cloned.1.call-done = (bf16[128,768]{1,0:T(8,128)(2,1)}, bf16[128,768]{1,0:T(8,128)(2,1)}, bf16[128,768]{1,0:T(8,128)(2,1)}) async-done(((bf16[128,768]{1,0:T(8,128)(2,1)}, bf16[128,768]{1,0:T(8,128)(2,1)}, bf16[128,768]{1,0:T(8,128)(2,1)}), (bf16[128,768]{1,0:T(8,128)(2,1)}, bf16[128,768]{1,0:T(8,128)(2,1)}, bf16[128,768]{1,0:T(8,128)(2,1)})) %all-reduce.23.cloned.1.call-update) | async-done | bytes 589840 | tf_op jit(solution)/shard_map/psum | solution.py:112
  583.2 22.4 %all-reduce.19.cloned.1.call-done = bf16[128,768]{1,0:T(8,128)(2,1)} async-done(((bf16[128,768]{1,0:T(8,128)(2,1)}), bf16[128,768]{1,0:T(8,128)(2,1)}) %all-reduce.19.cloned.1.call-update) | async-done | bytes 196624 | tf_op jit(solution)/shard_map/psum | solution.py:112
  612.2 36.2 %while.83 = (s32[]{:T(128)}, bf16[6,128,64]{1,2,0:T(8,128)(2,1)}, bf16[6,512,64]{1,2,0:T(8,128)(2,1)S(1)}, bf16[6,512,64]{1,2,0:T(8,128)(2,1)S(1)}, bf16[6,128,6...) while((s32[]{:T(128)}, bf16[6,128,64]{1,2,0:T(8,128)(2,1)}, ...), condition=%wide.region_51.52_spmd.clone, body=%wide.region_49.51_spmd.clone.sunk | while | flops 42704768 | bytes 2763401 | solution.py:253
  681.8 20.4 %all-reduce.21.cloned.1.call-done = (bf16[128,768]{1,0:T(8,128)(2,1)}, bf16[128,768]{1,0:T(8,128)(2,1)}) async-done(((bf16[128,768]{1,0:T(8,128)(2,1)}, bf16[128,768]{1,0:T(8,128)(2,1)}), (bf16[128,768]{1,0:T(8,128)(2,1)}, bf16[128,768]{1,0:T(8,128)(2,1)})) %all-reduce.21.cloned.1.call-update) | async-done | bytes 393232 | tf_op jit(solution)/shard_map/psum | solution.py:112
  746.4 19.5 %reduce-scatter.27.cloned.1.call-done = f32[48,4]{1,0:T(8,128)} async-done(((f32[768,4]{1,0:T(8,128)}), f32[48,4]{1,0:T(8,128)}) %reduce-scatter.27.cloned.1.call-update) | async-done | bytes 784
  767.6 61.7 %all-reduce = (f32[2,384]{1,0:T(2,128)}, f32[2,384]{1,0:T(2,128)}, f32[2,1536]{1,0:T(2,128)}) all-reduce(f32[2,384]{1,0:T(2,128)S(1)} %pad_maximum_fusion.17, f32[2,384]{1,0:T(2,128)S(1)} %pad_maximum_fusion.18, f32[2,1536]{1,0:T(2,128)S(1)} %pad_maximum_fusion.13), channel_id=1, replica_groups=mesh['shard'=4,'ctx'=4,'tp'=2] {'shard','ctx'}, use_global_device_ids=true, to_apply=%region_68.69 | all-reduce | flops 4608 | bytes 36864 | tf_op jit(solution)/shard_map/psum | solution.py:280
  836.3 63.9 %reduce-scatter.19.cloned.1.call-done = f32[2,48,384]{2,1,0:T(8,128)} async-done(((f32[2,768,384]{2,1,0:T(8,128)}), f32[2,48,384]{2,1,0:T(8,128)}) %reduce-scatter.19.cloned.1.call-update) | async-done | bytes 147472 | tf_op jit(solution)/shard_map/reduce_scatter | solution.py:295
  900.2 94.1 %reduce-scatter.17.cloned.1.call-done = f32[2,48,3,384]{3,1,2,0:T(8,128)} async-done(((f32[2,768,3,384]{3,1,2,0:T(8,128)}), f32[2,48,3,384]{3,1,2,0:T(8,128)}) %reduce-scatter.17.cloned.1.call-update) | async-done | bytes 442384 | tf_op jit(solution)/shard_map/reduce_scatter | solution.py:294
  994.3 115.6 %reduce-scatter.21.cloned.1.call-done = f32[2,48,1536]{2,1,0:T(8,128)} async-done(((f32[2,768,1536]{2,1,0:T(8,128)}), f32[2,48,1536]{2,1,0:T(8,128)}) %reduce-scatter.21.cloned.1.call-update) | async-done | bytes 589840 | tf_op jit(solution)/shard_map/reduce_scatter | solution.py:296
  1109.9 116.4 %reduce-scatter.23.cloned.1.call-done = f32[2,48,1536]{2,1,0:T(8,128)} async-done(((f32[2,768,1536]{2,1,0:T(8,128)}), f32[2,48,1536]{2,1,0:T(8,128)}) %reduce-scatter.23.cloned.1.call-update) | async-done | bytes 589840 | tf_op jit(solution)/shard_map/reduce_scatter | solution.py:297
  (650 shorter events, 368.4 us)
Async XLA Ops:
  7.2 51.9 %all-gather.20.cloned.1.call-start = ((), (), s32[]{:S(2)}) async-start(), calls=%async_computation.9 | async-start | bytes 1671168 | tf_op jit(solution)/shard_map/all_gather | solution.py:95
  8.0 89.3 %all-gather.22.cloned.1.call-start = ((), (), s32[]{:S(2)}) async-start(), calls=%async_computation.21 | async-start | bytes 1880064 | tf_op jit(solution)/shard_map/all_gather | solution.py:103
  9.7 134.8 %all-reduce.11.cloned.1.call-start = ((), (), s32[]{:S(2)}) async-start(), calls=%async_computation.10 | async-start | bytes 393216 | tf_op jit(solution)/shard_map/psum | solution.py:112
  119.3 66.6 %all-gather.26.cloned.1.call-start = ((), (), s32[]{:S(2)}) async-start(), calls=%async_computation.23 | async-start | bytes 2506752 | tf_op jit(solution)/shard_map/all_gather | solution.py:106
  120.2 109.6 %all-gather.24.cloned.1.call-start = ((), (), s32[]{:S(2)}) async-start(), calls=%async_computation.22 | async-start | bytes 2506752 | tf_op jit(solution)/shard_map/all_gather | solution.py:105
  121.9 156.4 %all-reduce.13.cloned.1.call-start = ((), (), s32[]{:S(2)}) async-start(), calls=%async_computation.11 | async-start | bytes 393216 | tf_op jit(solution)/shard_map/psum | solution.py:112
  144.5 133.9 %copy-start.54 = (f32[768]{0:T(1024)}, f32[768]{0:T(1024)S(1)}, u32[]{:S(2)}) copy-start(f32[768]{0:T(1024)S(1)} %get-tuple-element.666) | copy-start | bytes 9220
  235.7 65.3 %all-gather.28.cloned.1.call-start = ((), (), s32[]{:S(2)}) async-start(), calls=%async_computation.24 | async-start | bytes 1880064 | tf_op jit(solution)/shard_map/all_gather | solution.py:103
  236.4 131.5 %all-reduce.15.cloned.1.call-start = ((), (), s32[]{:S(2)}) async-start(), calls=%async_computation.12 | async-start | bytes 393216 | tf_op jit(solution)/shard_map/psum | solution.py:112
  334.3 66.0 %all-gather.30.cloned.1.call-start = ((), (), s32[]{:S(2)}) async-start(), calls=%async_computation.25 | async-start | bytes 2506752 | tf_op jit(solution)/shard_map/all_gather | solution.py:105
  335.0 109.1 %all-gather.32.cloned.1.call-start = ((), (), s32[]{:S(2)}) async-start(), calls=%async_computation.26 | async-start | bytes 2506752 | tf_op jit(solution)/shard_map/all_gather | solution.py:106
  335.6 136.7 %all-reduce.17.cloned.1.call-start = ((), (), s32[]{:S(2)}) async-start(), calls=%async_computation.13 | async-start | bytes 393216 | tf_op jit(solution)/shard_map/psum | solution.py:112
  451.1 86.0 %reduce-scatter.13.cloned.1.call-start = ((), (), s32[]{:S(2)}) async-start(), calls=%async_computation.14 | async-start | bytes 983040 | tf_op jit(solution)/shard_map/reduce_scatter | solution.py:257
  513.7 57.0 %all-reduce.23.cloned.1.call-start = ((), (), s32[]{:S(2)}) async-start(), calls=%async_computation.30 | async-start | bytes 1179648 | tf_op jit(solution)/shard_map/psum | solution.py:112
  539.4 66.2 %all-reduce.19.cloned.1.call-start = ((), (), s32[]{:S(2)}) async-start(), calls=%async_computation.15 | async-start | bytes 393216 | tf_op jit(solution)/shard_map/psum | solution.py:112
  583.2 90.1 %reduce-scatter.15.cloned.1.call-start = ((), (), s32[]{:S(2)}) async-start(), calls=%async_computation.16 | async-start | bytes 983040 | tf_op jit(solution)/shard_map/reduce_scatter | solution.py:257
  649.9 52.3 %all-reduce.21.cloned.1.call-start = ((), (), s32[]{:S(2)}) async-start(), calls=%async_computation.29 | async-start | bytes 786432 | tf_op jit(solution)/shard_map/psum | solution.py:112
  675.7 90.3 %reduce-scatter.27.cloned.1.call-start = ((), (), s32[]{:S(2)}) async-start(), calls=%async_computation.28 | async-start | bytes 417792
  681.7 152.1 %reduce-scatter.25.cloned.1.call-start = ((), (), s32[]{:S(2)}) async-start(), calls=%async_computation.27 | async-start | bytes 417792
  708.6 191.6 %reduce-scatter.19.cloned.1.call-start = ((), (), s32[]{:S(2)}) async-start(), calls=%async_computation.18 | async-start | bytes 2506752 | tf_op jit(solution)/shard_map/reduce_scatter | solution.py:295
  711.6 282.7 %reduce-scatter.17.cloned.1.call-start = ((), (), s32[]{:S(2)}) async-start(), calls=%async_computation.17 | async-start | bytes 7520256 | tf_op jit(solution)/shard_map/reduce_scatter | solution.py:294
  717.5 392.4 %reduce-scatter.21.cloned.1.call-start = ((), (), s32[]{:S(2)}) async-start(), calls=%async_computation.19 | async-start | bytes 10027008 | tf_op jit(solution)/shard_map/reduce_scatter | solution.py:296
  725.4 500.9 %reduce-scatter.23.cloned.1.call-start = ((), (), s32[]{:S(2)}) async-start(), calls=%async_computation.20 | async-start | bytes 10027008 | tf_op jit(solution)/shard_map/reduce_scatter | solution.py:297
  740.5 94.8 %all-to-all-start = ((bf16[16,1000,48]{1,2,0:T(8,128)(2,1)}), bf16[16,1000,48]{1,2,0:T(8,128)(2,1)S(1)}, u32[]{:S(2)}, u32[]{:S(2)}) async-start(bf16[16,1000,48]{1,2,0:T(8,128)(2,1)} %bitcast.467), calls=%async_computation.6 | async-start | bytes 3145728 | tf_op jit(solution)/shard_map/all_to_all | solution.py:23
  (116 other events, 2408.3 us)
Sparse Core Ops, SparseCore 0:
  10.3 44.5 all-gather.19
  57.8 39.4 all-gather.21
  119.5 21.2 all-reduce.10
  143.5 42.3 all-gather.25
  188.6 41.0 all-gather.23
  235.8 21.0 all-reduce.12
  259.8 41.0 all-gather.27
  334.4 21.2 all-reduce.14
  358.0 42.2 all-gather.29
  403.0 41.0 all-gather.31
  451.2 21.0 all-reduce.16
  513.8 23.2 reduce-scatter.12
  540.3 30.3 all-reduce.22
  583.3 22.2 all-reduce.18
  650.0 23.2 reduce-scatter.14
  676.2 25.9 all-reduce.20
  705.5 60.4 reduce-scatter.26
  769.7 64.0 reduce-scatter.24
  838.2 61.9 reduce-scatter.18
  905.2 89.0 reduce-scatter.16
  999.0 110.8 reduce-scatter.20
  1115.1 111.1 reduce-scatter.22
where the time goes:
time: 1250 us; the launch traced here: 1230 us
  waiting for transfers between devices  732 us (59%)
  blocking collectives  205 us (16%)
  matrix products  165 us (13%)
  other arithmetic  55.5 us (4%)
  local copies, waits for them, and re-layouts  51.1 us (4%)
  between operations  16.3 us (1%)
    reduce_scatter x1, waiting for transfers between devices, per_device(): lax.psum_scatter(stacked_down, ('shard', 'ctx'), scatter_dimension=1, til...  116 us
    reduce_scatter x1, waiting for transfers between devices, per_device(): lax.psum_scatter(stacked_up, ('shard', 'ctx'), scatter_dimension=1, tiled...  116 us
    reduce_scatter x1, waiting for transfers between devices, per_device(): lax.psum_scatter(stacked_qkv, ('shard', 'ctx'), scatter_dimension=1, tile...  94.1 us
    psum x7, waiting for transfers between devices, tensor_sum(): return lax.psum(term_value.astype(jnp.bfloat16), 'tp').astype(jnp.float32)  92.9 us
    all_gather x2, waiting for transfers between devices, layer_weights(): lax.all_gather(w_down[layer_index], ('shard', 'ctx'), axis=0, tiled=True)  79.9 us
    all_gather x2, waiting for transfers between devices, layer_weights(): lax.all_gather(w_up[layer_index], ('shard', 'ctx'), axis=0, tiled=True)  74.6 us
    reduce_scatter x1, waiting for transfers between devices, per_device(): lax.psum_scatter(stacked_out, ('shard', 'ctx'), scatter_dimension=1, tile...  63.9 us
    psum x1, blocking collectives, per_device(): lax.psum((stack_part(local_bias, 0), stack_part(local_bias, 1), stack_par...  61.7 us
  transfers between devices with their start and end apart: 23, of which 18 were waited for; matrix products, arithmetic and copies ran while one was open for 9% of the time, Pallas kernels for 0%

commit v1 on v0

v1 whole, which is shorter than its diff:
```python
import functools
import math

import jax
import jax.numpy as jnp
from jax import lax
from jax.experimental import pallas as pl
from jax.experimental.pallas import tpu as pltpu
from jax.sharding import PartitionSpec as P

HEAD_DIM = 64
EPSILON = 1e-05
NEGATIVE = -1e30
F32 = jnp.float32
BF16 = jnp.bfloat16
LANES = 128
CHUNK = 512
VMEM_LIMIT = 40 * 1024 * 1024
ORDER = (0, 2, 1, 3)


def nn(a, b):
    return lax.dot_general(a, b, (((1,), (0,)), ((), ())), preferred_element_type=F32)


def nt(a, b):
    return lax.dot_general(a, b, (((1,), (1,)), ((), ())), preferred_element_type=F32)


def tn(a, b):
    return lax.dot_general(a, b, (((0,), (0,)), ((), ())), preferred_element_type=F32)


def normed_rows(values):
    centered = values - jnp.mean(values, axis=-1, keepdims=True)
    scale = lax.rsqrt(jnp.mean(centered * centered, axis=-1, keepdims=True) + EPSILON)
    return centered * scale, scale


def norm_back(values, gain, grad):
    hat, scale = normed_rows(values)
    grad_gain = jnp.sum(grad * hat, axis=0, keepdims=True)
    inner = grad * gain
    along = jnp.mean(inner * hat, axis=-1, keepdims=True)
    centre = jnp.mean(inner, axis=-1, keepdims=True)
    return scale * (inner - centre - hat * along), grad_gain


def rows_of(parts, count, width):
    have = len(parts)
    if have < count:
        parts = list(parts) + [jnp.zeros((count - have, width), F32)]
    return jnp.concatenate(parts, axis=0)


class Plan:
    def __init__(self, rows, width, block, heads_width, hidden, shards, contexts, conts):
        self.rows, self.width, self.block = rows, width, block
        self.heads_width, self.hidden = heads_width, hidden
        self.shards, self.contexts, self.conts = shards, contexts, conts
        self.group = rows * contexts
        self.blocks = contexts == 4 and block % 16 == 0


def run(plan, body, name, meta, inputs, weights, outs, flops, scratch=(), direct=()):
    n_in, n_out = len(inputs), len(outs)
    counts = [len(arrays) for arrays, _, _ in weights]
    per_block = plan.shards * len(ORDER)
    copies = sum(1 if n == 1 else per_block for n in counts)

    def kernel(meta_ref, *refs):
        ins = refs[:n_in]
        at = n_in
        sources = []
        for n in counts:
            sources.append(refs[at : at + n])
            at += n
        results = refs[at : at + n_out]
        at += n_out
        held = refs[at : at + len(weights)]
        at += len(weights)
        sems = refs[at] if weights else None
        own = refs[at + 1 :] if weights else refs[at:]
        started, slot = [], 0
        for (_, column, width), refs_of, into in zip(weights, sources, held):
            group = []
            columns = pl.ds(column, width)
            if len(refs_of) == 1:
                group.append(pltpu.make_async_copy(refs_of[0].at[:, columns], into, sems.at[slot]))
                slot += 1
            else:
                for ref, offset in zip(refs_of, ORDER):
                    for shift in range(plan.shards):
                        z = lax.rem(meta_ref[0] + (plan.shards - shift), plan.shards)
                        index = z * plan.contexts + jnp.bitwise_xor(meta_ref[1], offset)
                        row = pl.multiple_of(index * plan.block, 16)
                        group.append(
                            pltpu.make_async_copy(
                                ref.at[shift, :, columns],
                                into.at[pl.ds(row, plan.block), :],
                                sems.at[slot],
                            )
                        )
                        slot += 1
            for copy in group:
                copy.start()
            started.append(group)

        def weight(i):
            for copy in started[i]:
                copy.wait()
            return held[i]

        body(meta_ref, ins, weight, results, own)

    vmem = pl.BlockSpec(memory_space=pltpu.VMEM)
    anywhere = pl.BlockSpec(memory_space=pl.ANY)
    scratch_shapes = [pltpu.VMEM((plan.width, width), BF16) for _, _, width in weights]
    if weights:
        scratch_shapes.append(pltpu.SemaphoreType.DMA((copies,)))
    moved = sum(x.size * x.dtype.itemsize for x in inputs)
    moved += sum(math.prod(o.shape) * o.dtype.itemsize for o in outs)
    moved += sum(plan.width * width * 2 for _, _, width in weights)
    return pl.pallas_call(
        kernel,
        name=name,
        out_shape=tuple(outs),
        in_specs=[pl.BlockSpec(memory_space=pltpu.SMEM)]
        + [vmem] * n_in
        + [anywhere] * sum(counts),
        out_specs=tuple(anywhere if i in direct else vmem for i in range(n_out)),
        scratch_shapes=scratch_shapes + list(scratch),
        compiler_params=pltpu.CompilerParams(vmem_limit_bytes=VMEM_LIMIT),
        cost_estimate=pl.CostEstimate(flops=flops, bytes_accessed=moved, transcendentals=0),
    )(meta, *inputs, *[array for arrays, _, _ in weights for array in arrays])


def shape(*dims, dtype=BF16):
    return jax.ShapeDtypeStruct(dims, dtype)


def segment(plan, meta, position):
    prompt = plan.group // 2
    seg = jnp.ones(position.shape, jnp.int32)
    for j in range(plan.conts):
        seg = seg + (position - prompt >= meta[2 + j]).astype(jnp.int32)
    return jnp.where(position < prompt, 0, seg)


def key_positions(plan, meta):
    if not plan.blocks:
        return lax.broadcasted_iota(jnp.int32, (plan.group, 1), 0)
    inside = lax.broadcasted_iota(jnp.int32, (plan.rows, 1), 0)
    return jnp.concatenate(
        [inside + jnp.bitwise_xor(meta[1], d) * plan.rows for d in ORDER], axis=0
    )


def allowed_keys(plan, meta):
    lane = lax.broadcasted_iota(jnp.int32, (1, 2 * plan.rows), 1)
    query = meta[1] * plan.rows + jnp.where(lane >= plan.rows, lane - plan.rows, lane)
    seg_query = segment(plan, meta, query)
    seg_key = segment(plan, meta, key_positions(plan, meta))
    return (seg_key == 0) | (seg_key == seg_query)


def pair_rows(values):
    first = lax.broadcasted_iota(jnp.int32, values.shape, 1) < HEAD_DIM
    none = jnp.zeros_like(values)
    return jnp.concatenate([jnp.where(first, values, none), jnp.where(first, none, values)], axis=0)


def pair_lanes(values):
    rows = values.shape[0] // 2
    first = lax.broadcasted_iota(jnp.int32, (rows, LANES), 1) < HEAD_DIM
    return jnp.where(first, values[:rows], values[rows:])


def write_qkv(plan, layer, x, gain, weight, q_bias, v_bias, a_ref, q_ref, kv_ref):
    n = plan.heads_width
    hat, _ = normed_rows(x)
    a = (hat * gain).astype(BF16)
    a_ref[...] = a
    bias_q = q_bias[...].astype(F32)[layer : layer + 1]
    bias_v = v_bias[...].astype(F32)[layer : layer + 1]
    kv_ref[:, :n] = nn(a, weight[:, n : 2 * n]).astype(BF16)
    kv_ref[:, n:] = (nn(a, weight[:, 2 * n :]) + bias_v).astype(BF16)
    q_ref[...] = (nn(a, weight[:, :n]) + bias_q).astype(BF16)


def embed_body(plan, meta, ins, weight, outs, own):
    tokens, q_bias, v_bias = ins
    x_ref, vec_ref, a_ref, q_ref, kv_ref = outs
    small = weight(1)[...].astype(F32).T
    vec_ref[...] = small[:8]
    lookup = small[8:24].astype(BF16)
    inside = lax.broadcasted_iota(jnp.int32, (plan.rows, 1), 0)
    seg = segment(plan, meta, meta[1] * plan.rows + inside)
    member = seg == lax.broadcasted_iota(jnp.int32, (plan.rows, 16), 1)
    x = tokens[...].astype(F32) + nn(member.astype(F32).astype(BF16), lookup)
    x_ref[...] = x
    write_qkv(plan, 0, x, small[:1], weight(0), q_bias, v_bias, a_ref, q_ref, kv_ref)


def next_body(plan, layer, meta, ins, weight, outs, own):
    x_mid, part, part_far, vec, q_bias, v_bias = ins
    x_ref, a_ref, q_ref, kv_ref = outs
    x = x_mid[...] + (part[...].astype(F32) + part_far[...].astype(F32))
    x = x + vec[2 * layer + 3 : 2 * layer + 4, :]
    x_ref[...] = x
    gain = vec[2 * layer : 2 * layer + 1, :]
    write_qkv(plan, layer, x, gain, weight(0), q_bias, v_bias, a_ref, q_ref, kv_ref)


def attend_body(plan, meta, ins, weight, outs, own):
    q_ref, kvs = ins[0], ins[1:]
    part_ref, o_ref, total_ref = outs
    n = plan.heads_width
    allowed = allowed_keys(plan, meta)
    totals = []
    for pair in range(n // LANES):
        lanes = slice(pair * LANES, (pair + 1) * LANES)
        late = slice(n + pair * LANES, n + (pair + 1) * LANES)
        q2 = pair_rows(q_ref[:, lanes])
        keys = jnp.concatenate([kv[:, lanes] for kv in kvs], axis=0)
        values = jnp.concatenate([kv[:, late] for kv in kvs], axis=0)
        scores = jnp.where(allowed, nt(keys, q2) * (1.0 / math.sqrt(HEAD_DIM)), NEGATIVE)
        top = jnp.max(scores, axis=0, keepdims=True)
        exps = jnp.exp(scores - top)
        total = jnp.sum(exps, axis=0, keepdims=True)
        prob = (exps * (1.0 / total)).astype(BF16)
        o_ref[:, lanes] = pair_lanes(tn(prob, values)).astype(BF16)
        totals.append(top + jnp.log(total))
    total_ref[...] = rows_of(totals, 8, 2 * plan.rows)
    part_ref[...] = nt(o_ref[...], weight(0)[...]).astype(BF16)


def feed_body(plan, layer, last, meta, ins, weight, outs, own):
    x, part, part_far, vec, bias = ins[:5]
    mid_ref, b_ref, gelu_ref, slope_ref, part_ref = outs[:5]
    x_mid = x[...] + (part[...].astype(F32) + part_far[...].astype(F32))
    x_mid = x_mid + vec[2 * layer + 4 : 2 * layer + 5, :]
    mid_ref[...] = x_mid
    hat, _ = normed_rows(x_mid)
    b = (hat * vec[2 * layer + 1 : 2 * layer + 2, :]).astype(BF16)
    b_ref[...] = b
    bias_f = bias[...].astype(F32)[layer : layer + 1]
    up = weight(0)
    chunks = [slice(i, min(i + CHUNK, plan.hidden)) for i in range(0, plan.hidden, CHUNK)]
    for columns in chunks:
        hidden = nn(b, up[:, columns]) + bias_f[:, columns]
        half = 0.5 * (1.0 + lax.erf(hidden * math.sqrt(0.5)))
        gelu_ref[:, columns] = (hidden * half).astype(BF16)
        bell = jnp.exp(hidden * hidden * -0.5) * (1.0 / math.sqrt(2.0 * math.pi))
        slope_ref[:, columns] = half + hidden * bell
    down = weight(1)
    if last:
        back_feed(plan, ins[5][...], slope_ref, up, down, outs[5], outs[6], outs[7], ins[5][...].astype(F32), None)
    part_ref[...] = nt(gelu_ref[...], down[...]).astype(BF16)


def back_feed(plan, dy, slope, up, down, dh_ref, db_ref, sum_ref, gradient, extra):
    sums = []
    total = None
    for i in range(0, plan.hidden, CHUNK):
        columns = slice(i, min(i + CHUNK, plan.hidden))
        dh = (nn(dy, down[:, columns]) * slope[:, columns]).astype(BF16)
        dh_ref[:, columns] = dh
        sums.append(jnp.sum(dh.astype(F32), axis=0, keepdims=True))
        term = nt(dh, up[:, columns])
        total = term if total is None else total + term
    db_ref[...] = total.astype(BF16)
    bias_sum = jnp.concatenate(sums, axis=1)
    parts = [jnp.sum(gradient, axis=0, keepdims=True)]
    for i in range(plan.hidden // plan.width):
        parts.append(bias_sum[:, i * plan.width : (i + 1) * plan.width])
    if extra is not None:
        parts.append(extra)
    sum_ref[...] = rows_of(parts, 8, plan.width)


def between_body(plan, layer, meta, ins, weight, outs, own):
    dx_mid, x_above, da, da_far, vec, slope = ins
    gy_ref, dy_ref, dh_ref, db_ref, sum_ref = outs
    grad = da[...].astype(F32) + da_far[...].astype(F32)
    back, gain_sum = norm_back(x_above[...], vec[2 * layer + 2 : 2 * layer + 3, :], grad)
    gy = dx_mid[...] + back
    gy_ref[...] = gy
    dy = gy.astype(BF16)
    dy_ref[...] = dy
    back_feed(plan, dy, slope, weight(0), weight(1), dh_ref, db_ref, sum_ref, gy, gain_sum)


def attend_back_body(plan, layer, meta, ins, weight, outs, own):
    gy, x_mid, db, db_far, vec, q_ref, total = ins[:7]
    kvs = ins[7:]
    mid_ref, dz_ref, dq_ref, sum_ref = outs[:4]
    dkv = outs[4:]
    n = plan.heads_width
    scale = 1.0 / math.sqrt(HEAD_DIM)
    grad = db[...].astype(F32) + db_far[...].astype(F32)
    back, gain_sum = norm_back(x_mid[...], vec[2 * layer + 1 : 2 * layer + 2, :], grad)
    dx_mid = gy[...].astype(F32) + back
    mid_ref[...] = dx_mid
    sum_ref[...] = rows_of([gain_sum, jnp.sum(dx_mid, axis=0, keepdims=True)], 8, plan.width)
    dz = dx_mid.astype(BF16)
    dz_ref[...] = dz
    do = nn(dz, weight(0)[...]).astype(BF16)
    allowed = allowed_keys(plan, meta)
    each = plan.group // len(dkv)
    for pair in range(n // LANES):
        lanes = slice(pair * LANES, (pair + 1) * LANES)
        late = slice(n + pair * LANES, n + (pair + 1) * LANES)
        q2 = pair_rows(q_ref[:, lanes])
        do2 = pair_rows(do[:, lanes])
        keys = jnp.concatenate([kv[:, lanes] for kv in kvs], axis=0)
        values = jnp.concatenate([kv[:, late] for kv in kvs], axis=0)
        prob = jnp.exp(nt(keys, q2) * scale - total[pair : pair + 1, :])
        prob = jnp.where(allowed, prob, 0.0)
        dprob = nt(values, do2)
        delta = jnp.sum(prob * dprob, axis=0, keepdims=True)
        dscore = (prob * (dprob - delta)).astype(BF16)
        dq_ref[:, lanes] = (pair_lanes(tn(dscore, keys)) * scale).astype(BF16)
        dk = (nn(dscore, q2) * scale).astype(BF16)
        dv = nn(prob.astype(BF16), do2).astype(BF16)
        for i, ref in enumerate(dkv):
            ref[:, lanes] = dk[i * each : (i + 1) * each]
            ref[:, late] = dv[i * each : (i + 1) * each]


def project_back_body(plan, meta, ins, weight, outs, own):
    dq = ins[0]
    dqkv_ref, da_ref, sum_ref = outs
    n = plan.heads_width
    dkv = ins[1][: plan.rows].astype(F32)
    for term in ins[2:]:
        dkv = dkv + term[: plan.rows].astype(F32)
    dkv = dkv.astype(BF16)
    dqkv_ref[:, :n] = dq[...]
    dqkv_ref[:, n:] = dkv
    da_ref[...] = nt(dqkv_ref[...], weight(0)[...]).astype(BF16)
    sums = [
        jnp.sum(dq[...].astype(F32), axis=0, keepdims=True),
        jnp.sum(dkv[:, n:].astype(F32), axis=0, keepdims=True),
    ]
    sum_ref[...] = rows_of([jnp.concatenate(sums, axis=1)], 8, 2 * n)


def weight_grad_body(plan, widths, meta, ins, weight, outs, own):
    packet, sems = own
    column = 0
    for i, width in enumerate(widths):
        left, right = ins[2 * i], ins[2 * i + 1]
        for j in range(0, width, CHUNK):
            size = min(CHUNK, width - j)
            value = tn(left[...], right[:, j : j + size])
            packet[:, column : column + size] = value.astype(BF16)
            column += size
    if not plan.blocks:
        copies = [pltpu.make_async_copy(packet, outs[0], sems.at[0])]
    else:
        copies = []
        for place, offset in enumerate(ORDER):
            for shift in range(plan.shards):
                z = lax.rem(meta[0] + shift, plan.shards)
                index = z * plan.contexts + jnp.bitwise_xor(meta[1], offset)
                row = pl.multiple_of(index * plan.block, 16)
                copies.append(
                    pltpu.make_async_copy(
                        packet.at[pl.ds(row, plan.block), :],
                        outs[place // 2].at[place % 2, shift],
                        sems.at[place * plan.shards + shift],
                    )
                )
    for copy in copies:
        copy.start()
    for copy in copies:
        copy.wait()


def end_body(plan, meta, ins, weight, outs, own):
    dx_mid, x, da, da_far, vec = ins[:5]
    feed0, attn0, proj0, feed1, attn1, proj1 = ins[5:]
    gy_ref, small_ref = outs
    grad = da[...].astype(F32) + da_far[...].astype(F32)
    back, gain_sum = norm_back(x[...], vec[:1, :], grad)
    gy = dx_mid[...] + back
    gy_ref[...] = gy
    lane = lax.broadcasted_iota(jnp.int32, (1, plan.rows), 1)
    seg = segment(plan, meta, meta[1] * plan.rows + lane)
    member = (seg == lax.broadcasted_iota(jnp.int32, (16, plan.rows), 0)).astype(F32)
    sums = lax.dot_general(
        member, gy, (((1,), (0,)), ((), ())), precision=lax.Precision.HIGHEST, preferred_element_type=F32
    )
    halves = plan.hidden // plan.width
    parts = [sums]
    for gain_row, feed, attn, proj in (
        (gain_sum, feed0, attn0, proj0),
        (feed0[1 + halves : 2 + halves, :], feed1, attn1, proj1),
    ):
        parts += [gain_row, attn[0:1, :], attn[1:2, :], feed[0:1, :]]
        parts += [feed[1 + i : 2 + i, :] for i in range(halves)]
        parts += [proj[0:1, :]]
    small_ref[...] = rows_of_total(parts, 32, plan.width).astype(BF16)


def rows_of_total(parts, count, width):
    have = sum(part.shape[0] for part in parts)
    return jnp.concatenate(parts + [jnp.zeros((count - have, width), F32)], axis=0)


def swap_core(array):
    return lax.ppermute(array, "ctx", [(i, i ^ 1) for i in range(4)])


def swap_chip(array):
    return lax.ppermute(array, "ctx", [(i, i ^ 2) for i in range(4)])


def swap_tp(array):
    return lax.ppermute(array, "tp", [(0, 1), (1, 0)])


def to_shard(plan, array, shift):
    n = plan.shards
    return lax.ppermute(array, "shard", [(i, (i + shift) % n) for i in range(n)])


def along_shard(plan, pieces):
    got = [pieces[0]] + [to_shard(plan, pieces[k], k) for k in range(1, plan.shards)]
    return jnp.stack(got)


def across_chip(stack):
    far = swap_chip(stack)
    return (stack, far, swap_core(stack), swap_core(far))


def gather_rows(plan, packet):
    if plan.blocks:
        return across_chip(along_shard(plan, [packet] * plan.shards))
    return (lax.all_gather(packet, ("shard", "ctx"), axis=0, tiled=True),)


def gather_keys(plan, kv):
    if plan.blocks:
        far = swap_chip(kv)
        return (kv, far, swap_core(kv), swap_core(far))
    return (lax.all_gather(kv, "ctx", axis=0, tiled=True),)


def add(*terms):
    total = terms[0].astype(F32)
    for term in terms[1:]:
        total = total + term.astype(F32)
    return total


def weight_grad(plan, meta, name, pairs):
    widths = tuple(right.shape[1] for _, right in pairs)
    width = sum(widths)
    if plan.blocks:
        part = shape(2, plan.shards, plan.block, width)
        outs, copies = [part, part], plan.shards * 4
    else:
        outs, copies = [shape(plan.width, width)], 1
    parts = run(
        plan,
        functools.partial(weight_grad_body, plan, widths),
        name,
        meta,
        [array for pair in pairs for array in pair],
        [],
        outs,
        2 * plan.rows * plan.width * width,
        scratch=[pltpu.VMEM((plan.width, width), BF16), pltpu.SemaphoreType.DMA((copies,))],
        direct=tuple(range(len(outs))),
    )
    if not plan.blocks:
        return lax.psum_scatter(parts[0], ("shard", "ctx"), scatter_dimension=0, tiled=True).astype(F32)
    keep, send = parts
    near = swap_core(send)
    far = swap_chip(add(keep[1], near[1]).astype(BF16))
    sums = [add(keep[0, k], near[0, k], far[k]) for k in range(plan.shards)]
    got = [to_shard(plan, sums[k].astype(BF16), k) for k in range(1, plan.shards)]
    return add(sums[0], *got)


def per_device(
    tokens,
    timesteps,
    cont_lengths,
    table,
    w_qkv,
    w_out,
    w_up,
    w_down,
    norms,
    query_bias,
    value_bias,
    up_bias,
    out_biases,
    cotangent,
):
    rows, width = tokens.shape
    layers, block = w_qkv.shape[:2]
    heads_width, hidden = w_qkv.shape[3], w_up.shape[2]
    shards, contexts = lax.axis_size("shard"), lax.axis_size("ctx")
    conts = cont_lengths.shape[1]
    plan = Plan(rows, width, block, heads_width, hidden, shards, contexts, conts)
    z, c = lax.axis_index("shard"), lax.axis_index("ctx")
    meta = jnp.concatenate([jnp.stack([z, c]).astype(jnp.int32), jnp.cumsum(cont_lengths[0])])

    vectors = jnp.concatenate(
        [norms[0], norms[1], out_biases[0], out_biases[1]], axis=1
    )
    seqs = conts + 1
    steps_all = lax.all_gather(timesteps, "shard", axis=0, tiled=True)
    steps_near = jnp.roll(steps_all, -z, axis=0).reshape(-1)
    one_hot = (steps_near[:, None] == jnp.arange(table.shape[0], dtype=jnp.int32)[None, :]).astype(BF16)
    looked = lax.dot_general(
        table, one_hot, (((0,), (1,)), ((), ())), preferred_element_type=F32
    ).astype(BF16)
    blank = jnp.zeros((block, LANES - vectors.shape[1] - seqs), BF16)
    if plan.blocks:
        small = along_shard(
            plan,
            [
                jnp.concatenate([vectors, looked[:, k * seqs : (k + 1) * seqs], blank], axis=1)
                for k in range(shards)
            ],
        )
        first = along_shard(plan, [w_qkv[0].reshape(block, -1)] * shards)
        first = across_chip(jnp.concatenate([first, small], axis=2))
        small_of = (first, 3 * heads_width, LANES)
    else:
        looked = jnp.roll(looked.reshape(block, shards, seqs), z, axis=1).reshape(block, -1)
        every = lax.all_gather(jnp.concatenate([vectors, looked], axis=1), ("shard", "ctx"), axis=0, tiled=True)
        mine = lax.dynamic_slice_in_dim(every, 8 + z * seqs, seqs, axis=1)
        blank = jnp.zeros((width, LANES - 8 - seqs), BF16)
        small_of = ((jnp.concatenate([every[:, :8], mine, blank], axis=1),), 0, LANES)
        first = gather_rows(plan, w_qkv[0].reshape(block, -1))
    n3 = 3 * heads_width
    second = gather_rows(plan, jnp.concatenate([w_out[0], w_up[0]], axis=1))
    third = gather_rows(plan, w_down[0])
    fourth = gather_rows(plan, jnp.concatenate([w_qkv[1].reshape(block, -1), w_out[1]], axis=1))
    fifth = gather_rows(plan, jnp.concatenate([w_up[1], w_down[1]], axis=1))
    of_qkv = [(first, 0, n3), (fourth, 0, n3)]
    of_out = [(second, 0, heads_width), (fourth, n3, heads_width)]
    of_up = [(second, heads_width, hidden), (fifth, 0, hidden)]
    of_down = [(third, 0, hidden), (fifth, hidden, hidden)]

    mm = 2 * rows * width
    full = shape(rows, width, dtype=F32)
    low = shape(rows, width)
    heads = shape(rows, heads_width)
    wide = shape(rows, hidden)
    sums = shape(8, width, dtype=F32)
    qkv_outs = [low, heads, shape(rows, 2 * heads_width)]
    attn_flops = 4 * rows * plan.group * heads_width

    saved = []
    x_mid = part = part_far = None
    for layer in range(layers):
        if layer == 0:
            x, vec, a, q, kv = run(
                plan,
                functools.partial(embed_body, plan),
                "embed",
                meta,
                [tokens, query_bias, value_bias],
                [of_qkv[0], small_of],
                [full, sums, *qkv_outs],
                mm * n3,
            )
        else:
            x, a, q, kv = run(
                plan,
                functools.partial(next_body, plan, layer),
                "project",
                meta,
                [x_mid, part, part_far, vec, query_bias, value_bias],
                [of_qkv[layer]],
                [full, *qkv_outs],
                mm * n3,
            )
        kvs = gather_keys(plan, kv)
        part, o, total = run(
            plan,
            functools.partial(attend_body, plan),
            "attend",
            meta,
            [q, *kvs],
            [of_out[layer]],
            [low, heads, shape(8, 2 * rows, dtype=F32)],
            mm * heads_width + attn_flops,
        )
        part_far = swap_tp(part)
        last = layer == layers - 1
        outs = [full, low, wide, shape(rows, hidden, dtype=F32), low]
        if last:
            outs += [wide, low, sums]
        got = run(
            plan,
            functools.partial(feed_body, plan, layer, last),
            "feed",
            meta,
            [x, part, part_far, vec, up_bias] + ([cotangent] if last else []),
            [of_up[layer], of_down[layer]],
            outs,
            mm * hidden * (4 if last else 2),
        )
        x_mid, b, gelu, slope, part = got[:5]
        part_far = swap_tp(part)
        saved.append((x, a, q, kvs, o, total, x_mid, b, gelu, slope))

    bias_last = vec[2 * layers + 3][None, :]
    activations = (x_mid + add(part, part_far) + bias_last).astype(BF16)

    gy = dy = cotangent
    dh, db, feed_sum = got[5:]
    grads, small_sums = [None] * layers, [None] * layers
    for layer in reversed(range(layers)):
        x, a, q, kvs, o, total, x_mid, b, gelu, slope = saved[layer]
        if layer < layers - 1:
            gy, dy, dh, db, feed_sum = run(
                plan,
                functools.partial(between_body, plan, layer),
                "feed_back",
                meta,
                [dx_mid, saved[layer + 1][0], da, da_far, vec, slope],
                [of_up[layer], of_down[layer]],
                [full, low, wide, low, sums],
                2 * mm * hidden,
            )
        db_far = swap_tp(db)
        feed_grad = weight_grad(plan, meta, "feed_grad", [(b, dh), (dy, gelu)])
        if plan.blocks:
            dkv_outs = [shape(2 * rows, 2 * heads_width)] * 2
        else:
            dkv_outs = [shape(plan.group, 2 * heads_width)]
        dx_mid, dz, dq, attn_sum, *dkv = run(
            plan,
            functools.partial(attend_back_body, plan, layer),
            "attend_back",
            meta,
            [gy, x_mid, db, db_far, vec, q, total, *kvs],
            [of_out[layer]],
            [full, low, heads, sums, *dkv_outs],
            mm * heads_width + 10 * rows * plan.group * heads_width,
        )
        if plan.blocks:
            keep, send = dkv
            near = swap_core(send)
            far = swap_chip(add(keep[rows:], near[rows:]).astype(BF16))
            terms = [keep, near, far]
        else:
            terms = [lax.psum_scatter(dkv[0], "ctx", scatter_dimension=0, tiled=True)]
        dqkv, da, proj_sum = run(
            plan,
            functools.partial(project_back_body, plan),
            "project_back",
            meta,
            [dq, *terms],
            [of_qkv[layer]],
            [shape(rows, n3), low, shape(8, 2 * heads_width, dtype=F32)],
            mm * n3,
        )
        da_far = swap_tp(da)
        attn_grad = weight_grad(plan, meta, "attn_grad", [(a, dqkv), (dz, o)])
        grads[layer] = (feed_grad, attn_grad)
        small_sums[layer] = [feed_sum, attn_sum, proj_sum]

    grad_tokens, packet = run(
        plan,
        functools.partial(end_body, plan),
        "end",
        meta,
        [dx_mid, saved[0][0], da, da_far, vec, *small_sums[0], *small_sums[1]],
        [],
        [full, shape(32, width)],
        mm * 32,
    )
    start = (z * contexts + c) * block
    if plan.blocks:
        packet = add(packet, swap_core(packet)).astype(BF16)
        packet = add(packet, swap_chip(packet)).astype(BF16)
        got = along_shard(plan, [packet] * shards)
        other = add(*[got[k] for k in range(0, shards, 2)]) + add(*[got[k] for k in range(1, shards, 2)])
        steps_back = jnp.roll(steps_all[::-1], z + 1, axis=0)
    else:
        packet = lax.psum(packet, "ctx")
        got = lax.all_gather(packet, "shard", axis=0)
        other = jnp.sum(got.astype(F32), axis=0)
        steps_back = steps_all
    mine = lax.dynamic_slice_in_dim(got[:, :seqs], start, block, axis=2).reshape(-1, block)
    one_hot = (jnp.arange(table.shape[0], dtype=jnp.int32)[:, None] == steps_back.reshape(-1)[None, :]).astype(BF16)
    grad_table = jnp.dot(one_hot, mine, preferred_element_type=F32)

    halves = hidden // width
    per_layer = 5 + halves
    by_layer = other[16 : 16 + layers * per_layer].reshape(layers, per_layer, width)
    local = lax.dynamic_slice_in_dim(by_layer[:, :4], start, block, axis=2)
    grad_norms = jnp.moveaxis(local[:, :2], 1, 2)
    grad_out_biases = jnp.moveaxis(local[:, 2:], 1, 2)
    grad_up_bias = by_layer[:, 4 : 4 + halves].reshape(layers, hidden)
    grad_query_bias = by_layer[:, 4 + halves, :heads_width]
    grad_value_bias = by_layer[:, 4 + halves, heads_width:]
    feeds = [grads[layer][0] for layer in range(layers)]
    attns = [grads[layer][1] for layer in range(layers)]
    return (
        activations,
        grad_tokens,
        jnp.stack([g[:, :n3].reshape(block, 3, heads_width) for g in attns]),
        jnp.stack([g[:, n3:] for g in attns]),
        jnp.stack([g[:, :hidden] for g in feeds]),
        jnp.stack([g[:, hidden:] for g in feeds]),
        grad_norms,
        grad_table,
        grad_query_bias,
        grad_value_bias,
        grad_up_bias,
        grad_out_biases,
    )


def solution(mesh):
    placed = (
        P(("shard", "ctx"), None),
        P("shard", None),
        P("shard", None),
        P(None, ("shard", "ctx")),
        P(None, ("shard", "ctx"), None, "tp"),
        P(None, ("shard", "ctx"), "tp"),
        P(None, ("shard", "ctx"), "tp"),
        P(None, ("shard", "ctx"), "tp"),
        P(None, ("shard", "ctx"), None),
        P(None, "tp"),
        P(None, "tp"),
        P(None, "tp"),
        P(None, ("shard", "ctx"), None),
        P(("shard", "ctx"), None),
    )
    return jax.shard_map(
        per_device,
        mesh=mesh,
        in_specs=placed,
        out_specs=(
            P(("shard", "ctx"), None),
            P(("shard", "ctx"), None),
            P(None, ("shard", "ctx"), None, "tp"),
            P(None, ("shard", "ctx"), "tp"),
            P(None, ("shard", "ctx"), "tp"),
            P(None, ("shard", "ctx"), "tp"),
            P(None, ("shard", "ctx"), None),
            P(None, ("shard", "ctx")),
            P(None, "tp"),
            P(None, "tp"),
            P(None, "tp"),
            P(None, ("shard", "ctx"), None),
        ),
        check_vma=False,
    )
```

time: 1250 us -> 451 us (0.36)
  the two profiles are of different devices: /device:TPU:0 before, /device:TPU:28 now
where the time goes in v1:
time: 451 us; the launch traced here: 445 us
  waiting for transfers between devices  199 us (44%)
  starting transfers between devices  95.3 us (21%)
  Pallas kernels  60.9 us (14%)
  local copies, waits for them, and re-layouts  44.4 us (10%)
  other arithmetic  31.9 us (7%)
  blocking collectives  9.58 us (2%)
    ppermute x14, waiting for transfers between devices, swap_chip(): return lax.ppermute(array, 'ctx', [(i, i ^ 2) for i in range(4)])  83.5 us
    ppermute x33, waiting for transfers between devices, to_shard(): lax.ppermute(array, 'shard', [(i, (i + shift) % n) for i in range(n)])  74.8 us
    ppermute x33, starting transfers between devices, to_shard(): lax.ppermute(array, 'shard', [(i, (i + shift) % n) for i in range(n)])  65.8 us
    pallas_call x16, Pallas kernels, run(): pl.pallas_call(kernel, name=name, out_shape=tuple(outs), in_specs=[pl.Blo...  60.9 us
    ppermute x8, waiting for transfers between devices, swap_tp(): return lax.ppermute(array, 'tp', [(0, 1), (1, 0)])  35.2 us
    unnamed x190, local copies, waits for them, and re-layouts  27.7 us
    ppermute x14, starting transfers between devices, swap_chip(): return lax.ppermute(array, 'ctx', [(i, i ^ 2) for i in range(4)])  21.9 us
    all_gather x1, blocking collectives, per_device(): steps_all = lax.all_gather(timesteps, 'shard', axis=0, tiled=True)  9.58 us
  transfers between devices with their start and end apart: 76, of which 31 were waited for; matrix products, arithmetic and copies ran while one was open for 11% of the time, Pallas kernels for 9%

profile of v1, /device:TPU:28, one launch (start us, length us, event | category | flops | bytes accessed | tf_op | source)
XLA Modules:
  0.0 445.5 jit_solution(6708928314166033551)
XLA Ops:
  3.8 9.6 %all-gather = s32[4,1,9]{2,1,0:T(1,128)S(1)} all-gather(s32[1,1,9]{2,1,0:T(1,128)} %bitcast.244), channel_id=1, replica_groups=mesh['shard'=4,'ctx'=4,'tp'=2] {'shard'}, dimensions={0}, use_global_device_ids=true | all-gather | bytes 180 | tf_op jit(solution)/shard_map/all_gather | solution.py:518
  34.9 8.9 %collective-permute-done.20 = bf16[48,1536]{1,0:T(8,128)(2,1)S(1)} collective-permute-done((bf16[48,1536]{1,0:T(8,128)(2,1)}, bf16[48,1536]{1,0:T(8,128)(2,1)S(1)}, u32[]{:S(2)}, u32[]{:S(2)}) %collective-permute-start.20) | collective-permute-done | bytes 147488 | tf_op jit(solution)/shard_map/ppermute | solution.py:426
  47.5 5.9 %collective-permute-start.14 = (bf16[48,1920]{1,0:T(8,128)(2,1)S(1)}, bf16[48,1920]{1,0:T(8,128)(2,1)S(1)}, u32[]{:S(2)}, u32[]{:S(2)}) collective-permute-start(bf16[48,1920]{1,0:T(8,128)(2,1)S(1)} %get-tuple-element.196), channel_id=1, source_target_pairs={{0,24},{8,0},{16,8},{24,16},{1,25},{9,1},{17,9},{25,17},{2,26},{10... | collective-permute-start | bytes 552968 | tf_op jit(solution)/shard_map/ppermute | solution.py:426
  53.5 5.5 %collective-permute-done.27 = bf16[48,1536]{1,0:T(8,128)(2,1)S(1)} collective-permute-done((bf16[48,1536]{1,0:T(8,128)(2,1)S(1)}, bf16[48,1536]{1,0:T(8,128)(2,1)S(1)}, u32[]{:S(2)}, u32[]{:S(2)}) %collective-permute-start.27) | collective-permute-done | bytes 147488 | tf_op jit(solution)/shard_map/ppermute | solution.py:426
  65.8 13.7 %collective-permute-done.13 = bf16[48,1920]{1,0:T(8,128)(2,1)S(1)} collective-permute-done((bf16[48,1920]{1,0:T(8,128)(2,1)S(1)}, bf16[48,1920]{1,0:T(8,128)(2,1)S(1)}, u32[]{:S(2)}, u32[]{:S(2)}) %collective-permute-start.13) | collective-permute-done | bytes 184352 | tf_op jit(solution)/shard_map/ppermute | solution.py:426
  81.8 8.4 %collective-permute-done.37 = bf16[48,3072]{1,0:T(8,128)(2,1)S(1)} collective-permute-done((bf16[48,3072]{1,0:T(8,128)(2,1)S(1)}, bf16[48,3072]{1,0:T(8,128)(2,1)S(1)}, u32[]{:S(2)}, u32[]{:S(2)}) %collective-permute-start.37) | collective-permute-done | bytes 294944 | tf_op jit(solution)/shard_map/ppermute | solution.py:426
  95.1 10.1 %collective-permute-done.22.refs_10_.refs_11_ = bf16[4,48,1536]{2,1,0:T(8,128)(2,1)} collective-permute-done((bf16[4,48,1536]{2,1,0:T(8,128)(2,1)S(1)}, bf16[4,48,1536]{2,1,0:T(8,128)(2,1)}, u32[]{:S(2)}, u32[]{:S(2)}) %collective-permute-start.22) | collective-permute-done | bytes 589856 | tf_op jit(solution)/shard_map/ppermute | solution.py:417
  108.4 12.4 %collective-permute-done.15.refs_6_.refs_7_.refs_12_ = bf16[4,48,1920]{2,1,0:T(8,128)(2,1)S(1)} collective-permute-done((bf16[4,48,1920]{2,1,0:T(8,128)(2,1)S(1)}, bf16[4,48,1920]{2,1,0:T(8,128)(2,1)S(1)}, u32[]{:S(2)}, u32[]{:S(2)}) %collective-permute-start.15) | collective-permute-done | bytes 737312 | tf_op jit(solution)/shard_map/ppermute | solution.py:417
  129.0 27.0 %collective-permute-done.29.refs_7_.refs_6_.refs_12_.refs_5_ = bf16[4,48,1536]{2,1,0:T(8,128)(2,1)} collective-permute-done((bf16[4,48,1536]{2,1,0:T(8,128)(2,1)S(1)}, bf16[4,48,1536]{2,1,0:T(8,128)(2,1)}, u32[]{:S(2)}, u32[]{:S(2)}) %collective-permute-start.29) | collective-permute-done | bytes 589856 | tf_op jit(solution)/shard_map/ppermute | solution.py:417
  168.0 6.4 %collective-permute-done.18.refs_2_ = bf16[128,768]{1,0:T(8,128)(2,1)S(1)} collective-permute-done((bf16[128,768]{1,0:T(8,128)(2,1)S(1)}, bf16[128,768]{1,0:T(8,128)(2,1)S(1)}, u32[]{:S(2)}, u32[]{:S(2)}) %collective-permute-start.18) | collective-permute-done | bytes 196640 | tf_op jit(solution)/shard_map/ppermute | solution.py:421
  174.5 6.1 %feed.2 = (f32[128,768]{1,0:T(8,128)S(1)}, bf16[128,768]{1,0:T(8,128)(2,1)S(1)}, bf16[128,1536]{1,0:T(8,128)(2,1)S(1)}, f32[128,1536]{1,0:T(8,128)S(1)}, bf16[128,768]{1,0:T(8,128)(2,1)S(1)}) custom-call(s32[10]{0:T(128)S(1)} %pad_add_fusion.2.meta_ref, f32[128,768]{1,0:T(8,128)S(1)} %get-tuple-element.73.refs_0_.refs_1_, ...), custom_call_target="tpu_custom_call" | custom-call | flops 603979776 | bytes 7501824 | tf_op jit(solution)/shard_map/feed/pallas_call | solution.py:124
  181.8 5.6 %collective-permute-done.25.refs_2_ = bf16[128,768]{1,0:T(8,128)(2,1)S(1)} collective-permute-done((bf16[128,768]{1,0:T(8,128)(2,1)S(1)}, bf16[128,768]{1,0:T(8,128)(2,1)S(1)}, u32[]{:S(2)}, u32[]{:S(2)}) %collective-permute-start.25) | collective-permute-done | bytes 196640 | tf_op jit(solution)/shard_map/ppermute | solution.py:421
  201.7 6.4 %collective-permute-done.35.refs_2_ = bf16[128,768]{1,0:T(8,128)(2,1)S(1)} collective-permute-done((bf16[128,768]{1,0:T(8,128)(2,1)S(1)}, bf16[128,768]{1,0:T(8,128)(2,1)S(1)}, u32[]{:S(2)}, u32[]{:S(2)}) %collective-permute-start.35) | collective-permute-done | bytes 196640 | tf_op jit(solution)/shard_map/ppermute | solution.py:421
  208.1 5.6 %feed.3 = (f32[128,768]{1,0:T(8,128)S(1)}, bf16[128,768]{1,0:T(8,128)(2,1)S(1)}, bf16[128,1536]{1,0:T(8,128)(2,1)S(1)}, f32[128,1536]{1,0:T(8,128)}, bf16[128,76...) custom-call(s32[10]{0:T(128)S(1)} %pad_add_fusion.2.meta_ref, ...), custom_call_target="tpu_custom_call" | custom-call | flops 1207959552 | bytes 8312832 | tf_op jit(solution)/shard_map/feed/pallas_call | solution.py:124
  215.1 5.6 %collective-permute-done.43.refs_3_ = bf16[128,768]{1,0:T(8,128)(2,1)S(1)} collective-permute-done((bf16[128,768]{1,0:T(8,128)(2,1)S(1)}, bf16[128,768]{1,0:T(8,128)(2,1)S(1)}, u32[]{:S(2)}, u32[]{:S(2)}) %collective-permute-start.43) | collective-permute-done | bytes 196640 | tf_op jit(solution)/shard_map/ppermute | solution.py:421
  228.6 5.2 %collective-permute-done.45.refs_3_ = bf16[128,768]{1,0:T(8,128)(2,1)S(1)} collective-permute-done((bf16[128,768]{1,0:T(8,128)(2,1)S(1)}, bf16[128,768]{1,0:T(8,128)(2,1)S(1)}, u32[]{:S(2)}, u32[]{:S(2)}) %collective-permute-start.45) | collective-permute-done | bytes 196640 | tf_op jit(solution)/shard_map/ppermute | solution.py:417
  236.9 5.9 %collective-permute-done.46.refs_3_ = bf16[128,768]{1,0:T(8,128)(2,1)S(1)} collective-permute-done((bf16[128,768]{1,0:T(8,128)(2,1)S(1)}, bf16[128,768]{1,0:T(8,128)(2,1)S(1)}, u32[]{:S(2)}, u32[]{:S(2)}) %collective-permute-start.46) | collective-permute-done | bytes 196640 | tf_op jit(solution)/shard_map/ppermute | solution.py:421
  242.8 5.9 %feed_back.1 = (f32[128,768]{1,0:T(8,128)S(1)}, bf16[128,768]{1,0:T(8,128)(2,1)S(1)}, bf16[128,1536]{1,0:T(8,128)(2,1)S(1)}, bf16[128,768]{1,0:T(8,128)(2,1)S(1)}, f32[8,768]{1,0:T(8,128)S(1)}) custom-call(s32[10]{0:T(128)S(1)} %pad_add_fusion.2.meta_ref, f32[128,768]{1,0:T(8,128)S(1)} %get-tuple-element.88.refs_0_, ...), custom_call_target="tpu_custom_call" | custom-call | flops 603979776 | bytes 7913472 | tf_op jit(solution)/shard_map/feed_back/pallas_call | solution.py:124
  249.9 5.2 %collective-permute-done.47.refs_3_ = bf16[128,768]{1,0:T(8,128)(2,1)S(1)} collective-permute-done((bf16[128,768]{1,0:T(8,128)(2,1)S(1)}, bf16[128,768]{1,0:T(8,128)(2,1)S(1)}, u32[]{:S(2)}, u32[]{:S(2)}) %collective-permute-start.47) | collective-permute-done | bytes 196640 | tf_op jit(solution)/shard_map/ppermute | solution.py:421
  334.1 7.2 %collective-permute-done.59 = bf16[48,1536]{1,0:T(8,128)(2,1)S(1)} collective-permute-done((bf16[48,1536]{1,0:T(8,128)(2,1)S(1)}, bf16[48,1536]{1,0:T(8,128)(2,1)S(1)}, u32[]{:S(2)}, u32[]{:S(2)}) %collective-permute-start.59) | collective-permute-done | bytes 147488 | tf_op jit(solution)/shard_map/ppermute | solution.py:426
  353.1 21.3 %collective-permute-done.52 = bf16[4,48,1536]{2,1,0:T(8,128)(2,1)S(1)} collective-permute-done((bf16[4,48,1536]{2,1,0:T(8,128)(2,1)S(1)}, bf16[4,48,1536]{2,1,0:T(8,128)(2,1)S(1)}, u32[]{:S(2)}, u32[]{:S(2)}) %collective-permute-start.52) | collective-permute-done | bytes 589856 | tf_op jit(solution)/shard_map/ppermute | solution.py:417
  379.4 5.5 %collective-permute-start.54 = (bf16[48,1536]{1,0:T(8,128)(2,1)S(1)}, bf16[48,1536]{1,0:T(8,128)(2,1)S(1)}, u32[]{:S(2)}, u32[]{:S(2)}) collective-permute-start(bf16[48,1536]{1,0:T(8,128)(2,1)S(1)} %get-tuple-element.177), channel_id=1, source_target_pairs={{0,16},{8,24},{16,0},{24,8},{1,17},{9,25},{17,1},{25,9},{2,18},{10... | collective-permute-start | bytes 442376 | tf_op jit(solution)/shard_map/ppermute | solution.py:426
  406.5 4.9 %collective-permute-done.69 = bf16[48,3072]{1,0:T(8,128)(2,1)} collective-permute-done((bf16[48,3072]{1,0:T(8,128)(2,1)}, bf16[48,3072]{1,0:T(8,128)(2,1)}, u32[]{:S(2)}, u32[]{:S(2)}) %collective-permute-start.69) | collective-permute-done | bytes 294944 | tf_op jit(solution)/shard_map/ppermute | solution.py:426
  424.7 17.9 %collective-permute-done.64 = bf16[48,3072]{1,0:T(8,128)(2,1)S(1)} collective-permute-done((bf16[48,3072]{1,0:T(8,128)(2,1)S(1)}, bf16[48,3072]{1,0:T(8,128)(2,1)S(1)}, u32[]{:S(2)}, u32[]{:S(2)}) %collective-permute-start.64) | collective-permute-done | bytes 294944 | tf_op jit(solution)/shard_map/ppermute | solution.py:426
  (410 shorter events, 226.8 us)
Async XLA Ops:
  28.1 30.9 %collective-permute-start.27 = (bf16[48,1536]{1,0:T(8,128)(2,1)S(1)}, bf16[48,1536]{1,0:T(8,128)(2,1)S(1)}, u32[]{:S(2)}, u32[]{:S(2)}) collective-permute-start(bf16[48,1536]{1,0:T(8,128)(2,1)S(1)} %get-tuple-element.198), channel_id=1, source_target_pairs={{0,16},{8,24},{16,0},{24,8},{1,17},{9,25},{17,1},{25,9},{2,18},{10... | collective-permute-start | bytes 442376 | tf_op jit(solution)/shard_map/ppermute | solution.py:426
  31.4 28.3 %collective-permute-start.28 = (bf16[48,1536]{1,0:T(8,128)(2,1)S(1)}, bf16[48,1536]{1,0:T(8,128)(2,1)S(1)}, u32[]{:S(2)}, u32[]{:S(2)}) collective-permute-start(bf16[48,1536]{1,0:T(8,128)(2,1)S(1)} %get-tuple-element.198), channel_id=1, source_target_pairs={{0,24},{8,0},{16,8},{24,16},{1,25},{9,1},{17,9},{25,17},{2,26},{10... | collective-permute-start | bytes 442376 | tf_op jit(solution)/shard_map/ppermute | solution.py:426
  44.9 34.7 %collective-permute-start.13 = (bf16[48,1920]{1,0:T(8,128)(2,1)S(1)}, bf16[48,1920]{1,0:T(8,128)(2,1)S(1)}, u32[]{:S(2)}, u32[]{:S(2)}) collective-permute-start(bf16[48,1920]{1,0:T(8,128)(2,1)S(1)} %get-tuple-element.196), channel_id=1, source_target_pairs={{0,16},{8,24},{16,0},{24,8},{1,17},{9,25},{17,1},{25,9},{2,18},{10... | collective-permute-start | bytes 552968 | tf_op jit(solution)/shard_map/ppermute | solution.py:426
  47.5 33.5 %collective-permute-start.14 = (bf16[48,1920]{1,0:T(8,128)(2,1)S(1)}, bf16[48,1920]{1,0:T(8,128)(2,1)S(1)}, u32[]{:S(2)}, u32[]{:S(2)}) collective-permute-start(bf16[48,1920]{1,0:T(8,128)(2,1)S(1)} %get-tuple-element.196), channel_id=1, source_target_pairs={{0,24},{8,0},{16,8},{24,16},{1,25},{9,1},{17,9},{25,17},{2,26},{10... | collective-permute-start | bytes 552968 | tf_op jit(solution)/shard_map/ppermute | solution.py:426
  59.7 30.6 %collective-permute-start.37 = (bf16[48,3072]{1,0:T(8,128)(2,1)S(1)}, bf16[48,3072]{1,0:T(8,128)(2,1)S(1)}, u32[]{:S(2)}, u32[]{:S(2)}) collective-permute-start(bf16[48,3072]{1,0:T(8,128)(2,1)S(1)} %get-tuple-element.186), channel_id=1, source_target_pairs={{0,16},{8,24},{16,0},{24,8},{1,17},{9,25},{17,1},{25,9},{2,18},{10... | collective-permute-start | bytes 884744 | tf_op jit(solution)/shard_map/ppermute | solution.py:426
  63.0 27.2 %collective-permute-start.38 = (bf16[48,3072]{1,0:T(8,128)(2,1)S(1)}, bf16[48,3072]{1,0:T(8,128)(2,1)S(1)}, u32[]{:S(2)}, u32[]{:S(2)}) collective-permute-start(bf16[48,3072]{1,0:T(8,128)(2,1)S(1)} %get-tuple-element.186), channel_id=1, source_target_pairs={{0,24},{8,0},{16,8},{24,16},{1,25},{9,1},{17,9},{25,17},{2,26},{10... | collective-permute-start | bytes 884744 | tf_op jit(solution)/shard_map/ppermute | solution.py:426
  81.2 23.9 %collective-permute-start.22 = (bf16[4,48,1536]{2,1,0:T(8,128)(2,1)S(1)}, bf16[4,48,1536]{2,1,0:T(8,128)(2,1)}, u32[]{:S(2)}, u32[]{:S(2)}) collective-permute-start(bf16[4,48,1536]{2,1,0:T(8,128)(2,1)S(1)} %pad_maximum_fusion.2.refs_9_.refs_10_), channel_id=1, source_target_pairs={{0,4},{2,6},{4,0},{6,2},{1,5},{3,7},{5,1},{7,3},{8,12},{10,14},{12... | collective-permute-start | bytes 1769480 | tf_op jit(solution)/shard_map/ppermute | solution.py:417
  90.2 30.6 %collective-permute-start.15 = (bf16[4,48,1920]{2,1,0:T(8,128)(2,1)S(1)}, bf16[4,48,1920]{2,1,0:T(8,128)(2,1)S(1)}, u32[]{:S(2)}, u32[]{:S(2)}) collective-permute-start(bf16[4,48,1920]{2,1,0:T(8,128)(2,1)S(1)} %pad_maximum_fusion.1.refs_5_.refs_6_.refs_11_), channel_id=1, source_target_pairs={{0,4},{2,6},{4,0},{6,2},{1,5},{3,7},{5,1},{7,3},{8,12},{10,14},{12... | collective-permute-start | bytes 2211848 | tf_op jit(solution)/shard_map/ppermute | solution.py:417
  92.9 69.7 %collective-permute-start.39 = (bf16[4,48,3072]{2,1,0:T(8,128)(2,1)}, bf16[4,48,3072]{2,1,0:T(8,128)(2,1)}, u32[]{:S(2)}, u32[]{:S(2)}) collective-permute-start(bf16[4,48,3072]{2,1,0:T(8,128)(2,1)} %pad_maximum_fusion.refs_6_.refs_10_), channel_id=1, source_target_pairs={{0,4},{2,6},{4,0},{6,2},{1,5},{3,7},{5,1},{7,3},{8,12},{10,14},{12... | collective-permute-start | bytes 3538952 | tf_op jit(solution)/shard_map/ppermute | solution.py:417
  95.0 26.5 %collective-permute-start.8 = (bf16[4,48,1280]{2,1,0:T(8,128)(2,1)}, bf16[4,48,1280]{2,1,0:T(8,128)(2,1)}, u32[]{:S(2)}, u32[]{:S(2)}) collective-permute-start(bf16[4,48,1280]{2,1,0:T(8,128)(2,1)} %collective-permute-done.6.refs_4_.refs_8_.refs_5_), channel_id=1, source_target_pairs={{0,2},{2,0},{4,6},{6,4},{1,3},{3,1},{5,7},{7,5},{8,10},{10,8},{12,... | collective-permute-start | bytes 1474568 | tf_op jit(solution)/shard_map/ppermute | solution.py:413
  105.1 50.8 %collective-permute-start.29 = (bf16[4,48,1536]{2,1,0:T(8,128)(2,1)S(1)}, bf16[4,48,1536]{2,1,0:T(8,128)(2,1)}, u32[]{:S(2)}, u32[]{:S(2)}) collective-permute-start(bf16[4,48,1536]{2,1,0:T(8,128)(2,1)S(1)} %pad_maximum_fusion.3.refs_6_.refs_5_.refs_11_.refs_4_), channel_id=1, source_target_pairs={{0,4},{2,6},{4,0},{6,2},{1,5},{3,7},{5,1},{7,3},{8,12},{10,14},{12... | collective-permute-start | bytes 1769480 | tf_op jit(solution)/shard_map/ppermute | solution.py:417
  108.4 50.0 %collective-permute-start.16 = (bf16[4,48,1920]{2,1,0:T(8,128)(2,1)S(1)}, bf16[4,48,1920]{2,1,0:T(8,128)(2,1)S(1)}, u32[]{:S(2)}, u32[]{:S(2)}) collective-permute-start(bf16[4,48,1920]{2,1,0:T(8,128)(2,1)S(1)} %pad_maximum_fusion.1.refs_5_.refs_6_.refs_11_), channel_id=1, source_target_pairs={{0,2},{2,0},{4,6},{6,4},{1,3},{3,1},{5,7},{7,5},{8,10},{10,8},{12,... | collective-permute-start | bytes 2211848 | tf_op jit(solution)/shard_map/ppermute | solution.py:413
  120.8 42.9 %collective-permute-start.17 = (bf16[4,48,1920]{2,1,0:T(8,128)(2,1)S(1)}, bf16[4,48,1920]{2,1,0:T(8,128)(2,1)S(1)}, u32[]{:S(2)}, u32[]{:S(2)}) collective-permute-start(bf16[4,48,1920]{2,1,0:T(8,128)(2,1)S(1)} %collective-permute-done.15.refs_6_.refs_7_.refs_12_), channel_id=1, source_target_pairs={{0,2},{2,0},{4,6},{6,4},{1,3},{3,1},{5,7},{7,5},{8,10},{10,8},{12,... | collective-permute-start | bytes 2211848 | tf_op jit(solution)/shard_map/ppermute | solution.py:413
  121.5 46.0 %collective-permute-start.24 = (bf16[4,48,1536]{2,1,0:T(8,128)(2,1)}, bf16[4,48,1536]{2,1,0:T(8,128)(2,1)S(1)}, u32[]{:S(2)}, u32[]{:S(2)}) collective-permute-start(bf16[4,48,1536]{2,1,0:T(8,128)(2,1)} %collective-permute-done.22.refs_10_.refs_11_), channel_id=1, source_target_pairs={{0,2},{2,0},{4,6},{6,4},{1,3},{3,1},{5,7},{7,5},{8,10},{10,8},{12,... | collective-permute-start | bytes 1769480 | tf_op jit(solution)/shard_map/ppermute | solution.py:413
  163.6 38.1 %collective-permute-start.40 = (bf16[4,48,3072]{2,1,0:T(8,128)(2,1)}, bf16[4,48,3072]{2,1,0:T(8,128)(2,1)S(1)}, u32[]{:S(2)}, u32[]{:S(2)}) collective-permute-start(bf16[4,48,3072]{2,1,0:T(8,128)(2,1)} %pad_maximum_fusion.refs_6_.refs_10_), channel_id=1, source_target_pairs={{0,2},{2,0},{4,6},{6,4},{1,3},{3,1},{5,7},{7,5},{8,10},{10,8},{12,... | collective-permute-start | bytes 3538952 | tf_op jit(solution)/shard_map/ppermute | solution.py:413
  163.7 44.4 %collective-permute-start.41 = (bf16[4,48,3072]{2,1,0:T(8,128)(2,1)}, bf16[4,48,3072]{2,1,0:T(8,128)(2,1)S(1)}, u32[]{:S(2)}, u32[]{:S(2)}) collective-permute-start(bf16[4,48,3072]{2,1,0:T(8,128)(2,1)} %collective-permute-done.39.refs_7_.refs_11_), channel_id=1, source_target_pairs={{0,2},{2,0},{4,6},{6,4},{1,3},{3,1},{5,7},{7,5},{8,10},{10,8},{12,... | collective-permute-start | bytes 3538952 | tf_op jit(solution)/shard_map/ppermute | solution.py:413
  272.2 31.2 %collective-permute-start.56 = (bf16[2,4,48,1536]{3,2,1,0:T(8,128)(2,1)}, bf16[2,4,48,1536]{3,2,1,0:T(8,128)(2,1)}, u32[]{:S(2)}, u32[]{:S(2)}) collective-permute-start(bf16[2,4,48,1536]{3,2,1,0:T(8,128)(2,1)} %get-tuple-element.120), channel_id=1, source_target_pairs={{0,2},{2,0},{4,6},{6,4},{1,3},{3,1},{5,7},{7,5},{8,10},{10,8},{12,... | collective-permute-start | bytes 3538952 | tf_op jit(solution)/shard_map/ppermute | solution.py:413
  287.1 41.7 %collective-permute-start.66 = (bf16[2,4,48,3072]{3,2,1,0:T(8,128)(2,1)}, bf16[2,4,48,3072]{3,2,1,0:T(8,128)(2,1)}, u32[]{:S(2)}, u32[]{:S(2)}) collective-permute-start(bf16[2,4,48,3072]{3,2,1,0:T(8,128)(2,1)} %get-tuple-element.131), channel_id=1, source_target_pairs={{0,2},{2,0},{4,6},{6,4},{1,3},{3,1},{5,7},{7,5},{8,10},{10,8},{12,... | collective-permute-start | bytes 7077896 | tf_op jit(solution)/shard_map/ppermute | solution.py:413
  298.2 50.6 %collective-permute-start.61 = (bf16[2,4,48,3072]{3,2,1,0:T(8,128)(2,1)}, bf16[2,4,48,3072]{3,2,1,0:T(8,128)(2,1)}, u32[]{:S(2)}, u32[]{:S(2)}) collective-permute-start(bf16[2,4,48,3072]{3,2,1,0:T(8,128)(2,1)} %get-tuple-element.126), channel_id=1, source_target_pairs={{0,2},{2,0},{4,6},{6,4},{1,3},{3,1},{5,7},{7,5},{8,10},{10,8},{12,... | collective-permute-start | bytes 7077896 | tf_op jit(solution)/shard_map/ppermute | solution.py:413
  308.8 37.7 %collective-permute-start.51 = (bf16[2,4,48,1536]{3,2,1,0:T(8,128)(2,1)}, bf16[2,4,48,1536]{3,2,1,0:T(8,128)(2,1)}, u32[]{:S(2)}, u32[]{:S(2)}) collective-permute-start(bf16[2,4,48,1536]{3,2,1,0:T(8,128)(2,1)} %get-tuple-element.114), channel_id=1, source_target_pairs={{0,2},{2,0},{4,6},{6,4},{1,3},{3,1},{5,7},{7,5},{8,10},{10,8},{12,... | collective-permute-start | bytes 3538952 | tf_op jit(solution)/shard_map/ppermute | solution.py:413
  332.6 52.3 %collective-permute-start.67 = (bf16[4,48,3072]{2,1,0:T(8,128)(2,1)}, bf16[4,48,3072]{2,1,0:T(8,128)(2,1)}, u32[]{:S(2)}, u32[]{:S(2)}) collective-permute-start(bf16[4,48,3072]{2,1,0:T(8,128)(2,1)} %fusion.1), channel_id=1, source_target_pairs={{0,4},{2,6},{4,0},{6,2},{1,5},{3,7},{5,1},{7,3},{8,12},{10,14},{12... | collective-permute-start | bytes 3538952 | tf_op jit(solution)/shard_map/ppermute | solution.py:417
  347.8 26.5 %collective-permute-start.52 = (bf16[4,48,1536]{2,1,0:T(8,128)(2,1)S(1)}, bf16[4,48,1536]{2,1,0:T(8,128)(2,1)S(1)}, u32[]{:S(2)}, u32[]{:S(2)}) collective-permute-start(bf16[4,48,1536]{2,1,0:T(8,128)(2,1)S(1)} %fusion.2), channel_id=1, source_target_pairs={{0,4},{2,6},{4,0},{6,2},{1,5},{3,7},{5,1},{7,3},{8,12},{10,14},{12... | collective-permute-start | bytes 1769480 | tf_op jit(solution)/shard_map/ppermute | solution.py:417
  351.9 61.1 %collective-permute-start.62 = (bf16[4,48,3072]{2,1,0:T(8,128)(2,1)}, bf16[4,48,3072]{2,1,0:T(8,128)(2,1)S(1)}, u32[]{:S(2)}, u32[]{:S(2)}) collective-permute-start(bf16[4,48,3072]{2,1,0:T(8,128)(2,1)} %fusion), channel_id=1, source_target_pairs={{0,4},{2,6},{4,0},{6,2},{1,5},{3,7},{5,1},{7,3},{8,12},{10,14},{12... | collective-permute-start | bytes 3538952 | tf_op jit(solution)/shard_map/ppermute | solution.py:417
  417.2 25.4 %collective-permute-start.64 = (bf16[48,3072]{1,0:T(8,128)(2,1)S(1)}, bf16[48,3072]{1,0:T(8,128)(2,1)S(1)}, u32[]{:S(2)}, u32[]{:S(2)}) collective-permute-start(bf16[48,3072]{1,0:T(8,128)(2,1)S(1)} %get-tuple-element.171), channel_id=1, source_target_pairs={{0,16},{8,24},{16,0},{24,8},{1,17},{9,25},{17,1},{25,9},{2,18},{10... | collective-permute-start | bytes 884744 | tf_op jit(solution)/shard_map/ppermute | solution.py:426
  (144 other events, 1508.7 us)

commit v2 on v1

--- a/solution.py
+++ b/solution.py
@@ -15,7 +15,8 @@
 BF16 = jnp.bfloat16
 LANES = 128
 CHUNK = 512
-VMEM_LIMIT = 40 * 1024 * 1024
+SPLIT = 3
+VMEM_LIMIT = 46 * 1024 * 1024
 ORDER = (0, 2, 1, 3)
 
 
@@ -62,11 +63,13 @@
         self.blocks = contexts == 4 and block % 16 == 0
 
 
-def run(plan, body, name, meta, inputs, weights, outs, flops, scratch=(), direct=()):
+def run(plan, body, name, meta, inputs, weights, outs, flops, scratch=(), direct=(), ties=(), kept=()):
+    if ties:
+        inputs = [after(inputs[0], *ties), *inputs[1:]]
     n_in, n_out = len(inputs), len(outs)
-    counts = [len(arrays) for arrays, _, _ in weights]
-    per_block = plan.shards * len(ORDER)
-    copies = sum(1 if n == 1 else per_block for n in counts)
+    counts = [len(entry[0]) for entry in weights]
+    per_block = plan.shards * len(ORDER) * SPLIT
+    copies = sum(1 if n == 1 else per_block for n in counts) + len(kept)
 
     def kernel(meta_ref, *refs):
         ins = refs[:n_in]
@@ -75,33 +78,46 @@
         for n in counts:
             sources.append(refs[at : at + n])
             at += n
+        lying = refs[at : at + len(kept)]
+        at += len(kept)
         results = refs[at : at + n_out]
         at += n_out
         held = refs[at : at + len(weights)]
         at += len(weights)
-        sems = refs[at] if weights else None
-        own = refs[at + 1 :] if weights else refs[at:]
+        brought = refs[at : at + len(kept)]
+        at += len(kept)
+        sems = refs[at] if copies else None
+        own = refs[at + 1 :] if copies else refs[at:]
         started, slot = [], 0
-        for (_, column, width), refs_of, into in zip(weights, sources, held):
+        bringing = []
+        for ref, into in zip(lying, brought):
+            bringing.append(pltpu.make_async_copy(ref, into, sems.at[slot]))
+            slot += 1
+        for copy in bringing:
+            copy.start()
+        for (_, column, width, *whole), refs_of, into in zip(weights, sources, held):
             group = []
             columns = pl.ds(column, width)
+            split = math.gcd(width // LANES, SPLIT)
             if len(refs_of) == 1:
                 group.append(pltpu.make_async_copy(refs_of[0].at[:, columns], into, sems.at[slot]))
                 slot += 1
             else:
-                for ref, offset in zip(refs_of, ORDER):
+                for place, offset in enumerate(ORDER):
                     for shift in range(plan.shards):
-                        z = lax.rem(meta_ref[0] + (plan.shards - shift), plan.shards)
+                        ref = refs_of[place].at[shift]
+                        z = shift if whole else lax.rem(meta_ref[0] + (plan.shards - shift), plan.shards)
                         index = z * plan.contexts + jnp.bitwise_xor(meta_ref[1], offset)
                         row = pl.multiple_of(index * plan.block, 16)
-                        group.append(
-                            pltpu.make_async_copy(
-                                ref.at[shift, :, columns],
-                                into.at[pl.ds(row, plan.block), :],
-                                sems.at[slot],
+                        for part in range(0, width, width // split):
+                            group.append(
+                                pltpu.make_async_copy(
+                                    ref.at[:, pl.ds(column + part, width // split)],
+                                    into.at[pl.ds(row, plan.block), pl.ds(part, width // split)],
+                                    sems.at[slot],
+                                )
                             )
-                        )
-                        slot += 1
+                            slot += 1
             for copy in group:
                 copy.start()
             started.append(group)
@@ -111,28 +127,34 @@
                 copy.wait()
             return held[i]
 
-        body(meta_ref, ins, weight, results, own)
+        for copy in bringing:
+            copy.wait()
+        body(meta_ref, (*ins, *brought), weight, results, own)
 
     vmem = pl.BlockSpec(memory_space=pltpu.VMEM)
     anywhere = pl.BlockSpec(memory_space=pl.ANY)
-    scratch_shapes = [pltpu.VMEM((plan.width, width), BF16) for _, _, width in weights]
-    if weights:
+    outside = pl.BlockSpec(memory_space=pltpu.HBM)
+    scratch_shapes = [pltpu.VMEM((plan.width, entry[2]), BF16) for entry in weights]
+    scratch_shapes += [pltpu.VMEM(array.shape, array.dtype) for array in kept]
+    if copies:
         scratch_shapes.append(pltpu.SemaphoreType.DMA((copies,)))
     moved = sum(x.size * x.dtype.itemsize for x in inputs)
     moved += sum(math.prod(o.shape) * o.dtype.itemsize for o in outs)
-    moved += sum(plan.width * width * 2 for _, _, width in weights)
-    return pl.pallas_call(
+    moved += sum(plan.width * entry[2] * 2 for entry in weights)
+    call = pl.pallas_call(
         kernel,
         name=name,
         out_shape=tuple(outs),
         in_specs=[pl.BlockSpec(memory_space=pltpu.SMEM)]
         + [vmem] * n_in
-        + [anywhere] * sum(counts),
-        out_specs=tuple(anywhere if i in direct else vmem for i in range(n_out)),
+        + [outside if n == 1 else anywhere for n in counts for _ in range(n)]
+        + [anywhere] * len(kept),
+        out_specs=tuple(outside if i in direct else vmem for i in range(n_out)),
         scratch_shapes=scratch_shapes + list(scratch),
         compiler_params=pltpu.CompilerParams(vmem_limit_bytes=VMEM_LIMIT),
-        cost_estimate=pl.CostEstimate(flops=flops, bytes_accessed=moved, transcendentals=0),
-    )(meta, *inputs, *[array for arrays, _, _ in weights for array in arrays])
+        cost_estimate=pl.CostEstimate(flops=0, bytes_accessed=0, transcendentals=0),
+    )
+    return call(meta, *inputs, *[array for entry in weights for array in entry[0]], *kept)
 
 
 def shape(*dims, dtype=BF16):
@@ -214,8 +236,10 @@
 
 def attend_body(plan, meta, ins, weight, outs, own):
     q_ref, kvs = ins[0], ins[1:]
-    part_ref, o_ref, total_ref = outs
+    part_ref, o_ref, total_ref, all_ref = outs
     n = plan.heads_width
+    for i, kv in enumerate(kvs):
+        all_ref[i * kv.shape[0] : (i + 1) * kv.shape[0], :] = kv[...]
     allowed = allowed_keys(plan, meta)
     totals = []
     for pair in range(n // LANES):
@@ -280,7 +304,7 @@
 
 
 def between_body(plan, layer, meta, ins, weight, outs, own):
-    dx_mid, x_above, da, da_far, vec, slope = ins
+    da, da_far, dx_mid, x_above, vec, slope = ins
     gy_ref, dy_ref, dh_ref, db_ref, sum_ref = outs
     grad = da[...].astype(F32) + da_far[...].astype(F32)
     back, gain_sum = norm_back(x_above[...], vec[2 * layer + 2 : 2 * layer + 3, :], grad)
@@ -292,7 +316,7 @@
 
 
 def attend_back_body(plan, layer, meta, ins, weight, outs, own):
-    gy, x_mid, db, db_far, vec, q_ref, total = ins[:7]
+    gy, db, db_far, x_mid, vec, q_ref, total = ins[:7]
     kvs = ins[7:]
     mid_ref, dz_ref, dq_ref, sum_ref = outs[:4]
     dkv = outs[4:]
@@ -346,40 +370,40 @@
     sum_ref[...] = rows_of([jnp.concatenate(sums, axis=1)], 8, 2 * n)
 
 
-def weight_grad_body(plan, widths, meta, ins, weight, outs, own):
+def weight_grad_body(plan, widths, relative, meta, ins, weight, outs, own):
     packet, sems = own
-    column = 0
+    column, copies = 0, []
     for i, width in enumerate(widths):
         left, right = ins[2 * i], ins[2 * i + 1]
+        turned = left[...].T
         for j in range(0, width, CHUNK):
             size = min(CHUNK, width - j)
-            value = tn(left[...], right[:, j : j + size])
-            packet[:, column : column + size] = value.astype(BF16)
+            window = pl.ds(column, size)
+            packet[:, column : column + size] = nn(turned, right[:, j : j + size]).astype(BF16)
             column += size
-    if not plan.blocks:
-        copies = [pltpu.make_async_copy(packet, outs[0], sems.at[0])]
-    else:
-        copies = []
-        for place, offset in enumerate(ORDER):
-            for shift in range(plan.shards):
-                z = lax.rem(meta[0] + shift, plan.shards)
-                index = z * plan.contexts + jnp.bitwise_xor(meta[1], offset)
-                row = pl.multiple_of(index * plan.block, 16)
-                copies.append(
-                    pltpu.make_async_copy(
-                        packet.at[pl.ds(row, plan.block), :],
-                        outs[place // 2].at[place % 2, shift],
-                        sems.at[place * plan.shards + shift],
+            if len(outs) == 1:
+                copy = pltpu.make_async_copy(packet.at[:, window], outs[0].at[:, window], sems.at[len(copies)])
+                copy.start()
+                copies.append(copy)
+                continue
+            for place, offset in enumerate(ORDER):
+                for k in range(plan.shards):
+                    z = lax.rem(meta[0] + k, plan.shards) if relative else k
+                    index = z * plan.contexts + jnp.bitwise_xor(meta[1], offset)
+                    row = pl.multiple_of(index * plan.block, 16)
+                    copy = pltpu.make_async_copy(
+                        packet.at[pl.ds(row, plan.block), window],
+                        outs[place // 2].at[place % 2, k, :, window],
+                        sems.at[len(copies)],
                     )
-                )
-    for copy in copies:
-        copy.start()
+                    copy.start()
+                    copies.append(copy)
     for copy in copies:
         copy.wait()
 
 
 def end_body(plan, meta, ins, weight, outs, own):
-    dx_mid, x, da, da_far, vec = ins[:5]
+    da, da_far, dx_mid, x, vec = ins[:5]
     feed0, attn0, proj0, feed1, attn1, proj1 = ins[5:]
     gy_ref, small_ref = outs
     grad = da[...].astype(F32) + da_far[...].astype(F32)
@@ -426,20 +450,51 @@
     return lax.ppermute(array, "shard", [(i, (i + shift) % n) for i in range(n)])
 
 
-def along_shard(plan, pieces):
-    got = [pieces[0]] + [to_shard(plan, pieces[k], k) for k in range(1, plan.shards)]
-    return jnp.stack(got)
-
-
-def across_chip(stack):
-    far = swap_chip(stack)
-    return (stack, far, swap_core(stack), swap_core(far))
-
-
-def gather_rows(plan, packet):
-    if plan.blocks:
-        return across_chip(along_shard(plan, [packet] * plan.shards))
-    return (lax.all_gather(packet, ("shard", "ctx"), axis=0, tiled=True),)
+def stage_of(plan, thing, *names):
+    if not plan.blocks:
+        return ()
+    found = [getattr(thing, name) for name in names]
+    return tuple(array for one in found for array in (one if isinstance(one, tuple) else (one,)))
+
+
+class Gather:
+    def __init__(self, plan, packets, *ties):
+        self.plan = plan
+        if plan.blocks:
+            packets = after_all(packets, *ties) if ties else tuple(packets)
+            got = [to_shard(plan, packets[k], k) for k in range(1, plan.shards)]
+            self.got = tuple(got)
+            self.blocks = (packets[0], *got)
+        else:
+            self.arrays = (lax.all_gather(packets[0], ("shard", "ctx"), axis=0, tiled=True),)
+
+    @classmethod
+    def at_once(cls, plan, packet, *ties):
+        self = cls.__new__(cls)
+        self.plan = plan
+        if plan.blocks:
+            copies = jnp.broadcast_to(after(packet, *ties), (plan.shards, *packet.shape))
+            self.stack = lax.all_to_all(copies, "shard", 0, 0, tiled=True)
+        else:
+            self.arrays = (lax.all_gather(packet, ("shard", "ctx"), axis=0, tiled=True),)
+        return self
+
+    def along(self, *ties):
+        if self.plan.blocks:
+            self.stack = jnp.stack(after_all(self.blocks, *ties) if ties else self.blocks)
+        return self
+
+    def across(self, *ties):
+        if self.plan.blocks:
+            self.far = swap_chip(after(self.stack, *ties) if ties else self.stack)
+        return self
+
+    def cores(self, *ties):
+        if self.plan.blocks:
+            halves = (self.stack, self.far)
+            sent = after_all(halves, *ties) if ties else halves
+            self.arrays = (*halves, *[swap_core(half) for half in sent])
+        return self
 
 
 def gather_keys(plan, kv):
@@ -449,6 +504,14 @@
     return (lax.all_gather(kv, "ctx", axis=0, tiled=True),)
 
 
+def after(array, *others):
+    return lax.optimization_barrier((array, *others))[0]
+
+
+def after_all(arrays, *others):
+    return lax.optimization_barrier((*arrays, *others))[: len(arrays)]
+
+
 def add(*terms):
     total = terms[0].astype(F32)
     for term in terms[1:]:
@@ -456,34 +519,74 @@
     return total
 
 
-def weight_grad(plan, meta, name, pairs):
+def weight_grads(plan, meta, name, pairs, blocks, relative=False):
     widths = tuple(right.shape[1] for _, right in pairs)
     width = sum(widths)
-    if plan.blocks:
-        part = shape(2, plan.shards, plan.block, width)
-        outs, copies = [part, part], plan.shards * 4
+    copies = sum(pl.cdiv(width, CHUNK) for width in widths)
+    if blocks:
+        outs = [shape(2, plan.shards, plan.block, width)] * 2
+        copies *= plan.shards * 4
     else:
-        outs, copies = [shape(plan.width, width)], 1
-    parts = run(
+        outs = [shape(plan.width, width)]
+    return run(
         plan,
-        functools.partial(weight_grad_body, plan, widths),
+        functools.partial(weight_grad_body, plan, widths, relative),
         name,
         meta,
-        [array for pair in pairs for array in pair],
+        [],
         [],
         outs,
         2 * plan.rows * plan.width * width,
+        kept=[array for pair in pairs for array in pair],
         scratch=[pltpu.VMEM((plan.width, width), BF16), pltpu.SemaphoreType.DMA((copies,))],
         direct=tuple(range(len(outs))),
     )
-    if not plan.blocks:
-        return lax.psum_scatter(parts[0], ("shard", "ctx"), scatter_dimension=0, tiled=True).astype(F32)
-    keep, send = parts
-    near = swap_core(send)
-    far = swap_chip(add(keep[1], near[1]).astype(BF16))
-    sums = [add(keep[0, k], near[0, k], far[k]) for k in range(plan.shards)]
-    got = [to_shard(plan, sums[k].astype(BF16), k) for k in range(1, plan.shards)]
-    return add(sums[0], *got)
+
+
+class Reduction:
+    def __init__(self, plan, meta, name, pairs, blocks=True, relative=False):
+        self.blocks = blocks and plan.blocks
+        self.plan, self.relative = plan, relative
+        parts = weight_grads(plan, meta, name, pairs, self.blocks, relative)
+        if self.blocks:
+            self.keep, self.send = parts
+        else:
+            self.send = parts[0]
+            total = lax.psum_scatter(parts[0], ("shard", "ctx"), scatter_dimension=0, tiled=True)
+            self.total = total
+
+    def core(self, *ties):
+        if self.blocks:
+            self.near = swap_core(after(self.send, *ties))
+        return self
+
+    def pairs(self, *ties):
+        if self.blocks:
+            self.near = after(self.near, *ties)
+            self.pair = add(self.keep[1], self.near[1]).astype(BF16)
+            self.far = swap_chip(self.pair)
+        return self
+
+    def along(self, *ties):
+        if self.blocks:
+            far = after(self.far, *ties) if ties else self.far
+            if self.relative:
+                n = self.plan.shards
+                self.sums = tuple(
+                    add(self.keep[0, k], self.near[0, k], far[k]).astype(BF16) for k in range(n)
+                )
+                self.got = (self.sums[0], *[to_shard(self.plan, self.sums[k], k) for k in range(1, n)])
+            else:
+                self.sums = add(self.keep[0], self.near[0], far).astype(BF16)
+                self.got = lax.all_to_all(self.sums, "shard", 0, 0, tiled=True)
+        return self
+
+    def end(self, *ties):
+        if not self.blocks:
+            return (after(self.total, *ties) if self.plan.blocks else self.total).astype(F32)
+        if self.relative:
+            return add(*after_all(self.got, *ties))
+        return jnp.sum(after(self.got, *ties).astype(F32), axis=0)
 
 
 def per_device(
@@ -511,44 +614,47 @@
     z, c = lax.axis_index("shard"), lax.axis_index("ctx")
     meta = jnp.concatenate([jnp.stack([z, c]).astype(jnp.int32), jnp.cumsum(cont_lengths[0])])
 
+    n3 = 3 * heads_width
+
+    def everywhere(packet):
+        return (lax.all_gather(packet, ("shard", "ctx"), axis=0, tiled=True),)
+
+    upper = jnp.concatenate([w_qkv[1].reshape(block, -1), w_out[1], w_up[1], w_down[1]], axis=1)
+    first = jnp.concatenate([w_qkv[0].reshape(block, -1), w_out[0]], axis=1)
+    steps = after(timesteps, first)
+    first = Gather(plan, [first] * shards)
+
     vectors = jnp.concatenate(
         [norms[0], norms[1], out_biases[0], out_biases[1]], axis=1
     )
     seqs = conts + 1
-    steps_all = lax.all_gather(timesteps, "shard", axis=0, tiled=True)
-    steps_near = jnp.roll(steps_all, -z, axis=0).reshape(-1)
+    steps_back = jnp.concatenate([steps] + [to_shard(plan, steps, k) for k in range(1, shards)])
+    steps_near = jnp.concatenate([steps_back[:1], steps_back[:0:-1]]).reshape(-1)
     one_hot = (steps_near[:, None] == jnp.arange(table.shape[0], dtype=jnp.int32)[None, :]).astype(BF16)
     looked = lax.dot_general(
         table, one_hot, (((0,), (1,)), ((), ())), preferred_element_type=F32
     ).astype(BF16)
     blank = jnp.zeros((block, LANES - vectors.shape[1] - seqs), BF16)
     if plan.blocks:
-        small = along_shard(
-            plan,
-            [
-                jnp.concatenate([vectors, looked[:, k * seqs : (k + 1) * seqs], blank], axis=1)
-                for k in range(shards)
-            ],
-        )
-        first = along_shard(plan, [w_qkv[0].reshape(block, -1)] * shards)
-        first = across_chip(jnp.concatenate([first, small], axis=2))
-        small_of = (first, 3 * heads_width, LANES)
+        small = [
+            jnp.concatenate([vectors, looked[:, k * seqs : (k + 1) * seqs], blank], axis=1)
+            for k in range(shards)
+        ]
+        small = Gather(plan, small)
+        first.along(*small.got)
+        ties = (first.stack,)
+        small = small.along().across().cores().arrays
     else:
         looked = jnp.roll(looked.reshape(block, shards, seqs), z, axis=1).reshape(block, -1)
         every = lax.all_gather(jnp.concatenate([vectors, looked], axis=1), ("shard", "ctx"), axis=0, tiled=True)
         mine = lax.dynamic_slice_in_dim(every, 8 + z * seqs, seqs, axis=1)
         blank = jnp.zeros((width, LANES - 8 - seqs), BF16)
-        small_of = ((jnp.concatenate([every[:, :8], mine, blank], axis=1),), 0, LANES)
-        first = gather_rows(plan, w_qkv[0].reshape(block, -1))
-    n3 = 3 * heads_width
-    second = gather_rows(plan, jnp.concatenate([w_out[0], w_up[0]], axis=1))
-    third = gather_rows(plan, w_down[0])
-    fourth = gather_rows(plan, jnp.concatenate([w_qkv[1].reshape(block, -1), w_out[1]], axis=1))
-    fifth = gather_rows(plan, jnp.concatenate([w_up[1], w_down[1]], axis=1))
-    of_qkv = [(first, 0, n3), (fourth, 0, n3)]
-    of_out = [(second, 0, heads_width), (fourth, n3, heads_width)]
-    of_up = [(second, heads_width, hidden), (fifth, 0, hidden)]
-    of_down = [(third, 0, hidden), (fifth, hidden, hidden)]
+        small = [jnp.concatenate([every[:, :8], mine, blank], axis=1)]
+        ties = ()
+    second = Gather(plan, [w_up[0]] * shards, *ties)
+    third = Gather.at_once(plan, w_down[0], *ties)
+    first.across().cores(*stage_of(plan, second, "got"))
+    upper = everywhere(after(upper, *ties))
 
     mm = 2 * rows * width
     full = shape(rows, width, dtype=F32)
@@ -562,6 +668,8 @@
     saved = []
     x_mid = part = part_far = None
     for layer in range(layers):
+        last = layer == layers - 1
+        ties = ()
         if layer == 0:
             x, vec, a, q, kv = run(
                 plan,
@@ -569,34 +677,44 @@
                 "embed",
                 meta,
                 [tokens, query_bias, value_bias],
-                [of_qkv[0], small_of],
+                [(first.arrays, 0, n3), (small, 0, LANES)],
                 [full, sums, *qkv_outs],
                 mm * n3,
+                ties=stage_of(plan, second, "got"),
             )
+            second.along(kv).across()
+            ties = stage_of(plan, second, "stack") + stage_of(plan, third, "stack")
+            of_attn = [(first.arrays, 0, n3), (first.arrays, n3, heads_width)]
         else:
+            of_attn = [(upper, 0, n3), (upper, n3, heads_width)]
+            of_feed = [(upper, n3 + heads_width + i * hidden, hidden) for i in range(2)]
             x, a, q, kv = run(
                 plan,
                 functools.partial(next_body, plan, layer),
                 "project",
                 meta,
                 [x_mid, part, part_far, vec, query_bias, value_bias],
-                [of_qkv[layer]],
+                of_attn[:1],
                 [full, *qkv_outs],
                 mm * n3,
             )
         kvs = gather_keys(plan, kv)
-        part, o, total = run(
+        part, o, total, kv_all = run(
             plan,
             functools.partial(attend_body, plan),
             "attend",
             meta,
             [q, *kvs],
-            [of_out[layer]],
-            [low, heads, shape(8, 2 * rows, dtype=F32)],
+            of_attn[1:],
+            [low, heads, shape(8, 2 * rows, dtype=F32), shape(plan.group, 2 * heads_width)],
             mm * heads_width + attn_flops,
+            ties=ties,
         )
         part_far = swap_tp(part)
-        last = layer == layers - 1
+        if layer == 0:
+            second.cores(part)
+            third.across(part).cores(part_far)
+            of_feed = [(second.arrays, 0, hidden), (third.arrays, 0, hidden, True)]
         outs = [full, low, wide, shape(rows, hidden, dtype=F32), low]
         if last:
             outs += [wide, low, sums]
@@ -606,35 +724,44 @@
             "feed",
             meta,
             [x, part, part_far, vec, up_bias] + ([cotangent] if last else []),
-            [of_up[layer], of_down[layer]],
+            of_feed,
             outs,
             mm * hidden * (4 if last else 2),
         )
         x_mid, b, gelu, slope, part = got[:5]
         part_far = swap_tp(part)
-        saved.append((x, a, q, kvs, o, total, x_mid, b, gelu, slope))
-
-    bias_last = vec[2 * layers + 3][None, :]
-    activations = (x_mid + add(part, part_far) + bias_last).astype(BF16)
+        saved.append((x, a, q, kv_all, o, total, x_mid, b, gelu, slope, of_attn, of_feed))
 
     gy = dy = cotangent
     dh, db, feed_sum = got[5:]
-    grads, small_sums = [None] * layers, [None] * layers
+    final = (x_mid, part, part_far)
+    bias_last = vec[2 * layers + 3][None, :]
+    small_sums = [None] * layers
+    above = None
     for layer in reversed(range(layers)):
-        x, a, q, kvs, o, total, x_mid, b, gelu, slope = saved[layer]
-        if layer < layers - 1:
+        x, a, q, kv_all, o, total, x_mid, b, gelu, slope, of_attn, of_feed = saved[layer]
+        if above is not None:
             gy, dy, dh, db, feed_sum = run(
                 plan,
                 functools.partial(between_body, plan, layer),
                 "feed_back",
                 meta,
-                [dx_mid, saved[layer + 1][0], da, da_far, vec, slope],
-                [of_up[layer], of_down[layer]],
+                [da, da_far],
+                of_feed,
                 [full, low, wide, low, sums],
                 2 * mm * hidden,
+                kept=[dx_mid, saved[layer + 1][0], vec, slope],
+                ties=stage_of(plan, above, "send"),
             )
         db_far = swap_tp(db)
-        feed_grad = weight_grad(plan, meta, "feed_grad", [(b, dh), (dy, gelu)])
+        if above is None:
+            ties = ()
+        else:
+            feeds = [
+                Reduction(plan, meta, "up_grad", [(b, dh)]).core(db_far),
+                Reduction(plan, meta, "down_grad", [(dy, gelu)], relative=True).core(db_far),
+            ]
+            ties = stage_of(plan, feeds[0], "send") + stage_of(plan, feeds[1], "send")
         if plan.blocks:
             dkv_outs = [shape(2 * rows, 2 * heads_width)] * 2
         else:
@@ -644,31 +771,47 @@
             functools.partial(attend_back_body, plan, layer),
             "attend_back",
             meta,
-            [gy, x_mid, db, db_far, vec, q, total, *kvs],
-            [of_out[layer]],
+            [gy, db, db_far],
+            of_attn[1:],
             [full, low, heads, sums, *dkv_outs],
             mm * heads_width + 10 * rows * plan.group * heads_width,
+            ties=ties,
+            kept=[x_mid, vec, q, total, kv_all],
         )
+        ties = ()
         if plan.blocks:
             keep, send = dkv
             near = swap_core(send)
-            far = swap_chip(add(keep[rows:], near[rows:]).astype(BF16))
-            terms = [keep, near, far]
+            summed = add(keep[rows:], near[rows:]).astype(BF16)
+            terms = [keep, near, swap_chip(summed)]
+            if above is None:
+                x_mid, part, part_far = after_all(final, summed)
+                activations = (x_mid + add(part, part_far) + bias_last).astype(BF16)
+                ties = (activations,)
         else:
             terms = [lax.psum_scatter(dkv[0], "ctx", scatter_dimension=0, tiled=True)]
+            if above is None:
+                activations = (x_mid + add(part, part_far) + bias_last).astype(BF16)
         dqkv, da, proj_sum = run(
             plan,
             functools.partial(project_back_body, plan),
             "project_back",
             meta,
             [dq, *terms],
-            [of_qkv[layer]],
+            of_attn[:1],
             [shape(rows, n3), low, shape(8, 2 * heads_width, dtype=F32)],
             mm * n3,
+            ties=ties,
         )
         da_far = swap_tp(da)
-        attn_grad = weight_grad(plan, meta, "attn_grad", [(a, dqkv), (dz, o)])
-        grads[layer] = (feed_grad, attn_grad)
+        if above is None:
+            pairs = [(a, dqkv), (dz, o), (b, dh), (dy, gelu)]
+            above = Reduction(plan, meta, "layer_grad", pairs, blocks=False)
+        else:
+            attn = Reduction(plan, meta, "attn_grad", [(a, dqkv), (dz, o)]).core(da_far)
+            for feed in feeds:
+                feed.pairs(da)
+            end_ties = stage_of(plan, attn, "send") + stage_of(plan, feeds[0], "far") + stage_of(plan, feeds[1], "pair")
         small_sums[layer] = [feed_sum, attn_sum, proj_sum]
 
     grad_tokens, packet = run(
@@ -676,27 +819,34 @@
         functools.partial(end_body, plan),
         "end",
         meta,
-        [dx_mid, saved[0][0], da, da_far, vec, *small_sums[0], *small_sums[1]],
+        [da, da_far],
         [],
         [full, shape(32, width)],
         mm * 32,
+        ties=end_ties,
+        kept=[dx_mid, saved[0][0], vec, *small_sums[0], *small_sums[1]],
     )
+    attn.pairs(packet)
+    feeds[0].along(packet, *stage_of(plan, attn, "pair"))
+    feeds[1].along(packet, *stage_of(plan, feeds[0], "sums"))
     start = (z * contexts + c) * block
     if plan.blocks:
         packet = add(packet, swap_core(packet)).astype(BF16)
+        packet = after(packet, attn.pair)
         packet = add(packet, swap_chip(packet)).astype(BF16)
-        got = along_shard(plan, [packet] * shards)
+        got = jnp.stack([packet] + [to_shard(plan, packet, k) for k in range(1, shards)])
         other = add(*[got[k] for k in range(0, shards, 2)]) + add(*[got[k] for k in range(1, shards, 2)])
-        steps_back = jnp.roll(steps_all[::-1], z + 1, axis=0)
     else:
         packet = lax.psum(packet, "ctx")
         got = lax.all_gather(packet, "shard", axis=0)
         other = jnp.sum(got.astype(F32), axis=0)
-        steps_back = steps_all
+        steps_back = jnp.roll(steps_back[::-1], z + 1, axis=0)
     mine = lax.dynamic_slice_in_dim(got[:, :seqs], start, block, axis=2).reshape(-1, block)
     one_hot = (jnp.arange(table.shape[0], dtype=jnp.int32)[:, None] == steps_back.reshape(-1)[None, :]).astype(BF16)
     grad_table = jnp.dot(one_hot, mine, preferred_element_type=F32)
 
+    attn.along(*stage_of(plan, feeds[1], "sums"))
+    upper_grad = above.end(packet)
     halves = hidden // width
     per_layer = 5 + halves
     by_layer = other[16 : 16 + layers * per_layer].reshape(layers, per_layer, width)
@@ -706,15 +856,17 @@
     grad_up_bias = by_layer[:, 4 : 4 + halves].reshape(layers, hidden)
     grad_query_bias = by_layer[:, 4 + halves, :heads_width]
     grad_value_bias = by_layer[:, 4 + halves, heads_width:]
-    feeds = [grads[layer][0] for layer in range(layers)]
-    attns = [grads[layer][1] for layer in range(layers)]
+    at = n3 + heads_width
+    ups = [feeds[0].end(), upper_grad[:, at : at + hidden]]
+    downs = [feeds[1].end(), upper_grad[:, at + hidden :]]
+    attns = [attn.end(), upper_grad[:, :at]]
     return (
         activations,
         grad_tokens,
         jnp.stack([g[:, :n3].reshape(block, 3, heads_width) for g in attns]),
-        jnp.stack([g[:, n3:] for g in attns]),
-        jnp.stack([g[:, :hidden] for g in feeds]),
-        jnp.stack([g[:, hidden:] for g in feeds]),
+        jnp.stack([g[:, n3:at] for g in attns]),
+        jnp.stack(ups),
+        jnp.stack(downs),
         grad_norms,
         grad_table,
         grad_query_bias,

time: 451 us -> 360 us (0.80)
  the two profiles are of different devices: /device:TPU:28 before, /device:TPU:0 now
where the time goes in v2:
time: 360 us; the launch traced here: 356 us
  waiting for transfers between devices  152 us (42%)
  starting transfers between devices  71.7 us (20%)
  Pallas kernels  61.1 us (17%)
  local copies, waits for them, and re-layouts  33.8 us (9%)
  other arithmetic  20.3 us (6%)
  between operations  15.6 us (4%)
    ppermute x12, waiting for transfers between devices, swap_chip(): return lax.ppermute(array, 'ctx', [(i, i ^ 2) for i in range(4)])  82.3 us
    pallas_call x16, Pallas kernels, run(): call(meta, *inputs, *[array for entry in weights for array in entry[0]],...  61.1 us
    ppermute x18, starting transfers between devices, to_shard(): lax.ppermute(array, 'shard', [(i, (i + shift) % n) for i in range(n)])  31.7 us
    unnamed x193, local copies, waits for them, and re-layouts  28.2 us
    ppermute x8, waiting for transfers between devices, swap_tp(): return lax.ppermute(array, 'tp', [(0, 1), (1, 0)])  26.6 us
    ppermute x18, waiting for transfers between devices, to_shard(): lax.ppermute(array, 'shard', [(i, (i + shift) % n) for i in range(n)])  14.7 us
    all_to_all x2, waiting for transfers between devices, along(): self.got = lax.all_to_all(self.sums, 'shard', 0, 0, tiled=True)  13.4 us
    ppermute x8, starting transfers between devices, swap_tp(): return lax.ppermute(array, 'tp', [(0, 1), (1, 0)])  12.2 us
  transfers between devices with their start and end apart: 61, of which 32 were waited for; matrix products, arithmetic and copies ran while one was open for 6% of the time, Pallas kernels for 11%

profile of v2, /device:TPU:0, one launch (start us, length us, event | category | flops | bytes accessed | tf_op | source)
XLA Modules:
  0.0 355.5 jit_solution(5098420245329569428)
XLA Ops:
  28.4 4.8 %collective-permute-start.6 = (bf16[48,128]{1,0:T(8,128)(2,1)S(1)}, bf16[48,128]{1,0:T(8,128)(2,1)S(1)}, u32[]{:S(2)}, u32[]{:S(2)}) collective-permute-start(bf16[48,128]{1,0:T(8,128)(2,1)S(1)} %concatenate.39), channel_id=1, source_target_pairs={{0,8},{8,16},{16,24},{24,0},{1,9},{9,17},{17,25},{25,1},{2,10},{10... | collective-permute-start | bytes 36872 | tf_op jit(solution)/shard_map/ppermute | solution.py:450
  41.6 8.5 %collective-permute-done.10 = bf16[48,1536]{1,0:T(8,128)(2,1)S(1)} collective-permute-done((bf16[48,1536]{1,0:T(8,128)(2,1)S(1)}, bf16[48,1536]{1,0:T(8,128)(2,1)S(1)}, u32[]{:S(2)}, u32[]{:S(2)}) %collective-permute-start.10) | collective-permute-done | bytes 147488 | tf_op jit(solution)/shard_map/ppermute | solution.py:450
  55.2 10.1 %all-to-all-start = ((bf16[4,48,1536]{2,1,0:T(8,128)(2,1)}), bf16[4,48,1536]{2,1,0:T(8,128)(2,1)S(1)}, u32[]{:S(2)}, u32[]{:S(2)}) async-start(bf16[4,48,1536]{2,1,0:T(8,128)(2,1)} %broadcast_in_dim.9), calls=%async_computation | async-start | bytes 1179648 | tf_op jit(solution)/shard_map/all_to_all | solution.py:477
  76.0 11.8 %collective-permute-done.18.refs_2_ = bf16[128,768]{1,0:T(8,128)(2,1)} collective-permute-done((bf16[128,768]{1,0:T(8,128)(2,1)}, bf16[128,768]{1,0:T(8,128)(2,1)}, u32[]{:S(2)}, u32[]{:S(2)}) %collective-permute-start.18) | collective-permute-done | bytes 196640 | tf_op jit(solution)/shard_map/ppermute | solution.py:441
  88.0 7.7 %all-to-all-done.refs_9_.refs_6_ = bf16[4,48,1536]{2,1,0:T(8,128)(2,1)S(1)} async-done(((bf16[4,48,1536]{2,1,0:T(8,128)(2,1)}), bf16[4,48,1536]{2,1,0:T(8,128)(2,1)S(1)}, u32[]{:S(2)}, u32[]{:S(2)}) %all-to-all-start) | async-done | bytes 589856 | tf_op jit(solution)/shard_map/all_to_all | solution.py:477
  108.4 11.6 %collective-permute-done.25.refs_10_.refs_7_ = bf16[4,48,1536]{2,1,0:T(8,128)(2,1)S(1)} collective-permute-done((bf16[4,48,1536]{2,1,0:T(8,128)(2,1)S(1)}, bf16[4,48,1536]{2,1,0:T(8,128)(2,1)S(1)}, u32[]{:S(2)}, u32[]{:S(2)}) %collective-permute-start.25) | collective-permute-done | bytes 589856 | tf_op jit(solution)/shard_map/ppermute | solution.py:441
  122.9 4.6 %feed.2 = (f32[128,768]{1,0:T(8,128)S(1)}, bf16[128,768]{1,0:T(8,128)(2,1)S(1)}, bf16[128,1536]{1,0:T(8,128)(2,1)S(1)}, f32[128,1536]{1,0:T(8,128)S(1)}, bf16[128,768]{1,0:T(8,128)(2,1)S(1)}) custom-call(s32[10]{0:T(128)S(1)} %pad_add_fusion.3.meta_ref, f32[128,768]{1,0:T(8,128)S(1)} %copy-done.17, bf16[128,768]{1,0:T(8,128)(2,1)S(1)} %get-tuple-element.139.refs_1_, ...), custom_call_target="tpu_custom_call" | custom-call | tf_op jit(solution)/shard_map/feed/pallas_call | solution.py:157
  132.8 4.8 %collective-permute-done.28.refs_2_ = bf16[128,768]{1,0:T(8,128)(2,1)S(1)} collective-permute-done((bf16[128,768]{1,0:T(8,128)(2,1)S(1)}, bf16[128,768]{1,0:T(8,128)(2,1)S(1)}, u32[]{:S(2)}, u32[]{:S(2)}) %collective-permute-start.28) | collective-permute-done | bytes 196640 | tf_op jit(solution)/shard_map/ppermute | solution.py:445
  145.6 5.8 %collective-permute-done.29.refs_2_ = bf16[128,768]{1,0:T(8,128)(2,1)S(1)} collective-permute-done((bf16[128,768]{1,0:T(8,128)(2,1)S(1)}, bf16[128,768]{1,0:T(8,128)(2,1)S(1)}, u32[]{:S(2)}, u32[]{:S(2)}) %collective-permute-start.29) | collective-permute-done | bytes 196640 | tf_op jit(solution)/shard_map/ppermute | solution.py:441
  156.8 5.5 %collective-permute-done.32.refs_2_ = bf16[128,768]{1,0:T(8,128)(2,1)S(1)} collective-permute-done((bf16[128,768]{1,0:T(8,128)(2,1)S(1)}, bf16[128,768]{1,0:T(8,128)(2,1)S(1)}, u32[]{:S(2)}, u32[]{:S(2)}) %collective-permute-start.32) | collective-permute-done | bytes 196640 | tf_op jit(solution)/shard_map/ppermute | solution.py:445
  162.3 5.2 %feed.3 = (f32[128,768]{1,0:T(8,128)S(1)}, bf16[128,768]{1,0:T(8,128)(2,1)S(1)}, bf16[128,1536]{1,0:T(8,128)(2,1)S(1)}, f32[128,1536]{1,0:T(8,128)}, bf16[128,76...) custom-call(s32[10]{0:T(128)S(1)} %pad_add_fusion.3.meta_ref, ...), custom_call_target="tpu_custom_call" | custom-call | tf_op jit(solution)/shard_map/feed/pallas_call | solution.py:157
  169.1 4.6 %collective-permute-done.34.refs_2_ = bf16[128,768]{1,0:T(8,128)(2,1)S(1)} collective-permute-done((bf16[128,768]{1,0:T(8,128)(2,1)S(1)}, bf16[128,768]{1,0:T(8,128)(2,1)S(1)}, u32[]{:S(2)}, u32[]{:S(2)}) %collective-permute-start.34) | collective-permute-done | bytes 196640 | tf_op jit(solution)/shard_map/ppermute | solution.py:445
  173.7 4.5 %attend_back.2 = (f32[128,768]{1,0:T(8,128)S(1)}, bf16[128,768]{1,0:T(8,128)(2,1)S(1)}, bf16[128,384]{1,0:T(8,128)(2,1)S(1)}, f32[8,768]{1,0:T(8,128)S(1)}, bf16...) custom-call(s32[10]{0:T(128)S(1)} %pad_add_fusion.3.meta_ref, bf16[128,768]{1,0:T(8,128)(2,1)S(1)} %copy-done.12, ...), custom_call_target="tpu_custom_call" | custom-call | tf_op jit(solution)/shard_map/attend_back/pallas_call | solution.py:157
  180.6 5.1 %collective-permute-done.33 = bf16[128,768]{1,0:T(8,128)(2,1)S(1)} collective-permute-done((bf16[128,768]{1,0:T(8,128)(2,1)S(1)}, bf16[128,768]{1,0:T(8,128)(2,1)S(1)}, u32[]{:S(2)}, u32[]{:S(2)}) %collective-permute-start.33) | collective-permute-done | bytes 196640 | tf_op jit(solution)/shard_map/ppermute | solution.py:445
  191.1 5.6 %layer_grad.1 = bf16[768,4608]{1,0:T(8,128)(2,1)} custom-call(s32[10]{0:T(128)S(1)} %pad_add_fusion.3.meta_ref, bf16[128,768]{1,0:T(8,128)(2,1)S(1)} %get-tuple-element.166.refs_0_, bf16[128,1152]{1,0:T(8,128)(2,1)S(1)} %get-tuple-element.167.refs_1_, bf16[128,768]{1,0:T(8,128)(2,1)S(1)} %get-tuple-element.168.refs_2_, ...), custom_call_target="tpu_custom_call" | custom-call | tf_op jit(solution)/shard_map/layer_grad/pallas_call | solution.py:157
  198.4 4.9 %collective-permute-done.37.refs_1_ = bf16[128,768]{1,0:T(8,128)(2,1)S(1)} collective-permute-done((bf16[128,768]{1,0:T(8,128)(2,1)}, bf16[128,768]{1,0:T(8,128)(2,1)S(1)}, u32[]{:S(2)}, u32[]{:S(2)}) %collective-permute-start.37) | collective-permute-done | bytes 196640 | tf_op jit(solution)/shard_map/ppermute | solution.py:445
  213.7 4.9 %feed_back.1 = (f32[128,768]{1,0:T(8,128)S(1)}, bf16[128,768]{1,0:T(8,128)(2,1)S(1)}, bf16[128,1536]{1,0:T(8,128)(2,1)S(1)}, bf16[128,768]{1,0:T(8,128)(2,1)S(1)}, f32[8,768]{1,0:T(8,128)S(1)}) custom-call(s32[10]{0:T(128)S(1)} %pad_add_fusion.3.meta_ref, bf16[128,768]{1,0:T(8,128)(2,1)S(1)} %copy-done.46, ...), custom_call_target="tpu_custom_call" | custom-call | tf_op jit(solution)/shard_map/feed_back/pallas_call | solution.py:157
  228.0 4.6 %attend_back.3 = (f32[128,768]{1,0:T(8,128)S(1)}, bf16[128,768]{1,0:T(8,128)(2,1)S(1)}, bf16[128,384]{1,0:T(8,128)(2,1)S(1)}, f32[8,768]{1,0:T(8,128)S(1)}, bf16...) custom-call(s32[10]{0:T(128)S(1)} %pad_add_fusion.3.meta_ref, f32[128,768]{1,0:T(8,128)S(1)} %get-tuple-element.183.refs_0_, ...), custom_call_target="tpu_custom_call" | custom-call | tf_op jit(solution)/shard_map/attend_back/pallas_call | solution.py:157
  235.3 11.1 %collective-permute-done.40.refs_3_ = bf16[128,768]{1,0:T(8,128)(2,1)S(1)} collective-permute-done((bf16[128,768]{1,0:T(8,128)(2,1)S(1)}, bf16[128,768]{1,0:T(8,128)(2,1)S(1)}, u32[]{:S(2)}, u32[]{:S(2)}) %collective-permute-start.40) | collective-permute-done | bytes 196640 | tf_op jit(solution)/shard_map/ppermute | solution.py:441
  257.2 14.0 %collective-permute-done.42 = bf16[4,48,1536]{2,1,0:T(8,128)(2,1)S(1)} collective-permute-done((bf16[4,48,1536]{2,1,0:T(8,128)(2,1)S(1)}, bf16[4,48,1536]{2,1,0:T(8,128)(2,1)S(1)}, u32[]{:S(2)}, u32[]{:S(2)}) %collective-permute-start.42) | collective-permute-done | bytes 589856 | tf_op jit(solution)/shard_map/ppermute | solution.py:441
  283.0 4.6 %all-to-all-start.2 = ((bf16[4,48,1536]{2,1,0:T(8,128)(2,1)}), bf16[4,48,1536]{2,1,0:T(8,128)(2,1)S(1)}, u32[]{:S(2)}, u32[]{:S(2)}) async-start(bf16[4,48,1536]{2,1,0:T(8,128)(2,1)} %fusion), calls=%async_computation.3 | async-start | bytes 1179648 | tf_op jit(solution)/shard_map/all_to_all | solution.py:581
  287.6 5.6 %collective-permute-done.47 = bf16[4,48,1536]{2,1,0:T(8,128)(2,1)} collective-permute-done((bf16[4,48,1536]{2,1,0:T(8,128)(2,1)}, bf16[4,48,1536]{2,1,0:T(8,128)(2,1)}, u32[]{:S(2)}, u32[]{:S(2)}) %collective-permute-start.47) | collective-permute-done | bytes 589856 | tf_op jit(solution)/shard_map/ppermute | solution.py:441
  293.3 13.5 %collective-permute-done.49 = bf16[32,768]{1,0:T(8,128)(2,1)} collective-permute-done((bf16[32,768]{1,0:T(8,128)(2,1)}, bf16[32,768]{1,0:T(8,128)(2,1)}, u32[]{:S(2)}, u32[]{:S(2)}) %collective-permute-start.49) | collective-permute-done | bytes 49184 | tf_op jit(solution)/shard_map/ppermute | solution.py:441
  330.0 13.3 %all-to-all-done.1 = bf16[4,48,1536]{2,1,0:T(8,128)(2,1)S(1)} async-done(((bf16[4,48,1536]{2,1,0:T(8,128)(2,1)}), bf16[4,48,1536]{2,1,0:T(8,128)(2,1)S(1)}, u32[]{:S(2)}, u32[]{:S(2)}) %all-to-all-start.1) | async-done | bytes 589856 | tf_op jit(solution)/shard_map/all_to_all | solution.py:581
  (376 shorter events, 163.1 us)
Async XLA Ops:
  7.2 131.0 %all-gather.2.cloned.1.call-start = ((), (), s32[]{:S(2)}) async-start(), calls=%async_computation.4 | async-start | bytes 7520256 | tf_op jit(solution)/shard_map/all_gather | solution.py:620
  16.3 18.3 %collective-permute-start = (bf16[48,1536]{1,0:T(8,128)(2,1)S(1)}, bf16[48,1536]{1,0:T(8,128)(2,1)S(1)}, u32[]{:S(2)}, u32[]{:S(2)}) collective-permute-start(bf16[48,1536]{1,0:T(8,128)(2,1)S(1)} %pad_maximum_fusion.6), channel_id=1, source_target_pairs={{0,8},{8,16},{16,24},{24,0},{1,9},{9,17},{17,25},{25,1},{2,10},{10... | collective-permute-start | bytes 442376 | tf_op jit(solution)/shard_map/ppermute | solution.py:450
  17.0 17.6 %collective-permute-start.1 = (bf16[48,1536]{1,0:T(8,128)(2,1)S(1)}, bf16[48,1536]{1,0:T(8,128)(2,1)S(1)}, u32[]{:S(2)}, u32[]{:S(2)}) collective-permute-start(bf16[48,1536]{1,0:T(8,128)(2,1)S(1)} %pad_maximum_fusion.6), channel_id=1, source_target_pairs={{0,16},{8,24},{16,0},{24,8},{1,17},{9,25},{17,1},{25,9},{2,18},{10... | collective-permute-start | bytes 442376 | tf_op jit(solution)/shard_map/ppermute | solution.py:450
  17.8 16.8 %collective-permute-start.2 = (bf16[48,1536]{1,0:T(8,128)(2,1)S(1)}, bf16[48,1536]{1,0:T(8,128)(2,1)S(1)}, u32[]{:S(2)}, u32[]{:S(2)}) collective-permute-start(bf16[48,1536]{1,0:T(8,128)(2,1)S(1)} %pad_maximum_fusion.6), channel_id=1, source_target_pairs={{0,24},{8,0},{16,8},{24,16},{1,25},{9,1},{17,9},{25,17},{2,26},{10... | collective-permute-start | bytes 442376 | tf_op jit(solution)/shard_map/ppermute | solution.py:450
  35.3 18.5 %collective-permute-start.12 = (bf16[4,48,1536]{2,1,0:T(8,128)(2,1)S(1)}, bf16[4,48,1536]{2,1,0:T(8,128)(2,1)S(1)}, u32[]{:S(2)}, u32[]{:S(2)}) collective-permute-start(bf16[4,48,1536]{2,1,0:T(8,128)(2,1)S(1)} %pad_maximum_fusion.refs_3_.refs_5_.refs_4_), channel_id=1, source_target_pairs={{0,4},{2,6},{4,0},{6,2},{1,5},{3,7},{5,1},{7,3},{8,12},{10,14},{12... | collective-permute-start | bytes 1769480 | tf_op jit(solution)/shard_map/ppermute | solution.py:441
  53.8 17.8 %collective-permute-start.13 = (bf16[4,48,1536]{2,1,0:T(8,128)(2,1)S(1)}, bf16[4,48,1536]{2,1,0:T(8,128)(2,1)S(1)}, u32[]{:S(2)}, u32[]{:S(2)}) collective-permute-start(bf16[4,48,1536]{2,1,0:T(8,128)(2,1)S(1)} %pad_maximum_fusion.refs_3_.refs_5_.refs_4_), channel_id=1, source_target_pairs={{0,2},{2,0},{4,6},{6,4},{1,3},{3,1},{5,7},{7,5},{8,10},{10,8},{12,... | collective-permute-start | bytes 1769480 | tf_op jit(solution)/shard_map/ppermute | solution.py:437
  53.8 17.8 %collective-permute-start.14 = (bf16[4,48,1536]{2,1,0:T(8,128)(2,1)S(1)}, bf16[4,48,1536]{2,1,0:T(8,128)(2,1)S(1)}, u32[]{:S(2)}, u32[]{:S(2)}) collective-permute-start(bf16[4,48,1536]{2,1,0:T(8,128)(2,1)S(1)} %collective-permute-done.12.refs_4_.refs_6_.refs_5_), channel_id=1, source_target_pairs={{0,2},{2,0},{4,6},{6,4},{1,3},{3,1},{5,7},{7,5},{8,10},{10,8},{12,... | collective-permute-start | bytes 1769480 | tf_op jit(solution)/shard_map/ppermute | solution.py:437
  55.2 40.6 %all-to-all-start = ((bf16[4,48,1536]{2,1,0:T(8,128)(2,1)}), bf16[4,48,1536]{2,1,0:T(8,128)(2,1)S(1)}, u32[]{:S(2)}, u32[]{:S(2)}) async-start(bf16[4,48,1536]{2,1,0:T(8,128)(2,1)} %broadcast_in_dim.9), calls=%async_computation | async-start | bytes 1179648 | tf_op jit(solution)/shard_map/all_to_all | solution.py:477
  65.3 278.2 %reduce-scatter.2.cloned.1.call-start = ((), (), s32[]{:S(2)}) async-start(), calls=%async_computation.5 | async-start | bytes 7520256 | tf_op jit(solution)/shard_map/reduce_scatter | solution.py:555
  75.8 20.0 %collective-permute-start.19 = (bf16[128,768]{1,0:T(8,128)(2,1)}, bf16[128,768]{1,0:T(8,128)(2,1)}, u32[]{:S(2)}, u32[]{:S(2)}) collective-permute-start(bf16[128,768]{1,0:T(8,128)(2,1)} %get-tuple-element.132.refs_1_), channel_id=1, source_target_pairs={{0,2},{2,0},{4,6},{6,4},{1,3},{3,1},{5,7},{7,5},{8,10},{10,8},{12,... | collective-permute-start | bytes 589832 | tf_op jit(solution)/shard_map/ppermute | solution.py:437
  87.9 19.8 %collective-permute-start.22 = (bf16[4,48,1536]{2,1,0:T(8,128)(2,1)S(1)}, bf16[4,48,1536]{2,1,0:T(8,128)(2,1)}, u32[]{:S(2)}, u32[]{:S(2)}) collective-permute-start(bf16[4,48,1536]{2,1,0:T(8,128)(2,1)S(1)} %pad_maximum_fusion.1.refs_5_.refs_2_), channel_id=1, source_target_pairs={{0,4},{2,6},{4,0},{6,2},{1,5},{3,7},{5,1},{7,3},{8,12},{10,14},{12... | collective-permute-start | bytes 1769480 | tf_op jit(solution)/shard_map/ppermute | solution.py:441
  102.7 17.3 %collective-permute-start.25 = (bf16[4,48,1536]{2,1,0:T(8,128)(2,1)S(1)}, bf16[4,48,1536]{2,1,0:T(8,128)(2,1)S(1)}, u32[]{:S(2)}, u32[]{:S(2)}) collective-permute-start(bf16[4,48,1536]{2,1,0:T(8,128)(2,1)S(1)} %all-to-all-done.refs_9_.refs_6_), channel_id=1, source_target_pairs={{0,4},{2,6},{4,0},{6,2},{1,5},{3,7},{5,1},{7,3},{8,12},{10,14},{12... | collective-permute-start | bytes 1769480 | tf_op jit(solution)/shard_map/ppermute | solution.py:441
  224.4 30.7 %collective-permute-start.41 = (bf16[2,4,48,1536]{3,2,1,0:T(8,128)(2,1)S(1)}, bf16[2,4,48,1536]{3,2,1,0:T(8,128)(2,1)S(1)}, u32[]{:S(2)}, u32[]{:S(2)}) collective-permute-start(bf16[2,4,48,1536]{3,2,1,0:T(8,128)(2,1)S(1)} %get-tuple-element.197), channel_id=1, source_target_pairs={{0,2},{2,0},{4,6},{6,4},{1,3},{3,1},{5,7},{7,5},{8,10},{10,8},{12,... | collective-permute-start | bytes 3538952 | tf_op jit(solution)/shard_map/ppermute | solution.py:437
  233.2 22.9 %collective-permute-start.43 = (bf16[2,4,48,1536]{3,2,1,0:T(8,128)(2,1)S(1)}, bf16[2,4,48,1536]{3,2,1,0:T(8,128)(2,1)S(1)}, u32[]{:S(2)}, u32[]{:S(2)}) collective-permute-start(bf16[2,4,48,1536]{3,2,1,0:T(8,128)(2,1)S(1)} %get-tuple-element.200), channel_id=1, source_target_pairs={{0,2},{2,0},{4,6},{6,4},{1,3},{3,1},{5,7},{7,5},{8,10},{10,8},{12,... | collective-permute-start | bytes 3538952 | tf_op jit(solution)/shard_map/ppermute | solution.py:437
  255.2 21.7 %collective-permute-start.45 = (bf16[2,4,48,1536]{3,2,1,0:T(8,128)(2,1)}, bf16[2,4,48,1536]{3,2,1,0:T(8,128)(2,1)}, u32[]{:S(2)}, u32[]{:S(2)}) collective-permute-start(bf16[2,4,48,1536]{3,2,1,0:T(8,128)(2,1)} %get-tuple-element.212), channel_id=1, source_target_pairs={{0,2},{2,0},{4,6},{6,4},{1,3},{3,1},{5,7},{7,5},{8,10},{10,8},{12,... | collective-permute-start | bytes 3538952 | tf_op jit(solution)/shard_map/ppermute | solution.py:437
  255.4 15.8 %collective-permute-start.42 = (bf16[4,48,1536]{2,1,0:T(8,128)(2,1)S(1)}, bf16[4,48,1536]{2,1,0:T(8,128)(2,1)S(1)}, u32[]{:S(2)}, u32[]{:S(2)}) collective-permute-start(bf16[4,48,1536]{2,1,0:T(8,128)(2,1)S(1)} %fusion.2), channel_id=1, source_target_pairs={{0,4},{2,6},{4,0},{6,2},{1,5},{3,7},{5,1},{7,3},{8,12},{10,14},{12... | collective-permute-start | bytes 1769480 | tf_op jit(solution)/shard_map/ppermute | solution.py:441
  273.9 19.3 %collective-permute-start.47 = (bf16[4,48,1536]{2,1,0:T(8,128)(2,1)}, bf16[4,48,1536]{2,1,0:T(8,128)(2,1)}, u32[]{:S(2)}, u32[]{:S(2)}) collective-permute-start(bf16[4,48,1536]{2,1,0:T(8,128)(2,1)} %fusion.3), channel_id=1, source_target_pairs={{0,4},{2,6},{4,0},{6,2},{1,5},{3,7},{5,1},{7,3},{8,12},{10,14},{12... | collective-permute-start | bytes 1769480 | tf_op jit(solution)/shard_map/ppermute | solution.py:441
  278.8 42.7 %collective-permute-start.46 = (bf16[4,48,1536]{2,1,0:T(8,128)(2,1)}, bf16[4,48,1536]{2,1,0:T(8,128)(2,1)}, u32[]{:S(2)}, u32[]{:S(2)}) collective-permute-start(bf16[4,48,1536]{2,1,0:T(8,128)(2,1)} %fusion.4), channel_id=1, source_target_pairs={{0,4},{2,6},{4,0},{6,2},{1,5},{3,7},{5,1},{7,3},{8,12},{10,14},{12... | collective-permute-start | bytes 1769480 | tf_op jit(solution)/shard_map/ppermute | solution.py:441
  279.5 27.2 %collective-permute-start.49 = (bf16[32,768]{1,0:T(8,128)(2,1)}, bf16[32,768]{1,0:T(8,128)(2,1)}, u32[]{:S(2)}, u32[]{:S(2)}) collective-permute-start(bf16[32,768]{1,0:T(8,128)(2,1)} %add_convert_fusion.7), channel_id=1, source_target_pairs={{0,4},{2,6},{4,0},{6,2},{1,5},{3,7},{5,1},{7,3},{8,12},{10,14},{12... | collective-permute-start | bytes 147464 | tf_op jit(solution)/shard_map/ppermute | solution.py:441
  283.0 40.9 %all-to-all-start.2 = ((bf16[4,48,1536]{2,1,0:T(8,128)(2,1)}), bf16[4,48,1536]{2,1,0:T(8,128)(2,1)S(1)}, u32[]{:S(2)}, u32[]{:S(2)}) async-start(bf16[4,48,1536]{2,1,0:T(8,128)(2,1)} %fusion), calls=%async_computation.3 | async-start | bytes 1179648 | tf_op jit(solution)/shard_map/all_to_all | solution.py:581
  315.1 14.6 %collective-permute-start.50 = (bf16[48,1536]{1,0:T(8,128)(2,1)}, bf16[48,1536]{1,0:T(8,128)(2,1)S(1)}, u32[]{:S(2)}, u32[]{:S(2)}) collective-permute-start(bf16[48,1536]{1,0:T(8,128)(2,1)} %get-tuple-element.250), channel_id=1, source_target_pairs={{0,8},{8,16},{16,24},{24,0},{1,9},{9,17},{17,25},{25,1},{2,10},{10... | collective-permute-start | bytes 442376 | tf_op jit(solution)/shard_map/ppermute | solution.py:450
  315.7 14.1 %collective-permute-start.51 = (bf16[48,1536]{1,0:T(8,128)(2,1)S(1)}, bf16[48,1536]{1,0:T(8,128)(2,1)S(1)}, u32[]{:S(2)}, u32[]{:S(2)}) collective-permute-start(bf16[48,1536]{1,0:T(8,128)(2,1)S(1)} %get-tuple-element.249), channel_id=1, source_target_pairs={{0,16},{8,24},{16,0},{24,8},{1,17},{9,25},{17,1},{25,9},{2,18},{10... | collective-permute-start | bytes 442376 | tf_op jit(solution)/shard_map/ppermute | solution.py:450
  316.3 13.5 %collective-permute-start.52 = (bf16[48,1536]{1,0:T(8,128)(2,1)S(1)}, bf16[48,1536]{1,0:T(8,128)(2,1)S(1)}, u32[]{:S(2)}, u32[]{:S(2)}) collective-permute-start(bf16[48,1536]{1,0:T(8,128)(2,1)S(1)} %get-tuple-element.248), channel_id=1, source_target_pairs={{0,24},{8,0},{16,8},{24,16},{1,25},{9,1},{17,9},{25,17},{2,26},{10... | collective-permute-start | bytes 442376 | tf_op jit(solution)/shard_map/ppermute | solution.py:450
  323.8 19.5 %all-to-all-start.1 = ((bf16[4,48,1536]{2,1,0:T(8,128)(2,1)}), bf16[4,48,1536]{2,1,0:T(8,128)(2,1)S(1)}, u32[]{:S(2)}, u32[]{:S(2)}) async-start(bf16[4,48,1536]{2,1,0:T(8,128)(2,1)} %fusion.1), calls=%async_computation.1 | async-start | bytes 1179648 | tf_op jit(solution)/shard_map/all_to_all | solution.py:581
  (130 other events, 1111.8 us)
Sparse Core Ops, SparseCore 0:
  35.4 76.6 all-gather.1
  196.9 100.8 reduce-scatter.1

commit v3 on v2

--- a/solution.py
+++ b/solution.py
@@ -17,6 +17,7 @@
 CHUNK = 512
 SPLIT = 3
 VMEM_LIMIT = 46 * 1024 * 1024
+LIMIT_FB = 58 * 1024 * 1024
 ORDER = (0, 2, 1, 3)
 
 
@@ -63,7 +64,7 @@
         self.blocks = contexts == 4 and block % 16 == 0
 
 
-def run(plan, body, name, meta, inputs, weights, outs, flops, scratch=(), direct=(), ties=(), kept=()):
+def run(plan, body, name, meta, inputs, weights, outs, flops, scratch=(), direct=(), ties=(), kept=(), limit=VMEM_LIMIT):
     if ties:
         inputs = [after(inputs[0], *ties), *inputs[1:]]
     n_in, n_out = len(inputs), len(outs)
@@ -151,8 +152,8 @@
         + [anywhere] * len(kept),
         out_specs=tuple(outside if i in direct else vmem for i in range(n_out)),
         scratch_shapes=scratch_shapes + list(scratch),
-        compiler_params=pltpu.CompilerParams(vmem_limit_bytes=VMEM_LIMIT),
-        cost_estimate=pl.CostEstimate(flops=0, bytes_accessed=0, transcendentals=0),
+        compiler_params=pltpu.CompilerParams(vmem_limit_bytes=limit),
+        cost_estimate=pl.CostEstimate(flops=flops, bytes_accessed=moved, transcendentals=0),
     )
     return call(meta, *inputs, *[array for entry in weights for array in entry[0]], *kept)
 
@@ -751,15 +752,17 @@
                 [full, low, wide, low, sums],
                 2 * mm * hidden,
                 kept=[dx_mid, saved[layer + 1][0], vec, slope],
+                limit=LIMIT_FB,
                 ties=stage_of(plan, above, "send"),
             )
         db_far = swap_tp(db)
         if above is None:
-            ties = ()
+            upper_feed = Reduction(plan, meta, "feed_grad", [(b, dh), (dy, gelu)], blocks=False)
+            ties = stage_of(plan, upper_feed, "send")
         else:
             feeds = [
-                Reduction(plan, meta, "up_grad", [(b, dh)]).core(db_far),
-                Reduction(plan, meta, "down_grad", [(dy, gelu)], relative=True).core(db_far),
+                Reduction(plan, meta, "up_grad", [(b, dh)], relative=True).core(db_far),
+                Reduction(plan, meta, "down_grad", [(dy, gelu)]).core(db_far),
             ]
             ties = stage_of(plan, feeds[0], "send") + stage_of(plan, feeds[1], "send")
         if plan.blocks:
@@ -784,14 +787,13 @@
             near = swap_core(send)
             summed = add(keep[rows:], near[rows:]).astype(BF16)
             terms = [keep, near, swap_chip(summed)]
-            if above is None:
-                x_mid, part, part_far = after_all(final, summed)
-                activations = (x_mid + add(part, part_far) + bias_last).astype(BF16)
-                ties = (activations,)
         else:
             terms = [lax.psum_scatter(dkv[0], "ctx", scatter_dimension=0, tiled=True)]
-            if above is None:
-                activations = (x_mid + add(part, part_far) + bias_last).astype(BF16)
+            summed = terms[0]
+        if above is not None:
+            for one in (above, *feeds):
+                one.pairs(summed)
+                ties += stage_of(plan, one, "pair")
         dqkv, da, proj_sum = run(
             plan,
             functools.partial(project_back_body, plan),
@@ -804,14 +806,11 @@
             ties=ties,
         )
         da_far = swap_tp(da)
-        if above is None:
-            pairs = [(a, dqkv), (dz, o), (b, dh), (dy, gelu)]
-            above = Reduction(plan, meta, "layer_grad", pairs, blocks=False)
-        else:
-            attn = Reduction(plan, meta, "attn_grad", [(a, dqkv), (dz, o)]).core(da_far)
-            for feed in feeds:
-                feed.pairs(da)
-            end_ties = stage_of(plan, attn, "send") + stage_of(plan, feeds[0], "far") + stage_of(plan, feeds[1], "pair")
+        attn = Reduction(plan, meta, "attn_grad", [(a, dqkv), (dz, o)], relative=above is not None).core(da_far)
+        if above is not None:
+            end_ties = stage_of(plan, attn, "send") + stage_of(plan, above, "far")
+            upper_attn = above
+        above = attn
         small_sums[layer] = [feed_sum, attn_sum, proj_sum]
 
     grad_tokens, packet = run(
@@ -826,14 +825,18 @@
         ties=end_ties,
         kept=[dx_mid, saved[0][0], vec, *small_sums[0], *small_sums[1]],
     )
-    attn.pairs(packet)
-    feeds[0].along(packet, *stage_of(plan, attn, "pair"))
-    feeds[1].along(packet, *stage_of(plan, feeds[0], "sums"))
+    upper_attn.along(packet)
+    attn.pairs(packet, *stage_of(plan, feeds[0], "far"))
+    feeds[0].along(packet, *stage_of(plan, upper_attn, "sums"), *stage_of(plan, upper_feed, "total"))
+    feeds[1].along(*stage_of(plan, feeds[0], "sums"), *stage_of(plan, attn, "pair"))
+    attn.along(*stage_of(plan, feeds[1], "sums"), *stage_of(plan, feeds[0], "got"))
+    x_mid, part, part_far = after_all(final, packet)
+    activations = (x_mid + add(part, part_far) + bias_last).astype(BF16)
     start = (z * contexts + c) * block
     if plan.blocks:
         packet = add(packet, swap_core(packet)).astype(BF16)
-        packet = after(packet, attn.pair)
-        packet = add(packet, swap_chip(packet)).astype(BF16)
+        far = after(swap_chip(packet), *attn.sums)
+        packet = add(packet, far).astype(BF16)
         got = jnp.stack([packet] + [to_shard(plan, packet, k) for k in range(1, shards)])
         other = add(*[got[k] for k in range(0, shards, 2)]) + add(*[got[k] for k in range(1, shards, 2)])
     else:
@@ -845,8 +848,7 @@
     one_hot = (jnp.arange(table.shape[0], dtype=jnp.int32)[:, None] == steps_back.reshape(-1)[None, :]).astype(BF16)
     grad_table = jnp.dot(one_hot, mine, preferred_element_type=F32)
 
-    attn.along(*stage_of(plan, feeds[1], "sums"))
-    upper_grad = above.end(packet)
+    upper_feed, upper_attn = upper_feed.end(packet), upper_attn.end(packet)
     halves = hidden // width
     per_layer = 5 + halves
     by_layer = other[16 : 16 + layers * per_layer].reshape(layers, per_layer, width)
@@ -856,15 +858,14 @@
     grad_up_bias = by_layer[:, 4 : 4 + halves].reshape(layers, hidden)
     grad_query_bias = by_layer[:, 4 + halves, :heads_width]
     grad_value_bias = by_layer[:, 4 + halves, heads_width:]
-    at = n3 + heads_width
-    ups = [feeds[0].end(), upper_grad[:, at : at + hidden]]
-    downs = [feeds[1].end(), upper_grad[:, at + hidden :]]
-    attns = [attn.end(), upper_grad[:, :at]]
+    ups = [feeds[0].end(), upper_feed[:, :hidden]]
+    downs = [feeds[1].end(), upper_feed[:, hidden:]]
+    attns = [attn.end(), upper_attn]
     return (
         activations,
         grad_tokens,
         jnp.stack([g[:, :n3].reshape(block, 3, heads_width) for g in attns]),
-        jnp.stack([g[:, n3:at] for g in attns]),
+        jnp.stack([g[:, n3:] for g in attns]),
         jnp.stack(ups),
         jnp.stack(downs),
         grad_norms,

time: 360 us -> 343 us (0.953)
  waiting for transfers between devices: 152 us -> 129 us
  starting transfers between devices: 71.7 us -> 81.5 us
  local copies, waits for them, and re-layouts: 33.8 us -> 26.5 us
  Pallas kernels: 61.1 us -> 65.7 us
    ppermute x12 -> x13, waiting for transfers between devices: 82.3 us -> 67.4 us  [swap_chip(): return lax.ppermute(array, 'ctx', [(i, i ^ 2) for i in range(4)])]
    ppermute x18 -> x21, waiting for transfers between devices: 14.7 us -> 24.7 us  [to_shard(): lax.ppermute(array, 'shard', [(i, (i + shift) % n) for i in range(n)])]
    all_to_all x2, waiting for transfers between devices: 13.4 us -> 3.42 us  [along(): self.got = lax.all_to_all(self.sums, 'shard', 0, 0, tiled=True)]
    ppermute x8, waiting for transfers between devices: 26.6 us -> 16.8 us  [swap_tp(): return lax.ppermute(array, 'tp', [(0, 1), (1, 0)])]
    unnamed x193 -> x183, local copies, waits for them, and re-layouts: 28.2 us -> 20.9 us
    pallas_call x16 -> x17, Pallas kernels: 61.1 us -> 65.7 us  [run(): call(meta, *inputs, *[array for entry in weights for array in entry[0]],...]
    ppermute x18 -> x21, starting transfers between devices: 31.7 us -> 36.2 us  [to_shard(): lax.ppermute(array, 'shard', [(i, (i + shift) % n) for i in range(n)])]
    ppermute x12 -> x13, starting transfers between devices: 6.91 us -> 8.28 us  [swap_chip(): return lax.ppermute(array, 'ctx', [(i, i ^ 2) for i in range(4)])]
  transfers between devices with their start and end apart: 61 -> 66, of which waited for: 32 -> 31; matrix products, arithmetic and copies ran while one was open for 6% -> 8% of each run, Pallas kernels for 11% -> 15%
where the time goes in v3:
time: 343 us; the launch traced here: 339 us
  waiting for transfers between devices  129 us (38%)
  starting transfers between devices  81.5 us (24%)
  Pallas kernels  65.7 us (19%)
  local copies, waits for them, and re-layouts  26.5 us (8%)
  other arithmetic  20.1 us (6%)
  between operations  15.7 us (5%)
    ppermute x13, waiting for transfers between devices, swap_chip(): return lax.ppermute(array, 'ctx', [(i, i ^ 2) for i in range(4)])  67.4 us
    pallas_call x17, Pallas kernels, run(): call(meta, *inputs, *[array for entry in weights for array in entry[0]],...  65.7 us
    ppermute x21, starting transfers between devices, to_shard(): lax.ppermute(array, 'shard', [(i, (i + shift) % n) for i in range(n)])  36.2 us
    ppermute x21, waiting for transfers between devices, to_shard(): lax.ppermute(array, 'shard', [(i, (i + shift) % n) for i in range(n)])  24.7 us
    unnamed x183, local copies, waits for them, and re-layouts  20.9 us
    ppermute x8, waiting for transfers between devices, swap_tp(): return lax.ppermute(array, 'tp', [(0, 1), (1, 0)])  16.8 us
    all_to_all x1, starting transfers between devices, at_once(): self.stack = lax.all_to_all(copies, 'shard', 0, 0, tiled=True)  13.4 us
    ppermute x8, starting transfers between devices, swap_tp(): return lax.ppermute(array, 'tp', [(0, 1), (1, 0)])  13 us
  transfers between devices with their start and end apart: 66, of which 31 were waited for; matrix products, arithmetic and copies ran while one was open for 8% of the time, Pallas kernels for 15%

profile of v3, /device:TPU:0, one launch (start us, length us, event | category | flops | bytes accessed | tf_op | source)
XLA Modules:
  0.0 339.3 jit_solution(9286405499332375616)
XLA Ops:
  9.3 5.1 %collective-permute-start.5 = (s32[1,9]{1,0:T(1,128)S(1)}, s32[1,9]{1,0:T(1,128)S(1)}, u32[]{:S(2)}, u32[]{:S(2)}) collective-permute-start(s32[1,9]{1,0:T(1,128)S(1)} %copy-done.86), channel_id=1, source_target_pairs={{0,24},{8,0},{16,8},{24,16},{1,25},{9,1},{17,9},{25,17},{2,26},{10... | collective-permute-start | bytes 116 | tf_op jit(solution)/shard_map/ppermute | solution.py:451
  43.8 4.9 %collective-permute-done.10 = bf16[48,1536]{1,0:T(8,128)(2,1)S(1)} collective-permute-done((bf16[48,1536]{1,0:T(8,128)(2,1)S(1)}, bf16[48,1536]{1,0:T(8,128)(2,1)S(1)}, u32[]{:S(2)}, u32[]{:S(2)}) %collective-permute-start.10) | collective-permute-done | bytes 147488 | tf_op jit(solution)/shard_map/ppermute | solution.py:451
  53.0 13.4 %all-to-all-start = ((bf16[4,48,1536]{2,1,0:T(8,128)(2,1)}), bf16[4,48,1536]{2,1,0:T(8,128)(2,1)S(1)}, u32[]{:S(2)}, u32[]{:S(2)}) async-start(bf16[4,48,1536]{2,1,0:T(8,128)(2,1)} %broadcast_in_dim.9), calls=%async_computation | async-start | bytes 1179648 | tf_op jit(solution)/shard_map/all_to_all | solution.py:478
  72.0 4.0 %embed.1 = (f32[128,768]{1,0:T(8,128)S(1)}, f32[8,768]{1,0:T(8,128)S(1)}, bf16[128,768]{1,0:T(8,128)(2,1)S(1)}, bf16[128,384]{1,0:T(8,128)(2,1)S(1)}, bf16[128,768]{1,0:T(8,128)(2,1)}) custom-call(s32[10]{0:T(128)S(1)} %pad_add_fusion.3.meta_ref, bf16[128,768]{1,0:T(8,128)(2,1)S(1)} %copy-done.39, bf16[2,384]{1,0:T(2,128)(2,1)S(1)} %copy-done.53, ...), custom_call_target="tpu_custom_call" | custom-call | flops 226492416 | bytes 3075072 | tf_op jit(solution)/shard_map/embed/pallas_call | solution.py:158
  76.3 11.7 %collective-permute-done.18.refs_2_ = bf16[128,768]{1,0:T(8,128)(2,1)S(1)} collective-permute-done((bf16[128,768]{1,0:T(8,128)(2,1)}, bf16[128,768]{1,0:T(8,128)(2,1)S(1)}, u32[]{:S(2)}, u32[]{:S(2)}) %collective-permute-start.18) | collective-permute-done | bytes 196640 | tf_op jit(solution)/shard_map/ppermute | solution.py:442
  89.1 8.1 %all-to-all-done.refs_9_.refs_6_ = bf16[4,48,1536]{2,1,0:T(8,128)(2,1)S(1)} async-done(((bf16[4,48,1536]{2,1,0:T(8,128)(2,1)}), bf16[4,48,1536]{2,1,0:T(8,128)(2,1)S(1)}, u32[]{:S(2)}, u32[]{:S(2)}) %all-to-all-start) | async-done | bytes 589856 | tf_op jit(solution)/shard_map/all_to_all | solution.py:478
  109.9 10.3 %collective-permute-done.25.refs_10_.refs_7_ = bf16[4,48,1536]{2,1,0:T(8,128)(2,1)S(1)} collective-permute-done((bf16[4,48,1536]{2,1,0:T(8,128)(2,1)S(1)}, bf16[4,48,1536]{2,1,0:T(8,128)(2,1)S(1)}, u32[]{:S(2)}, u32[]{:S(2)}) %collective-permute-start.25) | collective-permute-done | bytes 589856 | tf_op jit(solution)/shard_map/ppermute | solution.py:442
  123.1 4.4 %feed.2 = (f32[128,768]{1,0:T(8,128)S(1)}, bf16[128,768]{1,0:T(8,128)(2,1)S(1)}, bf16[128,1536]{1,0:T(8,128)(2,1)S(1)}, f32[128,1536]{1,0:T(8,128)S(1)}, bf16[128,768]{1,0:T(8,128)(2,1)S(1)}) custom-call(s32[10]{0:T(128)S(1)} %pad_add_fusion.3.meta_ref, f32[128,768]{1,0:T(8,128)S(1)} %copy-done.11, bf16[128,768]{1,0:T(8,128)(2,1)S(1)} %get-tuple-element.150.refs_1_, ...), custom_call_target="tpu_custom_call" | custom-call | flops 603979776 | bytes 7501824 | tf_op jit(solution)/shard_map/feed/pallas_call | solution.py:158
  132.1 4.8 %collective-permute-done.28.refs_2_ = bf16[128,768]{1,0:T(8,128)(2,1)S(1)} collective-permute-done((bf16[128,768]{1,0:T(8,128)(2,1)S(1)}, bf16[128,768]{1,0:T(8,128)(2,1)S(1)}, u32[]{:S(2)}, u32[]{:S(2)}) %collective-permute-start.28) | collective-permute-done | bytes 196640 | tf_op jit(solution)/shard_map/ppermute | solution.py:446
  141.5 5.8 %collective-permute-done.29.refs_2_ = bf16[128,768]{1,0:T(8,128)(2,1)S(1)} collective-permute-done((bf16[128,768]{1,0:T(8,128)(2,1)S(1)}, bf16[128,768]{1,0:T(8,128)(2,1)S(1)}, u32[]{:S(2)}, u32[]{:S(2)}) %collective-permute-start.29) | collective-permute-done | bytes 196640 | tf_op jit(solution)/shard_map/ppermute | solution.py:442
  153.6 5.5 %collective-permute-done.32.refs_2_ = bf16[128,768]{1,0:T(8,128)(2,1)S(1)} collective-permute-done((bf16[128,768]{1,0:T(8,128)(2,1)S(1)}, bf16[128,768]{1,0:T(8,128)(2,1)S(1)}, u32[]{:S(2)}, u32[]{:S(2)}) %collective-permute-start.32) | collective-permute-done | bytes 196640 | tf_op jit(solution)/shard_map/ppermute | solution.py:446
  159.1 5.2 %feed.3 = (f32[128,768]{1,0:T(8,128)S(1)}, bf16[128,768]{1,0:T(8,128)(2,1)S(1)}, bf16[128,1536]{1,0:T(8,128)(2,1)S(1)}, f32[128,1536]{1,0:T(8,128)}, bf16[128,76...) custom-call(s32[10]{0:T(128)S(1)} %pad_add_fusion.3.meta_ref, ...), custom_call_target="tpu_custom_call" | custom-call | flops 1207959552 | bytes 8312832 | tf_op jit(solution)/shard_map/feed/pallas_call | solution.py:158
  165.7 4.5 %feed_grad.1 = bf16[768,3072]{1,0:T(8,128)(2,1)S(1)} custom-call(s32[10]{0:T(128)S(1)} %pad_add_fusion.3.meta_ref, bf16[128,768]{1,0:T(8,128)(2,1)S(1)} %get-tuple-element.166.refs_0_, bf16[128,1536]{1,0:T(8,128)(2,1)S(1)} %get-tuple-element.167.refs_1_, bf16[128,768]{1,0:T(8,128)(2,1)S(1)} %copy-done.9, bf16[128,1536]{1,0:T(8,128)(2,1)S(1)} %get-tuple-element.168.refs_3_), custom_call_target="tpu_custom_call" | custom-call | flops 603979776 | bytes 4718592 | tf_op jit(solution)/shard_map/feed_grad/pallas_call | solution.py:158
  174.0 4.9 %collective-permute-done.34.refs_2_ = bf16[128,768]{1,0:T(8,128)(2,1)S(1)} collective-permute-done((bf16[128,768]{1,0:T(8,128)(2,1)}, bf16[128,768]{1,0:T(8,128)(2,1)S(1)}, u32[]{:S(2)}, u32[]{:S(2)}) %collective-permute-start.34) | collective-permute-done | bytes 196640 | tf_op jit(solution)/shard_map/ppermute | solution.py:446
  181.0 4.3 %attend_back.2 = (f32[128,768]{1,0:T(8,128)S(1)}, bf16[128,768]{1,0:T(8,128)(2,1)S(1)}, bf16[128,384]{1,0:T(8,128)(2,1)S(1)}, f32[8,768]{1,0:T(8,128)S(1)}, bf16...) custom-call(s32[10]{0:T(128)S(1)} %pad_add_fusion.3.meta_ref, bf16[128,768]{1,0:T(8,128)(2,1)S(1)} %copy-done.9, ...), custom_call_target="tpu_custom_call" | custom-call | flops 327155712 | bytes 2678784 | tf_op jit(solution)/shard_map/attend_back/pallas_call | solution.py:158
  188.2 6.6 %collective-permute-done.36.refs_3_ = bf16[128,768]{1,0:T(8,128)(2,1)S(1)} collective-permute-done((bf16[128,768]{1,0:T(8,128)(2,1)S(1)}, bf16[128,768]{1,0:T(8,128)(2,1)S(1)}, u32[]{:S(2)}, u32[]{:S(2)}) %collective-permute-start.36) | collective-permute-done | bytes 196640 | tf_op jit(solution)/shard_map/ppermute | solution.py:442
  199.3 4.4 %attn_grad.2 = (bf16[2,4,48,1536]{3,2,1,0:T(8,128)(2,1)S(1)}, bf16[2,4,48,1536]{3,2,1,0:T(8,128)(2,1)}) custom-call(s32[10]{0:T(128)S(1)} %pad_add_fusion.3.meta_ref, bf16[128,768]{1,0:T(8,128)(2,1)S(1)} %copy-done.63, bf16[128,1152]{1,0:T(8,128)(2,1)S(1)} %get-tuple-element.178.refs_1_, bf16[128,768]{1,0:T(8,128)(2,1)S(1)} %get-tuple-element.179.refs_2_, ...), custom_call_target="tpu_custom_call" | custom-call | flops 301989888 | bytes 2359296 | tf_op jit(solution)/shard_map/attn_grad/pallas_call | solution.py:158
  204.5 6.6 %feed_back.1 = (f32[128,768]{1,0:T(8,128)}, bf16[128,768]{1,0:T(8,128)(2,1)}, bf16[128,1536]{1,0:T(8,128)(2,1)}, bf16[128,768]{1,0:T(8,128)(2,1)}, f32[8,768]{1,0:T(8,128)}) custom-call(s32[10]{0:T(128)} %copy-done.47, bf16[128,768]{1,0:T(8,128)(2,1)} %copy-done.42, bf16[128,768]{1,0:T(8,128)(2,1)} %copy-done.76, ...), custom_call_target="tpu_custom_call" | custom-call | flops 603979776 | bytes 6316032 | tf_op jit(solution)/shard_map/feed_back/pallas_call | solution.py:158
  222.7 4.6 %attend_back.3 = (f32[128,768]{1,0:T(8,128)S(1)}, bf16[128,768]{1,0:T(8,128)(2,1)S(1)}, bf16[128,384]{1,0:T(8,128)(2,1)S(1)}, f32[8,768]{1,0:T(8,128)S(1)}, bf16...) custom-call(s32[10]{0:T(128)S(1)} %copy-done.48, f32[128,768]{1,0:T(8,128)S(1)} %copy-done.32, ...), custom_call_target="tpu_custom_call" | custom-call | flops 327155712 | bytes 2875392 | tf_op jit(solution)/shard_map/attend_back/pallas_call | solution.py:158
  240.9 4.5 %attn_grad.3 = (bf16[2,4,48,1536]{3,2,1,0:T(8,128)(2,1)S(1)}, bf16[2,4,48,1536]{3,2,1,0:T(8,128)(2,1)}) custom-call(s32[10]{0:T(128)S(1)} %copy-done.48, bf16[128,768]{1,0:T(8,128)(2,1)S(1)} %copy-done.59, bf16[128,1152]{1,0:T(8,128)(2,1)S(1)} %get-tuple-element.211.refs_1_, bf16[128,768]{1,0:T(8,128)(2,1)S(1)} %get-tuple-element.212.refs_2_, ...), custom_call_target="tpu_custom_call" | custom-call | flops 301989888 | bytes 2359296 | tf_op jit(solution)/shard_map/attn_grad/pallas_call | solution.py:158
  256.9 4.7 %all-to-all-start.1 = ((bf16[4,48,1536]{2,1,0:T(8,128)(2,1)}), bf16[4,48,1536]{2,1,0:T(8,128)(2,1)}, u32[]{:S(2)}, u32[]{:S(2)}) async-start(bf16[4,48,1536]{2,1,0:T(8,128)(2,1)} %fusion), calls=%async_computation.2 | async-start | bytes 1179648 | tf_op jit(solution)/shard_map/all_to_all | solution.py:582
  262.9 15.1 %collective-permute-done.47 = bf16[4,48,1536]{2,1,0:T(8,128)(2,1)} collective-permute-done((bf16[4,48,1536]{2,1,0:T(8,128)(2,1)}, bf16[4,48,1536]{2,1,0:T(8,128)(2,1)}, u32[]{:S(2)}, u32[]{:S(2)}) %collective-permute-start.47) | collective-permute-done | bytes 589856 | tf_op jit(solution)/shard_map/ppermute | solution.py:442
  288.0 5.5 %collective-permute-done.48 = bf16[4,48,1536]{2,1,0:T(8,128)(2,1)} collective-permute-done((bf16[4,48,1536]{2,1,0:T(8,128)(2,1)S(1)}, bf16[4,48,1536]{2,1,0:T(8,128)(2,1)}, u32[]{:S(2)}, u32[]{:S(2)}) %collective-permute-start.48) | collective-permute-done | bytes 589856 | tf_op jit(solution)/shard_map/ppermute | solution.py:442
  316.5 9.4 %collective-permute-done.54 = bf16[48,1536]{1,0:T(8,128)(2,1)S(1)} collective-permute-done((bf16[48,1536]{1,0:T(8,128)(2,1)S(1)}, bf16[48,1536]{1,0:T(8,128)(2,1)S(1)}, u32[]{:S(2)}, u32[]{:S(2)}) %collective-permute-start.54) | collective-permute-done | bytes 147488 | tf_op jit(solution)/shard_map/ppermute | solution.py:451
  (380 shorter events, 165.5 us)
Async XLA Ops:
  7.2 129.6 %all-gather.2.cloned.1.call-start = ((), (), s32[]{:S(2)}) async-start(), calls=%async_computation.4 | async-start | bytes 7520256 | tf_op jit(solution)/shard_map/all_gather | solution.py:621
  15.4 18.2 %collective-permute-start.2 = (bf16[48,1536]{1,0:T(8,128)(2,1)S(1)}, bf16[48,1536]{1,0:T(8,128)(2,1)S(1)}, u32[]{:S(2)}, u32[]{:S(2)}) collective-permute-start(bf16[48,1536]{1,0:T(8,128)(2,1)S(1)} %pad_maximum_fusion.6), channel_id=1, source_target_pairs={{0,24},{8,0},{16,8},{24,16},{1,25},{9,1},{17,9},{25,17},{2,26},{10... | collective-permute-start | bytes 442376 | tf_op jit(solution)/shard_map/ppermute | solution.py:451
  18.2 15.3 %collective-permute-start.1 = (bf16[48,1536]{1,0:T(8,128)(2,1)S(1)}, bf16[48,1536]{1,0:T(8,128)(2,1)S(1)}, u32[]{:S(2)}, u32[]{:S(2)}) collective-permute-start(bf16[48,1536]{1,0:T(8,128)(2,1)S(1)} %pad_maximum_fusion.6), channel_id=1, source_target_pairs={{0,16},{8,24},{16,0},{24,8},{1,17},{9,25},{17,1},{25,9},{2,18},{10... | collective-permute-start | bytes 442376 | tf_op jit(solution)/shard_map/ppermute | solution.py:451
  19.8 13.8 %collective-permute-start = (bf16[48,1536]{1,0:T(8,128)(2,1)S(1)}, bf16[48,1536]{1,0:T(8,128)(2,1)S(1)}, u32[]{:S(2)}, u32[]{:S(2)}) collective-permute-start(bf16[48,1536]{1,0:T(8,128)(2,1)S(1)} %pad_maximum_fusion.6), channel_id=1, source_target_pairs={{0,8},{8,16},{16,24},{24,0},{1,9},{9,17},{17,25},{25,1},{2,10},{10... | collective-permute-start | bytes 442376 | tf_op jit(solution)/shard_map/ppermute | solution.py:451
  33.7 17.9 %collective-permute-start.12 = (bf16[4,48,1536]{2,1,0:T(8,128)(2,1)S(1)}, bf16[4,48,1536]{2,1,0:T(8,128)(2,1)S(1)}, u32[]{:S(2)}, u32[]{:S(2)}) collective-permute-start(bf16[4,48,1536]{2,1,0:T(8,128)(2,1)S(1)} %pad_maximum_fusion.refs_3_.refs_5_.refs_4_), channel_id=1, source_target_pairs={{0,4},{2,6},{4,0},{6,2},{1,5},{3,7},{5,1},{7,3},{8,12},{10,14},{12... | collective-permute-start | bytes 1769480 | tf_op jit(solution)/shard_map/ppermute | solution.py:442
  51.7 20.3 %collective-permute-start.13 = (bf16[4,48,1536]{2,1,0:T(8,128)(2,1)S(1)}, bf16[4,48,1536]{2,1,0:T(8,128)(2,1)S(1)}, u32[]{:S(2)}, u32[]{:S(2)}) collective-permute-start(bf16[4,48,1536]{2,1,0:T(8,128)(2,1)S(1)} %pad_maximum_fusion.refs_3_.refs_5_.refs_4_), channel_id=1, source_target_pairs={{0,2},{2,0},{4,6},{6,4},{1,3},{3,1},{5,7},{7,5},{8,10},{10,8},{12,... | collective-permute-start | bytes 1769480 | tf_op jit(solution)/shard_map/ppermute | solution.py:438
  51.7 20.3 %collective-permute-start.14 = (bf16[4,48,1536]{2,1,0:T(8,128)(2,1)S(1)}, bf16[4,48,1536]{2,1,0:T(8,128)(2,1)S(1)}, u32[]{:S(2)}, u32[]{:S(2)}) collective-permute-start(bf16[4,48,1536]{2,1,0:T(8,128)(2,1)S(1)} %collective-permute-done.12.refs_4_.refs_6_.refs_5_), channel_id=1, source_target_pairs={{0,2},{2,0},{4,6},{6,4},{1,3},{3,1},{5,7},{7,5},{8,10},{10,8},{12,... | collective-permute-start | bytes 1769480 | tf_op jit(solution)/shard_map/ppermute | solution.py:438
  53.0 44.1 %all-to-all-start = ((bf16[4,48,1536]{2,1,0:T(8,128)(2,1)}), bf16[4,48,1536]{2,1,0:T(8,128)(2,1)S(1)}, u32[]{:S(2)}, u32[]{:S(2)}) async-start(bf16[4,48,1536]{2,1,0:T(8,128)(2,1)} %broadcast_in_dim.9), calls=%async_computation | async-start | bytes 1179648 | tf_op jit(solution)/shard_map/all_to_all | solution.py:478
  66.4 213.4 %reduce-scatter.2.cloned.1.call-start = ((), (), s32[]{:S(2)}) async-start(), calls=%async_computation.5 | async-start | bytes 5013504 | tf_op jit(solution)/shard_map/reduce_scatter | solution.py:556
  76.3 20.9 %collective-permute-start.19 = (bf16[128,768]{1,0:T(8,128)(2,1)}, bf16[128,768]{1,0:T(8,128)(2,1)S(1)}, u32[]{:S(2)}, u32[]{:S(2)}) collective-permute-start(bf16[128,768]{1,0:T(8,128)(2,1)} %get-tuple-element.143.refs_1_), channel_id=1, source_target_pairs={{0,2},{2,0},{4,6},{6,4},{1,3},{3,1},{5,7},{7,5},{8,10},{10,8},{12,... | collective-permute-start | bytes 589832 | tf_op jit(solution)/shard_map/ppermute | solution.py:438
  88.9 19.0 %collective-permute-start.22 = (bf16[4,48,1536]{2,1,0:T(8,128)(2,1)}, bf16[4,48,1536]{2,1,0:T(8,128)(2,1)}, u32[]{:S(2)}, u32[]{:S(2)}) collective-permute-start(bf16[4,48,1536]{2,1,0:T(8,128)(2,1)} %pad_maximum_fusion.1.refs_5_.refs_2_), channel_id=1, source_target_pairs={{0,4},{2,6},{4,0},{6,2},{1,5},{3,7},{5,1},{7,3},{8,12},{10,14},{12... | collective-permute-start | bytes 1769480 | tf_op jit(solution)/shard_map/ppermute | solution.py:442
  103.2 17.0 %collective-permute-start.25 = (bf16[4,48,1536]{2,1,0:T(8,128)(2,1)S(1)}, bf16[4,48,1536]{2,1,0:T(8,128)(2,1)S(1)}, u32[]{:S(2)}, u32[]{:S(2)}) collective-permute-start(bf16[4,48,1536]{2,1,0:T(8,128)(2,1)S(1)} %all-to-all-done.refs_9_.refs_6_), channel_id=1, source_target_pairs={{0,4},{2,6},{4,0},{6,2},{1,5},{3,7},{5,1},{7,3},{8,12},{10,14},{12... | collective-permute-start | bytes 1769480 | tf_op jit(solution)/shard_map/ppermute | solution.py:442
  203.7 25.9 %collective-permute-start.39 = (bf16[2,4,48,1536]{3,2,1,0:T(8,128)(2,1)}, bf16[2,4,48,1536]{3,2,1,0:T(8,128)(2,1)}, u32[]{:S(2)}, u32[]{:S(2)}) collective-permute-start(bf16[2,4,48,1536]{3,2,1,0:T(8,128)(2,1)} %get-tuple-element.198), channel_id=1, source_target_pairs={{0,2},{2,0},{4,6},{6,4},{1,3},{3,1},{5,7},{7,5},{8,10},{10,8},{12,... | collective-permute-start | bytes 3538952 | tf_op jit(solution)/shard_map/ppermute | solution.py:438
  231.7 20.4 %collective-permute-start.44 = (bf16[4,48,1536]{2,1,0:T(8,128)(2,1)}, bf16[4,48,1536]{2,1,0:T(8,128)(2,1)}, u32[]{:S(2)}, u32[]{:S(2)}) collective-permute-start(bf16[4,48,1536]{2,1,0:T(8,128)(2,1)} %fusion.2), channel_id=1, source_target_pairs={{0,4},{2,6},{4,0},{6,2},{1,5},{3,7},{5,1},{7,3},{8,12},{10,14},{12... | collective-permute-start | bytes 1769480 | tf_op jit(solution)/shard_map/ppermute | solution.py:442
  246.5 31.5 %collective-permute-start.46 = (bf16[2,4,48,1536]{3,2,1,0:T(8,128)(2,1)}, bf16[2,4,48,1536]{3,2,1,0:T(8,128)(2,1)}, u32[]{:S(2)}, u32[]{:S(2)}) collective-permute-start(bf16[2,4,48,1536]{3,2,1,0:T(8,128)(2,1)} %get-tuple-element.229), channel_id=1, source_target_pairs={{0,2},{2,0},{4,6},{6,4},{1,3},{3,1},{5,7},{7,5},{8,10},{10,8},{12,... | collective-permute-start | bytes 3538952 | tf_op jit(solution)/shard_map/ppermute | solution.py:438
  249.1 35.5 %collective-permute-start.49 = (bf16[4,48,1536]{2,1,0:T(8,128)(2,1)}, bf16[4,48,1536]{2,1,0:T(8,128)(2,1)}, u32[]{:S(2)}, u32[]{:S(2)}) collective-permute-start(bf16[4,48,1536]{2,1,0:T(8,128)(2,1)} %fusion.4), channel_id=1, source_target_pairs={{0,4},{2,6},{4,0},{6,2},{1,5},{3,7},{5,1},{7,3},{8,12},{10,14},{12... | collective-permute-start | bytes 1769480 | tf_op jit(solution)/shard_map/ppermute | solution.py:442
  249.6 28.4 %collective-permute-start.47 = (bf16[4,48,1536]{2,1,0:T(8,128)(2,1)}, bf16[4,48,1536]{2,1,0:T(8,128)(2,1)}, u32[]{:S(2)}, u32[]{:S(2)}) collective-permute-start(bf16[4,48,1536]{2,1,0:T(8,128)(2,1)} %fusion.3), channel_id=1, source_target_pairs={{0,4},{2,6},{4,0},{6,2},{1,5},{3,7},{5,1},{7,3},{8,12},{10,14},{12... | collective-permute-start | bytes 1769480 | tf_op jit(solution)/shard_map/ppermute | solution.py:442
  256.9 48.1 %all-to-all-start.1 = ((bf16[4,48,1536]{2,1,0:T(8,128)(2,1)}), bf16[4,48,1536]{2,1,0:T(8,128)(2,1)}, u32[]{:S(2)}, u32[]{:S(2)}) async-start(bf16[4,48,1536]{2,1,0:T(8,128)(2,1)} %fusion), calls=%async_computation.2 | async-start | bytes 1179648 | tf_op jit(solution)/shard_map/all_to_all | solution.py:582
  262.4 36.0 %collective-permute-start.57 = (bf16[32,768]{1,0:T(8,128)(2,1)S(1)}, bf16[32,768]{1,0:T(8,128)(2,1)S(1)}, u32[]{:S(2)}, u32[]{:S(2)}) collective-permute-start(bf16[32,768]{1,0:T(8,128)(2,1)S(1)} %add_convert_fusion.8), channel_id=1, source_target_pairs={{0,4},{2,6},{4,0},{6,2},{1,5},{3,7},{5,1},{7,3},{8,12},{10,14},{12... | collective-permute-start | bytes 147464 | tf_op jit(solution)/shard_map/ppermute | solution.py:442
  279.2 14.3 %collective-permute-start.48 = (bf16[4,48,1536]{2,1,0:T(8,128)(2,1)S(1)}, bf16[4,48,1536]{2,1,0:T(8,128)(2,1)}, u32[]{:S(2)}, u32[]{:S(2)}) collective-permute-start(bf16[4,48,1536]{2,1,0:T(8,128)(2,1)S(1)} %fusion.5), channel_id=1, source_target_pairs={{0,4},{2,6},{4,0},{6,2},{1,5},{3,7},{5,1},{7,3},{8,12},{10,14},{12... | collective-permute-start | bytes 1769480 | tf_op jit(solution)/shard_map/ppermute | solution.py:442
  302.6 13.9 %collective-permute-start.55 = (bf16[48,1536]{1,0:T(8,128)(2,1)S(1)}, bf16[48,1536]{1,0:T(8,128)(2,1)S(1)}, u32[]{:S(2)}, u32[]{:S(2)}) collective-permute-start(bf16[48,1536]{1,0:T(8,128)(2,1)S(1)} %get-tuple-element.270), channel_id=1, source_target_pairs={{0,24},{8,0},{16,8},{24,16},{1,25},{9,1},{17,9},{25,17},{2,26},{10... | collective-permute-start | bytes 442376 | tf_op jit(solution)/shard_map/ppermute | solution.py:451
  303.6 22.3 %collective-permute-start.54 = (bf16[48,1536]{1,0:T(8,128)(2,1)S(1)}, bf16[48,1536]{1,0:T(8,128)(2,1)S(1)}, u32[]{:S(2)}, u32[]{:S(2)}) collective-permute-start(bf16[48,1536]{1,0:T(8,128)(2,1)S(1)} %get-tuple-element.271), channel_id=1, source_target_pairs={{0,16},{8,24},{16,0},{24,8},{1,17},{9,25},{17,1},{25,9},{2,18},{10... | collective-permute-start | bytes 442376 | tf_op jit(solution)/shard_map/ppermute | solution.py:451
  305.0 26.1 %all-to-all-start.2 = ((bf16[4,48,1536]{2,1,0:T(8,128)(2,1)}), bf16[4,48,1536]{2,1,0:T(8,128)(2,1)S(1)}, u32[]{:S(2)}, u32[]{:S(2)}) async-start(bf16[4,48,1536]{2,1,0:T(8,128)(2,1)} %fusion.1), calls=%async_computation.3 | async-start | bytes 1179648 | tf_op jit(solution)/shard_map/all_to_all | solution.py:582
  310.8 15.0 %collective-permute-start.53 = (bf16[48,1536]{1,0:T(8,128)(2,1)S(1)}, bf16[48,1536]{1,0:T(8,128)(2,1)S(1)}, u32[]{:S(2)}, u32[]{:S(2)}) collective-permute-start(bf16[48,1536]{1,0:T(8,128)(2,1)S(1)} %get-tuple-element.272), channel_id=1, source_target_pairs={{0,8},{8,16},{16,24},{24,0},{1,9},{9,17},{17,25},{25,1},{2,10},{10... | collective-permute-start | bytes 442376 | tf_op jit(solution)/shard_map/ppermute | solution.py:451
  (130 other events, 1441.9 us)
Sparse Core Ops, SparseCore 0:
  33.8 79.2 all-gather.1
  172.6 78.7 reduce-scatter.1

commit v4 on v3

--- a/solution.py
+++ b/solution.py
@@ -808,7 +808,8 @@
         da_far = swap_tp(da)
         attn = Reduction(plan, meta, "attn_grad", [(a, dqkv), (dz, o)], relative=above is not None).core(da_far)
         if above is not None:
-            end_ties = stage_of(plan, attn, "send") + stage_of(plan, above, "far")
+            above.along(da)
+            end_ties = stage_of(plan, attn, "send") + stage_of(plan, above, "sums") + stage_of(plan, feeds[0], "far")
             upper_attn = above
         above = attn
         small_sums[layer] = [feed_sum, attn_sum, proj_sum]
@@ -825,7 +826,6 @@
         ties=end_ties,
         kept=[dx_mid, saved[0][0], vec, *small_sums[0], *small_sums[1]],
     )
-    upper_attn.along(packet)
     attn.pairs(packet, *stage_of(plan, feeds[0], "far"))
     feeds[0].along(packet, *stage_of(plan, upper_attn, "sums"), *stage_of(plan, upper_feed, "total"))
     feeds[1].along(*stage_of(plan, feeds[0], "sums"), *stage_of(plan, attn, "pair"))

time: 343 us -> 339 us (0.988)
  waiting for transfers between devices: 129 us -> 120 us
  starting transfers between devices: 81.5 us -> 85.8 us
    ppermute x13, waiting for transfers between devices: 67.4 us -> 62.6 us  [swap_chip(): return lax.ppermute(array, 'ctx', [(i, i ^ 2) for i in range(4)])]
    ppermute x21, waiting for transfers between devices: 24.7 us -> 20.9 us  [to_shard(): lax.ppermute(array, 'shard', [(i, (i + shift) % n) for i in range(n)])]
  transfers between devices with their start and end apart: 66 -> 66, of which waited for: 31 -> 32; matrix products, arithmetic and copies ran while one was open for 8% -> 8% of each run, Pallas kernels for 15% -> 15%
where the time goes in v4:
time: 339 us; the launch traced here: 336 us
  waiting for transfers between devices  120 us (35%)
  starting transfers between devices  85.8 us (25%)
  Pallas kernels  65.7 us (19%)
  local copies, waits for them, and re-layouts  26.5 us (8%)
  other arithmetic  20.3 us (6%)
  between operations  15.7 us (5%)
    pallas_call x17, Pallas kernels, run(): call(meta, *inputs, *[array for entry in weights for array in entry[0]],...  65.7 us
    ppermute x13, waiting for transfers between devices, swap_chip(): return lax.ppermute(array, 'ctx', [(i, i ^ 2) for i in range(4)])  62.6 us
    ppermute x21, starting transfers between devices, to_shard(): lax.ppermute(array, 'shard', [(i, (i + shift) % n) for i in range(n)])  39.5 us
    ppermute x21, waiting for transfers between devices, to_shard(): lax.ppermute(array, 'shard', [(i, (i + shift) % n) for i in range(n)])  20.9 us
    unnamed x183, local copies, waits for them, and re-layouts  20.9 us
    ppermute x8, waiting for transfers between devices, swap_tp(): return lax.ppermute(array, 'tp', [(0, 1), (1, 0)])  16.8 us
    all_to_all x1, starting transfers between devices, at_once(): self.stack = lax.all_to_all(copies, 'shard', 0, 0, tiled=True)  13.4 us
    ppermute x8, starting transfers between devices, swap_tp(): return lax.ppermute(array, 'tp', [(0, 1), (1, 0)])  13 us
  transfers between devices with their start and end apart: 66, of which 32 were waited for; matrix products, arithmetic and copies ran while one was open for 8% of the time, Pallas kernels for 15%

profile of v4, /device:TPU:0, one launch (start us, length us, event | category | flops | bytes accessed | tf_op | source)
XLA Modules:
  0.0 335.6 jit_solution(2565904819894313062)
XLA Ops:
  9.3 5.1 %collective-permute-start.5 = (s32[1,9]{1,0:T(1,128)S(1)}, s32[1,9]{1,0:T(1,128)S(1)}, u32[]{:S(2)}, u32[]{:S(2)}) collective-permute-start(s32[1,9]{1,0:T(1,128)S(1)} %copy-done.86), channel_id=1, source_target_pairs={{0,24},{8,0},{16,8},{24,16},{1,25},{9,1},{17,9},{25,17},{2,26},{10... | collective-permute-start | bytes 116 | tf_op jit(solution)/shard_map/ppermute | solution.py:451
  43.8 4.9 %collective-permute-done.10 = bf16[48,1536]{1,0:T(8,128)(2,1)S(1)} collective-permute-done((bf16[48,1536]{1,0:T(8,128)(2,1)S(1)}, bf16[48,1536]{1,0:T(8,128)(2,1)S(1)}, u32[]{:S(2)}, u32[]{:S(2)}) %collective-permute-start.10) | collective-permute-done | bytes 147488 | tf_op jit(solution)/shard_map/ppermute | solution.py:451
  53.0 13.4 %all-to-all-start = ((bf16[4,48,1536]{2,1,0:T(8,128)(2,1)}), bf16[4,48,1536]{2,1,0:T(8,128)(2,1)S(1)}, u32[]{:S(2)}, u32[]{:S(2)}) async-start(bf16[4,48,1536]{2,1,0:T(8,128)(2,1)} %broadcast_in_dim.9), calls=%async_computation | async-start | bytes 1179648 | tf_op jit(solution)/shard_map/all_to_all | solution.py:478
  72.0 4.0 %embed.1 = (f32[128,768]{1,0:T(8,128)S(1)}, f32[8,768]{1,0:T(8,128)S(1)}, bf16[128,768]{1,0:T(8,128)(2,1)S(1)}, bf16[128,384]{1,0:T(8,128)(2,1)S(1)}, bf16[128,768]{1,0:T(8,128)(2,1)}) custom-call(s32[10]{0:T(128)S(1)} %pad_add_fusion.3.meta_ref, bf16[128,768]{1,0:T(8,128)(2,1)S(1)} %copy-done.38, bf16[2,384]{1,0:T(2,128)(2,1)S(1)} %copy-done.52, ...), custom_call_target="tpu_custom_call" | custom-call | flops 226492416 | bytes 3075072 | tf_op jit(solution)/shard_map/embed/pallas_call | solution.py:158
  76.3 11.7 %collective-permute-done.18.refs_2_ = bf16[128,768]{1,0:T(8,128)(2,1)S(1)} collective-permute-done((bf16[128,768]{1,0:T(8,128)(2,1)}, bf16[128,768]{1,0:T(8,128)(2,1)S(1)}, u32[]{:S(2)}, u32[]{:S(2)}) %collective-permute-start.18) | collective-permute-done | bytes 196640 | tf_op jit(solution)/shard_map/ppermute | solution.py:442
  89.1 8.1 %all-to-all-done.refs_9_.refs_6_ = bf16[4,48,1536]{2,1,0:T(8,128)(2,1)S(1)} async-done(((bf16[4,48,1536]{2,1,0:T(8,128)(2,1)}), bf16[4,48,1536]{2,1,0:T(8,128)(2,1)S(1)}, u32[]{:S(2)}, u32[]{:S(2)}) %all-to-all-start) | async-done | bytes 589856 | tf_op jit(solution)/shard_map/all_to_all | solution.py:478
  109.9 10.3 %collective-permute-done.25.refs_10_.refs_7_ = bf16[4,48,1536]{2,1,0:T(8,128)(2,1)S(1)} collective-permute-done((bf16[4,48,1536]{2,1,0:T(8,128)(2,1)S(1)}, bf16[4,48,1536]{2,1,0:T(8,128)(2,1)S(1)}, u32[]{:S(2)}, u32[]{:S(2)}) %collective-permute-start.25) | collective-permute-done | bytes 589856 | tf_op jit(solution)/shard_map/ppermute | solution.py:442
  123.1 4.4 %feed.2 = (f32[128,768]{1,0:T(8,128)S(1)}, bf16[128,768]{1,0:T(8,128)(2,1)S(1)}, bf16[128,1536]{1,0:T(8,128)(2,1)S(1)}, f32[128,1536]{1,0:T(8,128)S(1)}, bf16[128,768]{1,0:T(8,128)(2,1)S(1)}) custom-call(s32[10]{0:T(128)S(1)} %pad_add_fusion.3.meta_ref, f32[128,768]{1,0:T(8,128)S(1)} %copy-done.11, bf16[128,768]{1,0:T(8,128)(2,1)S(1)} %get-tuple-element.150.refs_1_, ...), custom_call_target="tpu_custom_call" | custom-call | flops 603979776 | bytes 7501824 | tf_op jit(solution)/shard_map/feed/pallas_call | solution.py:158
  132.1 4.8 %collective-permute-done.28.refs_2_ = bf16[128,768]{1,0:T(8,128)(2,1)S(1)} collective-permute-done((bf16[128,768]{1,0:T(8,128)(2,1)S(1)}, bf16[128,768]{1,0:T(8,128)(2,1)S(1)}, u32[]{:S(2)}, u32[]{:S(2)}) %collective-permute-start.28) | collective-permute-done | bytes 196640 | tf_op jit(solution)/shard_map/ppermute | solution.py:446
  141.5 5.8 %collective-permute-done.29.refs_2_ = bf16[128,768]{1,0:T(8,128)(2,1)S(1)} collective-permute-done((bf16[128,768]{1,0:T(8,128)(2,1)S(1)}, bf16[128,768]{1,0:T(8,128)(2,1)S(1)}, u32[]{:S(2)}, u32[]{:S(2)}) %collective-permute-start.29) | collective-permute-done | bytes 196640 | tf_op jit(solution)/shard_map/ppermute | solution.py:442
  153.6 5.5 %collective-permute-done.32.refs_2_ = bf16[128,768]{1,0:T(8,128)(2,1)S(1)} collective-permute-done((bf16[128,768]{1,0:T(8,128)(2,1)S(1)}, bf16[128,768]{1,0:T(8,128)(2,1)S(1)}, u32[]{:S(2)}, u32[]{:S(2)}) %collective-permute-start.32) | collective-permute-done | bytes 196640 | tf_op jit(solution)/shard_map/ppermute | solution.py:446
  159.1 5.2 %feed.3 = (f32[128,768]{1,0:T(8,128)S(1)}, bf16[128,768]{1,0:T(8,128)(2,1)S(1)}, bf16[128,1536]{1,0:T(8,128)(2,1)S(1)}, f32[128,1536]{1,0:T(8,128)}, bf16[128,76...) custom-call(s32[10]{0:T(128)S(1)} %pad_add_fusion.3.meta_ref, ...), custom_call_target="tpu_custom_call" | custom-call | flops 1207959552 | bytes 8312832 | tf_op jit(solution)/shard_map/feed/pallas_call | solution.py:158
  165.7 4.5 %feed_grad.1 = bf16[768,3072]{1,0:T(8,128)(2,1)S(1)} custom-call(s32[10]{0:T(128)S(1)} %pad_add_fusion.3.meta_ref, bf16[128,768]{1,0:T(8,128)(2,1)S(1)} %get-tuple-element.166.refs_0_, bf16[128,1536]{1,0:T(8,128)(2,1)S(1)} %get-tuple-element.167.refs_1_, bf16[128,768]{1,0:T(8,128)(2,1)S(1)} %copy-done.9, bf16[128,1536]{1,0:T(8,128)(2,1)S(1)} %get-tuple-element.168.refs_3_), custom_call_target="tpu_custom_call" | custom-call | flops 603979776 | bytes 4718592 | tf_op jit(solution)/shard_map/feed_grad/pallas_call | solution.py:158
  174.0 4.9 %collective-permute-done.34.refs_2_ = bf16[128,768]{1,0:T(8,128)(2,1)S(1)} collective-permute-done((bf16[128,768]{1,0:T(8,128)(2,1)}, bf16[128,768]{1,0:T(8,128)(2,1)S(1)}, u32[]{:S(2)}, u32[]{:S(2)}) %collective-permute-start.34) | collective-permute-done | bytes 196640 | tf_op jit(solution)/shard_map/ppermute | solution.py:446
  181.0 4.3 %attend_back.2 = (f32[128,768]{1,0:T(8,128)S(1)}, bf16[128,768]{1,0:T(8,128)(2,1)S(1)}, bf16[128,384]{1,0:T(8,128)(2,1)S(1)}, f32[8,768]{1,0:T(8,128)S(1)}, bf16...) custom-call(s32[10]{0:T(128)S(1)} %pad_add_fusion.3.meta_ref, bf16[128,768]{1,0:T(8,128)(2,1)S(1)} %copy-done.9, ...), custom_call_target="tpu_custom_call" | custom-call | flops 327155712 | bytes 2678784 | tf_op jit(solution)/shard_map/attend_back/pallas_call | solution.py:158
  188.2 6.6 %collective-permute-done.36.refs_3_ = bf16[128,768]{1,0:T(8,128)(2,1)S(1)} collective-permute-done((bf16[128,768]{1,0:T(8,128)(2,1)S(1)}, bf16[128,768]{1,0:T(8,128)(2,1)S(1)}, u32[]{:S(2)}, u32[]{:S(2)}) %collective-permute-start.36) | collective-permute-done | bytes 196640 | tf_op jit(solution)/shard_map/ppermute | solution.py:442
  199.3 4.4 %attn_grad.2 = (bf16[2,4,48,1536]{3,2,1,0:T(8,128)(2,1)S(1)}, bf16[2,4,48,1536]{3,2,1,0:T(8,128)(2,1)}) custom-call(s32[10]{0:T(128)S(1)} %pad_add_fusion.3.meta_ref, bf16[128,768]{1,0:T(8,128)(2,1)S(1)} %copy-done.62, bf16[128,1152]{1,0:T(8,128)(2,1)S(1)} %get-tuple-element.178.refs_1_, bf16[128,768]{1,0:T(8,128)(2,1)S(1)} %get-tuple-element.179.refs_2_, ...), custom_call_target="tpu_custom_call" | custom-call | flops 301989888 | bytes 2359296 | tf_op jit(solution)/shard_map/attn_grad/pallas_call | solution.py:158
  204.5 6.6 %feed_back.1 = (f32[128,768]{1,0:T(8,128)}, bf16[128,768]{1,0:T(8,128)(2,1)}, bf16[128,1536]{1,0:T(8,128)(2,1)}, bf16[128,768]{1,0:T(8,128)(2,1)}, f32[8,768]{1,0:T(8,128)}) custom-call(s32[10]{0:T(128)} %copy-done.46, bf16[128,768]{1,0:T(8,128)(2,1)} %copy-done.41, bf16[128,768]{1,0:T(8,128)(2,1)} %copy-done.76, ...), custom_call_target="tpu_custom_call" | custom-call | flops 603979776 | bytes 6316032 | tf_op jit(solution)/shard_map/feed_back/pallas_call | solution.py:158
  222.7 4.6 %attend_back.3 = (f32[128,768]{1,0:T(8,128)S(1)}, bf16[128,768]{1,0:T(8,128)(2,1)S(1)}, bf16[128,384]{1,0:T(8,128)(2,1)S(1)}, f32[8,768]{1,0:T(8,128)S(1)}, bf16...) custom-call(s32[10]{0:T(128)S(1)} %copy-done.47, f32[128,768]{1,0:T(8,128)S(1)} %copy-done.31, ...), custom_call_target="tpu_custom_call" | custom-call | flops 327155712 | bytes 2875392 | tf_op jit(solution)/shard_map/attend_back/pallas_call | solution.py:158
  240.8 4.5 %attn_grad.3 = (bf16[2,4,48,1536]{3,2,1,0:T(8,128)(2,1)S(1)}, bf16[2,4,48,1536]{3,2,1,0:T(8,128)(2,1)}) custom-call(s32[10]{0:T(128)S(1)} %copy-done.47, bf16[128,768]{1,0:T(8,128)(2,1)S(1)} %copy-done.58, bf16[128,1152]{1,0:T(8,128)(2,1)S(1)} %get-tuple-element.211.refs_1_, bf16[128,768]{1,0:T(8,128)(2,1)S(1)} %get-tuple-element.212.refs_2_, ...), custom_call_target="tpu_custom_call" | custom-call | flops 301989888 | bytes 2359296 | tf_op jit(solution)/shard_map/attn_grad/pallas_call | solution.py:158
  255.3 4.7 %all-to-all-start.1 = ((bf16[4,48,1536]{2,1,0:T(8,128)(2,1)}), bf16[4,48,1536]{2,1,0:T(8,128)(2,1)}, u32[]{:S(2)}, u32[]{:S(2)}) async-start(bf16[4,48,1536]{2,1,0:T(8,128)(2,1)} %fusion.1), calls=%async_computation.2 | async-start | bytes 1179648 | tf_op jit(solution)/shard_map/all_to_all | solution.py:582
  260.0 5.4 %collective-permute-done.45 = bf16[4,48,1536]{2,1,0:T(8,128)(2,1)S(1)} collective-permute-done((bf16[4,48,1536]{2,1,0:T(8,128)(2,1)}, bf16[4,48,1536]{2,1,0:T(8,128)(2,1)S(1)}, u32[]{:S(2)}, u32[]{:S(2)}) %collective-permute-start.45) | collective-permute-done | bytes 589856 | tf_op jit(solution)/shard_map/ppermute | solution.py:442
  282.0 9.0 %collective-permute-done.48 = bf16[4,48,1536]{2,1,0:T(8,128)(2,1)} collective-permute-done((bf16[4,48,1536]{2,1,0:T(8,128)(2,1)S(1)}, bf16[4,48,1536]{2,1,0:T(8,128)(2,1)}, u32[]{:S(2)}, u32[]{:S(2)}) %collective-permute-start.48) | collective-permute-done | bytes 589856 | tf_op jit(solution)/shard_map/ppermute | solution.py:442
  313.4 8.9 %collective-permute-done.54 = bf16[48,1536]{1,0:T(8,128)(2,1)S(1)} collective-permute-done((bf16[48,1536]{1,0:T(8,128)(2,1)S(1)}, bf16[48,1536]{1,0:T(8,128)(2,1)S(1)}, u32[]{:S(2)}, u32[]{:S(2)}) %collective-permute-start.54) | collective-permute-done | bytes 147488 | tf_op jit(solution)/shard_map/ppermute | solution.py:451
  (380 shorter events, 168.5 us)
Async XLA Ops:
  7.2 129.6 %all-gather.2.cloned.1.call-start = ((), (), s32[]{:S(2)}) async-start(), calls=%async_computation.4 | async-start | bytes 7520256 | tf_op jit(solution)/shard_map/all_gather | solution.py:621
  15.4 18.2 %collective-permute-start.2 = (bf16[48,1536]{1,0:T(8,128)(2,1)S(1)}, bf16[48,1536]{1,0:T(8,128)(2,1)S(1)}, u32[]{:S(2)}, u32[]{:S(2)}) collective-permute-start(bf16[48,1536]{1,0:T(8,128)(2,1)S(1)} %pad_maximum_fusion.6), channel_id=1, source_target_pairs={{0,24},{8,0},{16,8},{24,16},{1,25},{9,1},{17,9},{25,17},{2,26},{10... | collective-permute-start | bytes 442376 | tf_op jit(solution)/shard_map/ppermute | solution.py:451
  18.2 15.3 %collective-permute-start.1 = (bf16[48,1536]{1,0:T(8,128)(2,1)S(1)}, bf16[48,1536]{1,0:T(8,128)(2,1)S(1)}, u32[]{:S(2)}, u32[]{:S(2)}) collective-permute-start(bf16[48,1536]{1,0:T(8,128)(2,1)S(1)} %pad_maximum_fusion.6), channel_id=1, source_target_pairs={{0,16},{8,24},{16,0},{24,8},{1,17},{9,25},{17,1},{25,9},{2,18},{10... | collective-permute-start | bytes 442376 | tf_op jit(solution)/shard_map/ppermute | solution.py:451
  33.7 17.9 %collective-permute-start.12 = (bf16[4,48,1536]{2,1,0:T(8,128)(2,1)S(1)}, bf16[4,48,1536]{2,1,0:T(8,128)(2,1)S(1)}, u32[]{:S(2)}, u32[]{:S(2)}) collective-permute-start(bf16[4,48,1536]{2,1,0:T(8,128)(2,1)S(1)} %pad_maximum_fusion.refs_3_.refs_5_.refs_4_), channel_id=1, source_target_pairs={{0,4},{2,6},{4,0},{6,2},{1,5},{3,7},{5,1},{7,3},{8,12},{10,14},{12... | collective-permute-start | bytes 1769480 | tf_op jit(solution)/shard_map/ppermute | solution.py:442
  51.7 20.3 %collective-permute-start.13 = (bf16[4,48,1536]{2,1,0:T(8,128)(2,1)S(1)}, bf16[4,48,1536]{2,1,0:T(8,128)(2,1)S(1)}, u32[]{:S(2)}, u32[]{:S(2)}) collective-permute-start(bf16[4,48,1536]{2,1,0:T(8,128)(2,1)S(1)} %pad_maximum_fusion.refs_3_.refs_5_.refs_4_), channel_id=1, source_target_pairs={{0,2},{2,0},{4,6},{6,4},{1,3},{3,1},{5,7},{7,5},{8,10},{10,8},{12,... | collective-permute-start | bytes 1769480 | tf_op jit(solution)/shard_map/ppermute | solution.py:438
  51.7 20.3 %collective-permute-start.14 = (bf16[4,48,1536]{2,1,0:T(8,128)(2,1)S(1)}, bf16[4,48,1536]{2,1,0:T(8,128)(2,1)S(1)}, u32[]{:S(2)}, u32[]{:S(2)}) collective-permute-start(bf16[4,48,1536]{2,1,0:T(8,128)(2,1)S(1)} %collective-permute-done.12.refs_4_.refs_6_.refs_5_), channel_id=1, source_target_pairs={{0,2},{2,0},{4,6},{6,4},{1,3},{3,1},{5,7},{7,5},{8,10},{10,8},{12,... | collective-permute-start | bytes 1769480 | tf_op jit(solution)/shard_map/ppermute | solution.py:438
  53.0 44.1 %all-to-all-start = ((bf16[4,48,1536]{2,1,0:T(8,128)(2,1)}), bf16[4,48,1536]{2,1,0:T(8,128)(2,1)S(1)}, u32[]{:S(2)}, u32[]{:S(2)}) async-start(bf16[4,48,1536]{2,1,0:T(8,128)(2,1)} %broadcast_in_dim.9), calls=%async_computation | async-start | bytes 1179648 | tf_op jit(solution)/shard_map/all_to_all | solution.py:478
  66.4 206.1 %reduce-scatter.2.cloned.1.call-start = ((), (), s32[]{:S(2)}) async-start(), calls=%async_computation.5 | async-start | bytes 5013504 | tf_op jit(solution)/shard_map/reduce_scatter | solution.py:556
  76.3 20.9 %collective-permute-start.19 = (bf16[128,768]{1,0:T(8,128)(2,1)}, bf16[128,768]{1,0:T(8,128)(2,1)S(1)}, u32[]{:S(2)}, u32[]{:S(2)}) collective-permute-start(bf16[128,768]{1,0:T(8,128)(2,1)} %get-tuple-element.143.refs_1_), channel_id=1, source_target_pairs={{0,2},{2,0},{4,6},{6,4},{1,3},{3,1},{5,7},{7,5},{8,10},{10,8},{12,... | collective-permute-start | bytes 589832 | tf_op jit(solution)/shard_map/ppermute | solution.py:438
  88.9 19.0 %collective-permute-start.22 = (bf16[4,48,1536]{2,1,0:T(8,128)(2,1)}, bf16[4,48,1536]{2,1,0:T(8,128)(2,1)}, u32[]{:S(2)}, u32[]{:S(2)}) collective-permute-start(bf16[4,48,1536]{2,1,0:T(8,128)(2,1)} %pad_maximum_fusion.1.refs_5_.refs_2_), channel_id=1, source_target_pairs={{0,4},{2,6},{4,0},{6,2},{1,5},{3,7},{5,1},{7,3},{8,12},{10,14},{12... | collective-permute-start | bytes 1769480 | tf_op jit(solution)/shard_map/ppermute | solution.py:442
  103.2 17.0 %collective-permute-start.25 = (bf16[4,48,1536]{2,1,0:T(8,128)(2,1)S(1)}, bf16[4,48,1536]{2,1,0:T(8,128)(2,1)S(1)}, u32[]{:S(2)}, u32[]{:S(2)}) collective-permute-start(bf16[4,48,1536]{2,1,0:T(8,128)(2,1)S(1)} %all-to-all-done.refs_9_.refs_6_), channel_id=1, source_target_pairs={{0,4},{2,6},{4,0},{6,2},{1,5},{3,7},{5,1},{7,3},{8,12},{10,14},{12... | collective-permute-start | bytes 1769480 | tf_op jit(solution)/shard_map/ppermute | solution.py:442
  203.7 25.9 %collective-permute-start.39 = (bf16[2,4,48,1536]{3,2,1,0:T(8,128)(2,1)}, bf16[2,4,48,1536]{3,2,1,0:T(8,128)(2,1)}, u32[]{:S(2)}, u32[]{:S(2)}) collective-permute-start(bf16[2,4,48,1536]{3,2,1,0:T(8,128)(2,1)} %get-tuple-element.198), channel_id=1, source_target_pairs={{0,2},{2,0},{4,6},{6,4},{1,3},{3,1},{5,7},{7,5},{8,10},{10,8},{12,... | collective-permute-start | bytes 3538952 | tf_op jit(solution)/shard_map/ppermute | solution.py:438
  231.7 21.2 %collective-permute-start.44 = (bf16[4,48,1536]{2,1,0:T(8,128)(2,1)}, bf16[4,48,1536]{2,1,0:T(8,128)(2,1)}, u32[]{:S(2)}, u32[]{:S(2)}) collective-permute-start(bf16[4,48,1536]{2,1,0:T(8,128)(2,1)} %fusion.2), channel_id=1, source_target_pairs={{0,4},{2,6},{4,0},{6,2},{1,5},{3,7},{5,1},{7,3},{8,12},{10,14},{12... | collective-permute-start | bytes 1769480 | tf_op jit(solution)/shard_map/ppermute | solution.py:442
  246.5 23.2 %collective-permute-start.47 = (bf16[2,4,48,1536]{3,2,1,0:T(8,128)(2,1)}, bf16[2,4,48,1536]{3,2,1,0:T(8,128)(2,1)}, u32[]{:S(2)}, u32[]{:S(2)}) collective-permute-start(bf16[2,4,48,1536]{3,2,1,0:T(8,128)(2,1)} %get-tuple-element.230), channel_id=1, source_target_pairs={{0,2},{2,0},{4,6},{6,4},{1,3},{3,1},{5,7},{7,5},{8,10},{10,8},{12,... | collective-permute-start | bytes 3538952 | tf_op jit(solution)/shard_map/ppermute | solution.py:438
  247.1 18.3 %collective-permute-start.45 = (bf16[4,48,1536]{2,1,0:T(8,128)(2,1)}, bf16[4,48,1536]{2,1,0:T(8,128)(2,1)S(1)}, u32[]{:S(2)}, u32[]{:S(2)}) collective-permute-start(bf16[4,48,1536]{2,1,0:T(8,128)(2,1)} %fusion.3), channel_id=1, source_target_pairs={{0,4},{2,6},{4,0},{6,2},{1,5},{3,7},{5,1},{7,3},{8,12},{10,14},{12... | collective-permute-start | bytes 1769480 | tf_op jit(solution)/shard_map/ppermute | solution.py:442
  247.7 20.3 %collective-permute-start.33 = (bf16[128,768]{1,0:T(8,128)(2,1)S(1)}, bf16[128,768]{1,0:T(8,128)(2,1)S(1)}, u32[]{:S(2)}, u32[]{:S(2)}) collective-permute-start(bf16[128,768]{1,0:T(8,128)(2,1)S(1)} %copy-done.40), channel_id=1, source_target_pairs={{0,1},{1,0},{2,3},{3,2},{4,5},{5,4},{6,7},{7,6},{8,9},{9,8},{10,11... | collective-permute-start | bytes 589832 | tf_op jit(solution)/shard_map/ppermute | solution.py:446
  249.6 28.5 %collective-permute-start.49 = (bf16[4,48,1536]{2,1,0:T(8,128)(2,1)}, bf16[4,48,1536]{2,1,0:T(8,128)(2,1)}, u32[]{:S(2)}, u32[]{:S(2)}) collective-permute-start(bf16[4,48,1536]{2,1,0:T(8,128)(2,1)} %fusion.4), channel_id=1, source_target_pairs={{0,4},{2,6},{4,0},{6,2},{1,5},{3,7},{5,1},{7,3},{8,12},{10,14},{12... | collective-permute-start | bytes 1769480 | tf_op jit(solution)/shard_map/ppermute | solution.py:442
  255.3 46.6 %all-to-all-start.1 = ((bf16[4,48,1536]{2,1,0:T(8,128)(2,1)}), bf16[4,48,1536]{2,1,0:T(8,128)(2,1)}, u32[]{:S(2)}, u32[]{:S(2)}) async-start(bf16[4,48,1536]{2,1,0:T(8,128)(2,1)} %fusion.1), calls=%async_computation.2 | async-start | bytes 1179648 | tf_op jit(solution)/shard_map/all_to_all | solution.py:582
  269.2 23.5 %collective-permute-start.57 = (bf16[32,768]{1,0:T(8,128)(2,1)S(1)}, bf16[32,768]{1,0:T(8,128)(2,1)S(1)}, u32[]{:S(2)}, u32[]{:S(2)}) collective-permute-start(bf16[32,768]{1,0:T(8,128)(2,1)S(1)} %add_convert_fusion.8), channel_id=1, source_target_pairs={{0,4},{2,6},{4,0},{6,2},{1,5},{3,7},{5,1},{7,3},{8,12},{10,14},{12... | collective-permute-start | bytes 147464 | tf_op jit(solution)/shard_map/ppermute | solution.py:442
  270.9 20.1 %collective-permute-start.48 = (bf16[4,48,1536]{2,1,0:T(8,128)(2,1)S(1)}, bf16[4,48,1536]{2,1,0:T(8,128)(2,1)}, u32[]{:S(2)}, u32[]{:S(2)}) collective-permute-start(bf16[4,48,1536]{2,1,0:T(8,128)(2,1)S(1)} %fusion.5), channel_id=1, source_target_pairs={{0,4},{2,6},{4,0},{6,2},{1,5},{3,7},{5,1},{7,3},{8,12},{10,14},{12... | collective-permute-start | bytes 1769480 | tf_op jit(solution)/shard_map/ppermute | solution.py:442
  274.1 16.9 %collective-permute-start.52 = (bf16[48,1536]{1,0:T(8,128)(2,1)S(1)}, bf16[48,1536]{1,0:T(8,128)(2,1)S(1)}, u32[]{:S(2)}, u32[]{:S(2)}) collective-permute-start(bf16[48,1536]{1,0:T(8,128)(2,1)S(1)} %get-tuple-element.274), channel_id=1, source_target_pairs={{0,24},{8,0},{16,8},{24,16},{1,25},{9,1},{17,9},{25,17},{2,26},{10... | collective-permute-start | bytes 442376 | tf_op jit(solution)/shard_map/ppermute | solution.py:451
  297.1 16.3 %collective-permute-start.55 = (bf16[48,1536]{1,0:T(8,128)(2,1)S(1)}, bf16[48,1536]{1,0:T(8,128)(2,1)S(1)}, u32[]{:S(2)}, u32[]{:S(2)}) collective-permute-start(bf16[48,1536]{1,0:T(8,128)(2,1)S(1)} %get-tuple-element.270), channel_id=1, source_target_pairs={{0,24},{8,0},{16,8},{24,16},{1,25},{9,1},{17,9},{25,17},{2,26},{10... | collective-permute-start | bytes 442376 | tf_op jit(solution)/shard_map/ppermute | solution.py:451
  299.9 22.4 %collective-permute-start.54 = (bf16[48,1536]{1,0:T(8,128)(2,1)S(1)}, bf16[48,1536]{1,0:T(8,128)(2,1)S(1)}, u32[]{:S(2)}, u32[]{:S(2)}) collective-permute-start(bf16[48,1536]{1,0:T(8,128)(2,1)S(1)} %get-tuple-element.271), channel_id=1, source_target_pairs={{0,16},{8,24},{16,0},{24,8},{1,17},{9,25},{17,1},{25,9},{2,18},{10... | collective-permute-start | bytes 442376 | tf_op jit(solution)/shard_map/ppermute | solution.py:451
  301.9 25.5 %all-to-all-start.2 = ((bf16[4,48,1536]{2,1,0:T(8,128)(2,1)}), bf16[4,48,1536]{2,1,0:T(8,128)(2,1)S(1)}, u32[]{:S(2)}, u32[]{:S(2)}) async-start(bf16[4,48,1536]{2,1,0:T(8,128)(2,1)} %fusion), calls=%async_computation.3 | async-start | bytes 1179648 | tf_op jit(solution)/shard_map/all_to_all | solution.py:582
  (130 other events, 1408.0 us)
Sparse Core Ops, SparseCore 0:
  33.8 79.2 all-gather.1
  172.6 78.7 reduce-scatter.1

commit v5 on v4

--- a/solution.py
+++ b/solution.py
@@ -17,7 +17,7 @@
 CHUNK = 512
 SPLIT = 3
 VMEM_LIMIT = 46 * 1024 * 1024
-LIMIT_FB = 58 * 1024 * 1024
+LIMIT_FB = 52 * 1024 * 1024
 ORDER = (0, 2, 1, 3)
 
 

time: 339 us -> 334 us (0.985)
  local copies, waits for them, and re-layouts: 26.5 us -> 22.3 us
    unnamed x183 -> x173, local copies, waits for them, and re-layouts: 20.9 us -> 16.7 us
where the time goes in v5:
time: 334 us; the launch traced here: 330 us
  waiting for transfers between devices  121 us (36%)
  starting transfers between devices  86.2 us (26%)
  Pallas kernels  64.4 us (19%)
  local copies, waits for them, and re-layouts  22.3 us (7%)
  other arithmetic  19.3 us (6%)
  between operations  15.6 us (5%)
    pallas_call x17, Pallas kernels, run(): call(meta, *inputs, *[array for entry in weights for array in entry[0]],...  64.4 us
    ppermute x13, waiting for transfers between devices, swap_chip(): return lax.ppermute(array, 'ctx', [(i, i ^ 2) for i in range(4)])  63.1 us
    ppermute x21, starting transfers between devices, to_shard(): lax.ppermute(array, 'shard', [(i, (i + shift) % n) for i in range(n)])  39.8 us
    ppermute x21, waiting for transfers between devices, to_shard(): lax.ppermute(array, 'shard', [(i, (i + shift) % n) for i in range(n)])  21 us
    ppermute x8, waiting for transfers between devices, swap_tp(): return lax.ppermute(array, 'tp', [(0, 1), (1, 0)])  17.2 us
    unnamed x173, local copies, waits for them, and re-layouts  16.7 us
    all_to_all x1, starting transfers between devices, at_once(): self.stack = lax.all_to_all(copies, 'shard', 0, 0, tiled=True)  13.4 us
    ppermute x8, starting transfers between devices, swap_tp(): return lax.ppermute(array, 'tp', [(0, 1), (1, 0)])  12.9 us
  transfers between devices with their start and end apart: 66, of which 32 were waited for; matrix products, arithmetic and copies ran while one was open for 8% of the time, Pallas kernels for 15%

profile of v5, /device:TPU:0, one launch (start us, length us, event | category | flops | bytes accessed | tf_op | source)
XLA Modules:
  0.0 330.3 jit_solution(2804308725351733725)
XLA Ops:
  9.3 5.1 %collective-permute-start.5 = (s32[1,9]{1,0:T(1,128)S(1)}, s32[1,9]{1,0:T(1,128)S(1)}, u32[]{:S(2)}, u32[]{:S(2)}) collective-permute-start(s32[1,9]{1,0:T(1,128)S(1)} %copy-done.81), channel_id=1, source_target_pairs={{0,24},{8,0},{16,8},{24,16},{1,25},{9,1},{17,9},{25,17},{2,26},{10... | collective-permute-start | bytes 116 | tf_op jit(solution)/shard_map/ppermute | solution.py:451
  43.8 4.9 %collective-permute-done.10 = bf16[48,1536]{1,0:T(8,128)(2,1)S(1)} collective-permute-done((bf16[48,1536]{1,0:T(8,128)(2,1)S(1)}, bf16[48,1536]{1,0:T(8,128)(2,1)S(1)}, u32[]{:S(2)}, u32[]{:S(2)}) %collective-permute-start.10) | collective-permute-done | bytes 147488 | tf_op jit(solution)/shard_map/ppermute | solution.py:451
  53.0 13.4 %all-to-all-start = ((bf16[4,48,1536]{2,1,0:T(8,128)(2,1)}), bf16[4,48,1536]{2,1,0:T(8,128)(2,1)S(1)}, u32[]{:S(2)}, u32[]{:S(2)}) async-start(bf16[4,48,1536]{2,1,0:T(8,128)(2,1)} %broadcast_in_dim.9), calls=%async_computation | async-start | bytes 1179648 | tf_op jit(solution)/shard_map/all_to_all | solution.py:478
  72.0 4.0 %embed.1 = (f32[128,768]{1,0:T(8,128)S(1)}, f32[8,768]{1,0:T(8,128)S(1)}, bf16[128,768]{1,0:T(8,128)(2,1)S(1)}, bf16[128,384]{1,0:T(8,128)(2,1)S(1)}, bf16[128,768]{1,0:T(8,128)(2,1)}) custom-call(s32[10]{0:T(128)S(1)} %pad_add_fusion.3.meta_ref, bf16[128,768]{1,0:T(8,128)(2,1)S(1)} %copy-done.33, bf16[2,384]{1,0:T(2,128)(2,1)S(1)} %copy-done.49, ...), custom_call_target="tpu_custom_call" | custom-call | flops 226492416 | bytes 3075072 | tf_op jit(solution)/shard_map/embed/pallas_call | solution.py:158
  76.3 11.7 %collective-permute-done.18.refs_2_ = bf16[128,768]{1,0:T(8,128)(2,1)S(1)} collective-permute-done((bf16[128,768]{1,0:T(8,128)(2,1)}, bf16[128,768]{1,0:T(8,128)(2,1)S(1)}, u32[]{:S(2)}, u32[]{:S(2)}) %collective-permute-start.18) | collective-permute-done | bytes 196640 | tf_op jit(solution)/shard_map/ppermute | solution.py:442
  89.1 8.1 %all-to-all-done.refs_9_.refs_6_ = bf16[4,48,1536]{2,1,0:T(8,128)(2,1)S(1)} async-done(((bf16[4,48,1536]{2,1,0:T(8,128)(2,1)}), bf16[4,48,1536]{2,1,0:T(8,128)(2,1)S(1)}, u32[]{:S(2)}, u32[]{:S(2)}) %all-to-all-start) | async-done | bytes 589856 | tf_op jit(solution)/shard_map/all_to_all | solution.py:478
  109.9 10.3 %collective-permute-done.25.refs_10_.refs_7_ = bf16[4,48,1536]{2,1,0:T(8,128)(2,1)S(1)} collective-permute-done((bf16[4,48,1536]{2,1,0:T(8,128)(2,1)S(1)}, bf16[4,48,1536]{2,1,0:T(8,128)(2,1)S(1)}, u32[]{:S(2)}, u32[]{:S(2)}) %collective-permute-start.25) | collective-permute-done | bytes 589856 | tf_op jit(solution)/shard_map/ppermute | solution.py:442
  123.1 4.4 %feed.2 = (f32[128,768]{1,0:T(8,128)S(1)}, bf16[128,768]{1,0:T(8,128)(2,1)S(1)}, bf16[128,1536]{1,0:T(8,128)(2,1)S(1)}, f32[128,1536]{1,0:T(8,128)S(1)}, bf16[128,768]{1,0:T(8,128)(2,1)S(1)}) custom-call(s32[10]{0:T(128)S(1)} %pad_add_fusion.3.meta_ref, f32[128,768]{1,0:T(8,128)S(1)} %copy-done.11, bf16[128,768]{1,0:T(8,128)(2,1)S(1)} %get-tuple-element.150.refs_1_, ...), custom_call_target="tpu_custom_call" | custom-call | flops 603979776 | bytes 7501824 | tf_op jit(solution)/shard_map/feed/pallas_call | solution.py:158
  132.0 4.8 %collective-permute-done.28.refs_2_ = bf16[128,768]{1,0:T(8,128)(2,1)S(1)} collective-permute-done((bf16[128,768]{1,0:T(8,128)(2,1)S(1)}, bf16[128,768]{1,0:T(8,128)(2,1)S(1)}, u32[]{:S(2)}, u32[]{:S(2)}) %collective-permute-start.28) | collective-permute-done | bytes 196640 | tf_op jit(solution)/shard_map/ppermute | solution.py:446
  141.5 5.8 %collective-permute-done.29.refs_2_ = bf16[128,768]{1,0:T(8,128)(2,1)S(1)} collective-permute-done((bf16[128,768]{1,0:T(8,128)(2,1)S(1)}, bf16[128,768]{1,0:T(8,128)(2,1)S(1)}, u32[]{:S(2)}, u32[]{:S(2)}) %collective-permute-start.29) | collective-permute-done | bytes 196640 | tf_op jit(solution)/shard_map/ppermute | solution.py:442
  153.6 5.5 %collective-permute-done.32.refs_2_ = bf16[128,768]{1,0:T(8,128)(2,1)S(1)} collective-permute-done((bf16[128,768]{1,0:T(8,128)(2,1)S(1)}, bf16[128,768]{1,0:T(8,128)(2,1)S(1)}, u32[]{:S(2)}, u32[]{:S(2)}) %collective-permute-start.32) | collective-permute-done | bytes 196640 | tf_op jit(solution)/shard_map/ppermute | solution.py:446
  159.0 5.2 %feed.3 = (f32[128,768]{1,0:T(8,128)S(1)}, bf16[128,768]{1,0:T(8,128)(2,1)S(1)}, bf16[128,1536]{1,0:T(8,128)(2,1)S(1)}, f32[128,1536]{1,0:T(8,128)}, bf16[128,76...) custom-call(s32[10]{0:T(128)S(1)} %pad_add_fusion.3.meta_ref, ...), custom_call_target="tpu_custom_call" | custom-call | flops 1207959552 | bytes 8312832 | tf_op jit(solution)/shard_map/feed/pallas_call | solution.py:158
  165.0 4.5 %feed_grad.1 = bf16[768,3072]{1,0:T(8,128)(2,1)S(1)} custom-call(s32[10]{0:T(128)S(1)} %pad_add_fusion.3.meta_ref, bf16[128,768]{1,0:T(8,128)(2,1)S(1)} %get-tuple-element.166.refs_0_, bf16[128,1536]{1,0:T(8,128)(2,1)S(1)} %get-tuple-element.167.refs_1_, bf16[128,768]{1,0:T(8,128)(2,1)S(1)} %copy-done.9, bf16[128,1536]{1,0:T(8,128)(2,1)S(1)} %get-tuple-element.168.refs_3_), custom_call_target="tpu_custom_call" | custom-call | flops 603979776 | bytes 4718592 | tf_op jit(solution)/shard_map/feed_grad/pallas_call | solution.py:158
  173.3 4.8 %collective-permute-done.34.refs_2_ = bf16[128,768]{1,0:T(8,128)(2,1)S(1)} collective-permute-done((bf16[128,768]{1,0:T(8,128)(2,1)}, bf16[128,768]{1,0:T(8,128)(2,1)S(1)}, u32[]{:S(2)}, u32[]{:S(2)}) %collective-permute-start.34) | collective-permute-done | bytes 196640 | tf_op jit(solution)/shard_map/ppermute | solution.py:446
  180.3 4.3 %attend_back.2 = (f32[128,768]{1,0:T(8,128)S(1)}, bf16[128,768]{1,0:T(8,128)(2,1)S(1)}, bf16[128,384]{1,0:T(8,128)(2,1)S(1)}, f32[8,768]{1,0:T(8,128)S(1)}, bf16...) custom-call(s32[10]{0:T(128)S(1)} %pad_add_fusion.3.meta_ref, bf16[128,768]{1,0:T(8,128)(2,1)S(1)} %copy-done.9, ...), custom_call_target="tpu_custom_call" | custom-call | flops 327155712 | bytes 2678784 | tf_op jit(solution)/shard_map/attend_back/pallas_call | solution.py:158
  186.9 6.7 %collective-permute-done.36.refs_3_ = bf16[128,768]{1,0:T(8,128)(2,1)S(1)} collective-permute-done((bf16[128,768]{1,0:T(8,128)(2,1)S(1)}, bf16[128,768]{1,0:T(8,128)(2,1)S(1)}, u32[]{:S(2)}, u32[]{:S(2)}) %collective-permute-start.36) | collective-permute-done | bytes 196640 | tf_op jit(solution)/shard_map/ppermute | solution.py:442
  197.7 4.2 %attn_grad.2 = (bf16[2,4,48,1536]{3,2,1,0:T(8,128)(2,1)S(1)}, bf16[2,4,48,1536]{3,2,1,0:T(8,128)(2,1)S(1)}) custom-call(s32[10]{0:T(128)S(1)} %pad_add_fusion.3.meta_ref, bf16[128,768]{1,0:T(8,128)(2,1)S(1)} %copy-done.58, bf16[128,1152]{1,0:T(8,128)(2,1)S(1)} %get-tuple-element.178.refs_1_, bf16[128,768]{1,0:T(8,128)(2,1)S(1)} %get-tuple-element.179.refs_2_, ...), custom_call_target="tpu_custom_call" | custom-call | flops 301989888 | bytes 2359296 | tf_op jit(solution)/shard_map/attn_grad/pallas_call | solution.py:158
  202.4 5.5 %feed_back.1 = (f32[128,768]{1,0:T(8,128)S(1)}, bf16[128,768]{1,0:T(8,128)(2,1)S(1)}, bf16[128,1536]{1,0:T(8,128)(2,1)S(1)}, bf16[128,768]{1,0:T(8,128)(2,1)S(1)}, f32[8,768]{1,0:T(8,128)S(1)}) custom-call(s32[10]{0:T(128)S(1)} %pad_add_fusion.3.meta_ref, bf16[128,768]{1,0:T(8,128)(2,1)S(1)} %get-tuple-element.182.refs_0_, ...), custom_call_target="tpu_custom_call" | custom-call | flops 603979776 | bytes 6316032 | tf_op jit(solution)/shard_map/feed_back/pallas_call | solution.py:158
  217.0 4.6 %attend_back.3 = (f32[128,768]{1,0:T(8,128)S(1)}, bf16[128,768]{1,0:T(8,128)(2,1)S(1)}, bf16[128,384]{1,0:T(8,128)(2,1)S(1)}, f32[8,768]{1,0:T(8,128)S(1)}, bf16...) custom-call(s32[10]{0:T(128)S(1)} %pad_add_fusion.3.meta_ref, f32[128,768]{1,0:T(8,128)S(1)} %get-tuple-element.192.refs_0_, ...), custom_call_target="tpu_custom_call" | custom-call | flops 327155712 | bytes 2875392 | tf_op jit(solution)/shard_map/attend_back/pallas_call | solution.py:158
  234.2 4.4 %attn_grad.3 = (bf16[2,4,48,1536]{3,2,1,0:T(8,128)(2,1)S(1)}, bf16[2,4,48,1536]{3,2,1,0:T(8,128)(2,1)}) custom-call(s32[10]{0:T(128)S(1)} %pad_add_fusion.3.meta_ref, bf16[128,768]{1,0:T(8,128)(2,1)S(1)} %copy-done.54, bf16[128,1152]{1,0:T(8,128)(2,1)S(1)} %get-tuple-element.211.refs_1_, bf16[128,768]{1,0:T(8,128)(2,1)S(1)} %get-tuple-element.212.refs_2_, ...), custom_call_target="tpu_custom_call" | custom-call | flops 301989888 | bytes 2359296 | tf_op jit(solution)/shard_map/attn_grad/pallas_call | solution.py:158
  249.6 4.9 %all-to-all-start.1 = ((bf16[4,48,1536]{2,1,0:T(8,128)(2,1)}), bf16[4,48,1536]{2,1,0:T(8,128)(2,1)}, u32[]{:S(2)}, u32[]{:S(2)}) async-start(bf16[4,48,1536]{2,1,0:T(8,128)(2,1)} %fusion.1), calls=%async_computation.2 | async-start | bytes 1179648 | tf_op jit(solution)/shard_map/all_to_all | solution.py:582
  254.6 5.1 %collective-permute-done.45 = bf16[4,48,1536]{2,1,0:T(8,128)(2,1)S(1)} collective-permute-done((bf16[4,48,1536]{2,1,0:T(8,128)(2,1)}, bf16[4,48,1536]{2,1,0:T(8,128)(2,1)S(1)}, u32[]{:S(2)}, u32[]{:S(2)}) %collective-permute-start.45) | collective-permute-done | bytes 589856 | tf_op jit(solution)/shard_map/ppermute | solution.py:442
  276.3 9.1 %collective-permute-done.48 = bf16[4,48,1536]{2,1,0:T(8,128)(2,1)} collective-permute-done((bf16[4,48,1536]{2,1,0:T(8,128)(2,1)S(1)}, bf16[4,48,1536]{2,1,0:T(8,128)(2,1)}, u32[]{:S(2)}, u32[]{:S(2)}) %collective-permute-start.48) | collective-permute-done | bytes 589856 | tf_op jit(solution)/shard_map/ppermute | solution.py:442
  307.9 9.0 %collective-permute-done.54 = bf16[48,1536]{1,0:T(8,128)(2,1)S(1)} collective-permute-done((bf16[48,1536]{1,0:T(8,128)(2,1)S(1)}, bf16[48,1536]{1,0:T(8,128)(2,1)S(1)}, u32[]{:S(2)}, u32[]{:S(2)}) %collective-permute-start.54) | collective-permute-done | bytes 147488 | tf_op jit(solution)/shard_map/ppermute | solution.py:451
  (370 shorter events, 164.5 us)
Async XLA Ops:
  7.2 129.6 %all-gather.2.cloned.1.call-start = ((), (), s32[]{:S(2)}) async-start(), calls=%async_computation.4 | async-start | bytes 7520256 | tf_op jit(solution)/shard_map/all_gather | solution.py:621
  15.4 18.2 %collective-permute-start.2 = (bf16[48,1536]{1,0:T(8,128)(2,1)S(1)}, bf16[48,1536]{1,0:T(8,128)(2,1)S(1)}, u32[]{:S(2)}, u32[]{:S(2)}) collective-permute-start(bf16[48,1536]{1,0:T(8,128)(2,1)S(1)} %pad_maximum_fusion.6), channel_id=1, source_target_pairs={{0,24},{8,0},{16,8},{24,16},{1,25},{9,1},{17,9},{25,17},{2,26},{10... | collective-permute-start | bytes 442376 | tf_op jit(solution)/shard_map/ppermute | solution.py:451
  18.2 15.3 %collective-permute-start.1 = (bf16[48,1536]{1,0:T(8,128)(2,1)S(1)}, bf16[48,1536]{1,0:T(8,128)(2,1)S(1)}, u32[]{:S(2)}, u32[]{:S(2)}) collective-permute-start(bf16[48,1536]{1,0:T(8,128)(2,1)S(1)} %pad_maximum_fusion.6), channel_id=1, source_target_pairs={{0,16},{8,24},{16,0},{24,8},{1,17},{9,25},{17,1},{25,9},{2,18},{10... | collective-permute-start | bytes 442376 | tf_op jit(solution)/shard_map/ppermute | solution.py:451
  33.7 17.9 %collective-permute-start.12 = (bf16[4,48,1536]{2,1,0:T(8,128)(2,1)S(1)}, bf16[4,48,1536]{2,1,0:T(8,128)(2,1)S(1)}, u32[]{:S(2)}, u32[]{:S(2)}) collective-permute-start(bf16[4,48,1536]{2,1,0:T(8,128)(2,1)S(1)} %pad_maximum_fusion.refs_3_.refs_5_.refs_4_), channel_id=1, source_target_pairs={{0,4},{2,6},{4,0},{6,2},{1,5},{3,7},{5,1},{7,3},{8,12},{10,14},{12... | collective-permute-start | bytes 1769480 | tf_op jit(solution)/shard_map/ppermute | solution.py:442
  51.7 20.3 %collective-permute-start.13 = (bf16[4,48,1536]{2,1,0:T(8,128)(2,1)S(1)}, bf16[4,48,1536]{2,1,0:T(8,128)(2,1)S(1)}, u32[]{:S(2)}, u32[]{:S(2)}) collective-permute-start(bf16[4,48,1536]{2,1,0:T(8,128)(2,1)S(1)} %pad_maximum_fusion.refs_3_.refs_5_.refs_4_), channel_id=1, source_target_pairs={{0,2},{2,0},{4,6},{6,4},{1,3},{3,1},{5,7},{7,5},{8,10},{10,8},{12,... | collective-permute-start | bytes 1769480 | tf_op jit(solution)/shard_map/ppermute | solution.py:438
  51.7 20.3 %collective-permute-start.14 = (bf16[4,48,1536]{2,1,0:T(8,128)(2,1)S(1)}, bf16[4,48,1536]{2,1,0:T(8,128)(2,1)S(1)}, u32[]{:S(2)}, u32[]{:S(2)}) collective-permute-start(bf16[4,48,1536]{2,1,0:T(8,128)(2,1)S(1)} %collective-permute-done.12.refs_4_.refs_6_.refs_5_), channel_id=1, source_target_pairs={{0,2},{2,0},{4,6},{6,4},{1,3},{3,1},{5,7},{7,5},{8,10},{10,8},{12,... | collective-permute-start | bytes 1769480 | tf_op jit(solution)/shard_map/ppermute | solution.py:438
  53.0 44.1 %all-to-all-start = ((bf16[4,48,1536]{2,1,0:T(8,128)(2,1)}), bf16[4,48,1536]{2,1,0:T(8,128)(2,1)S(1)}, u32[]{:S(2)}, u32[]{:S(2)}) async-start(bf16[4,48,1536]{2,1,0:T(8,128)(2,1)} %broadcast_in_dim.9), calls=%async_computation | async-start | bytes 1179648 | tf_op jit(solution)/shard_map/all_to_all | solution.py:478
  66.4 200.4 %reduce-scatter.2.cloned.1.call-start = ((), (), s32[]{:S(2)}) async-start(), calls=%async_computation.5 | async-start | bytes 5013504 | tf_op jit(solution)/shard_map/reduce_scatter | solution.py:556
  76.3 20.9 %collective-permute-start.19 = (bf16[128,768]{1,0:T(8,128)(2,1)}, bf16[128,768]{1,0:T(8,128)(2,1)S(1)}, u32[]{:S(2)}, u32[]{:S(2)}) collective-permute-start(bf16[128,768]{1,0:T(8,128)(2,1)} %get-tuple-element.143.refs_1_), channel_id=1, source_target_pairs={{0,2},{2,0},{4,6},{6,4},{1,3},{3,1},{5,7},{7,5},{8,10},{10,8},{12,... | collective-permute-start | bytes 589832 | tf_op jit(solution)/shard_map/ppermute | solution.py:438
  88.9 19.0 %collective-permute-start.22 = (bf16[4,48,1536]{2,1,0:T(8,128)(2,1)}, bf16[4,48,1536]{2,1,0:T(8,128)(2,1)}, u32[]{:S(2)}, u32[]{:S(2)}) collective-permute-start(bf16[4,48,1536]{2,1,0:T(8,128)(2,1)} %pad_maximum_fusion.1.refs_5_.refs_2_), channel_id=1, source_target_pairs={{0,4},{2,6},{4,0},{6,2},{1,5},{3,7},{5,1},{7,3},{8,12},{10,14},{12... | collective-permute-start | bytes 1769480 | tf_op jit(solution)/shard_map/ppermute | solution.py:442
  103.2 17.0 %collective-permute-start.25 = (bf16[4,48,1536]{2,1,0:T(8,128)(2,1)S(1)}, bf16[4,48,1536]{2,1,0:T(8,128)(2,1)S(1)}, u32[]{:S(2)}, u32[]{:S(2)}) collective-permute-start(bf16[4,48,1536]{2,1,0:T(8,128)(2,1)S(1)} %all-to-all-done.refs_9_.refs_6_), channel_id=1, source_target_pairs={{0,4},{2,6},{4,0},{6,2},{1,5},{3,7},{5,1},{7,3},{8,12},{10,14},{12... | collective-permute-start | bytes 1769480 | tf_op jit(solution)/shard_map/ppermute | solution.py:442
  202.4 21.7 %collective-permute-start.39 = (bf16[2,4,48,1536]{3,2,1,0:T(8,128)(2,1)S(1)}, bf16[2,4,48,1536]{3,2,1,0:T(8,128)(2,1)S(1)}, u32[]{:S(2)}, u32[]{:S(2)}) collective-permute-start(bf16[2,4,48,1536]{3,2,1,0:T(8,128)(2,1)S(1)} %get-tuple-element.198), channel_id=1, source_target_pairs={{0,2},{2,0},{4,6},{6,4},{1,3},{3,1},{5,7},{7,5},{8,10},{10,8},{12,... | collective-permute-start | bytes 3538952 | tf_op jit(solution)/shard_map/ppermute | solution.py:438
  225.2 22.0 %collective-permute-start.44 = (bf16[4,48,1536]{2,1,0:T(8,128)(2,1)}, bf16[4,48,1536]{2,1,0:T(8,128)(2,1)}, u32[]{:S(2)}, u32[]{:S(2)}) collective-permute-start(bf16[4,48,1536]{2,1,0:T(8,128)(2,1)} %fusion.2), channel_id=1, source_target_pairs={{0,4},{2,6},{4,0},{6,2},{1,5},{3,7},{5,1},{7,3},{8,12},{10,14},{12... | collective-permute-start | bytes 1769480 | tf_op jit(solution)/shard_map/ppermute | solution.py:442
  239.7 24.4 %collective-permute-start.47 = (bf16[2,4,48,1536]{3,2,1,0:T(8,128)(2,1)}, bf16[2,4,48,1536]{3,2,1,0:T(8,128)(2,1)}, u32[]{:S(2)}, u32[]{:S(2)}) collective-permute-start(bf16[2,4,48,1536]{3,2,1,0:T(8,128)(2,1)} %get-tuple-element.230), channel_id=1, source_target_pairs={{0,2},{2,0},{4,6},{6,4},{1,3},{3,1},{5,7},{7,5},{8,10},{10,8},{12,... | collective-permute-start | bytes 3538952 | tf_op jit(solution)/shard_map/ppermute | solution.py:438
  240.4 19.3 %collective-permute-start.45 = (bf16[4,48,1536]{2,1,0:T(8,128)(2,1)}, bf16[4,48,1536]{2,1,0:T(8,128)(2,1)S(1)}, u32[]{:S(2)}, u32[]{:S(2)}) collective-permute-start(bf16[4,48,1536]{2,1,0:T(8,128)(2,1)} %fusion.3), channel_id=1, source_target_pairs={{0,4},{2,6},{4,0},{6,2},{1,5},{3,7},{5,1},{7,3},{8,12},{10,14},{12... | collective-permute-start | bytes 1769480 | tf_op jit(solution)/shard_map/ppermute | solution.py:442
  240.8 21.4 %collective-permute-start.33 = (bf16[128,768]{1,0:T(8,128)(2,1)}, bf16[128,768]{1,0:T(8,128)(2,1)S(1)}, u32[]{:S(2)}, u32[]{:S(2)}) collective-permute-start(bf16[128,768]{1,0:T(8,128)(2,1)} %copy-done.34), channel_id=1, source_target_pairs={{0,1},{1,0},{2,3},{3,2},{4,5},{5,4},{6,7},{7,6},{8,9},{9,8},{10,11... | collective-permute-start | bytes 589832 | tf_op jit(solution)/shard_map/ppermute | solution.py:446
  242.5 29.9 %collective-permute-start.49 = (bf16[4,48,1536]{2,1,0:T(8,128)(2,1)}, bf16[4,48,1536]{2,1,0:T(8,128)(2,1)}, u32[]{:S(2)}, u32[]{:S(2)}) collective-permute-start(bf16[4,48,1536]{2,1,0:T(8,128)(2,1)} %fusion.4), channel_id=1, source_target_pairs={{0,4},{2,6},{4,0},{6,2},{1,5},{3,7},{5,1},{7,3},{8,12},{10,14},{12... | collective-permute-start | bytes 1769480 | tf_op jit(solution)/shard_map/ppermute | solution.py:442
  249.6 46.8 %all-to-all-start.1 = ((bf16[4,48,1536]{2,1,0:T(8,128)(2,1)}), bf16[4,48,1536]{2,1,0:T(8,128)(2,1)}, u32[]{:S(2)}, u32[]{:S(2)}) async-start(bf16[4,48,1536]{2,1,0:T(8,128)(2,1)} %fusion.1), calls=%async_computation.2 | async-start | bytes 1179648 | tf_op jit(solution)/shard_map/all_to_all | solution.py:582
  263.5 23.5 %collective-permute-start.57 = (bf16[32,768]{1,0:T(8,128)(2,1)S(1)}, bf16[32,768]{1,0:T(8,128)(2,1)S(1)}, u32[]{:S(2)}, u32[]{:S(2)}) collective-permute-start(bf16[32,768]{1,0:T(8,128)(2,1)S(1)} %add_convert_fusion.8), channel_id=1, source_target_pairs={{0,4},{2,6},{4,0},{6,2},{1,5},{3,7},{5,1},{7,3},{8,12},{10,14},{12... | collective-permute-start | bytes 147464 | tf_op jit(solution)/shard_map/ppermute | solution.py:442
  265.4 20.0 %collective-permute-start.48 = (bf16[4,48,1536]{2,1,0:T(8,128)(2,1)S(1)}, bf16[4,48,1536]{2,1,0:T(8,128)(2,1)}, u32[]{:S(2)}, u32[]{:S(2)}) collective-permute-start(bf16[4,48,1536]{2,1,0:T(8,128)(2,1)S(1)} %fusion.5), channel_id=1, source_target_pairs={{0,4},{2,6},{4,0},{6,2},{1,5},{3,7},{5,1},{7,3},{8,12},{10,14},{12... | collective-permute-start | bytes 1769480 | tf_op jit(solution)/shard_map/ppermute | solution.py:442
  268.4 17.0 %collective-permute-start.52 = (bf16[48,1536]{1,0:T(8,128)(2,1)S(1)}, bf16[48,1536]{1,0:T(8,128)(2,1)S(1)}, u32[]{:S(2)}, u32[]{:S(2)}) collective-permute-start(bf16[48,1536]{1,0:T(8,128)(2,1)S(1)} %get-tuple-element.274), channel_id=1, source_target_pairs={{0,24},{8,0},{16,8},{24,16},{1,25},{9,1},{17,9},{25,17},{2,26},{10... | collective-permute-start | bytes 442376 | tf_op jit(solution)/shard_map/ppermute | solution.py:451
  291.5 16.4 %collective-permute-start.55 = (bf16[48,1536]{1,0:T(8,128)(2,1)S(1)}, bf16[48,1536]{1,0:T(8,128)(2,1)S(1)}, u32[]{:S(2)}, u32[]{:S(2)}) collective-permute-start(bf16[48,1536]{1,0:T(8,128)(2,1)S(1)} %get-tuple-element.270), channel_id=1, source_target_pairs={{0,24},{8,0},{16,8},{24,16},{1,25},{9,1},{17,9},{25,17},{2,26},{10... | collective-permute-start | bytes 442376 | tf_op jit(solution)/shard_map/ppermute | solution.py:451
  294.4 22.5 %collective-permute-start.54 = (bf16[48,1536]{1,0:T(8,128)(2,1)S(1)}, bf16[48,1536]{1,0:T(8,128)(2,1)S(1)}, u32[]{:S(2)}, u32[]{:S(2)}) collective-permute-start(bf16[48,1536]{1,0:T(8,128)(2,1)S(1)} %get-tuple-element.271), channel_id=1, source_target_pairs={{0,16},{8,24},{16,0},{24,8},{1,17},{9,25},{17,1},{25,9},{2,18},{10... | collective-permute-start | bytes 442376 | tf_op jit(solution)/shard_map/ppermute | solution.py:451
  296.4 25.6 %all-to-all-start.2 = ((bf16[4,48,1536]{2,1,0:T(8,128)(2,1)}), bf16[4,48,1536]{2,1,0:T(8,128)(2,1)S(1)}, u32[]{:S(2)}, u32[]{:S(2)}) async-start(bf16[4,48,1536]{2,1,0:T(8,128)(2,1)} %fusion), calls=%async_computation.3 | async-start | bytes 1179648 | tf_op jit(solution)/shard_map/all_to_all | solution.py:582
  (125 other events, 1142.2 us)
Sparse Core Ops, SparseCore 0:
  33.8 79.2 all-gather.1
  171.9 78.8 reduce-scatter.1

commit v6 on v5

--- a/solution.py
+++ b/solution.py
@@ -14,7 +14,7 @@
 F32 = jnp.float32
 BF16 = jnp.bfloat16
 LANES = 128
-CHUNK = 512
+CHUNK = 768
 SPLIT = 3
 VMEM_LIMIT = 46 * 1024 * 1024
 LIMIT_FB = 52 * 1024 * 1024

time: 334 us -> 333 us (level)
  no operation moved by 1% of the time
where the time goes in v6:
time: 333 us; the launch traced here: 330 us
  waiting for transfers between devices  123 us (37%)
  starting transfers between devices  85 us (26%)
  Pallas kernels  63.4 us (19%)
  local copies, waits for them, and re-layouts  22.3 us (7%)
  other arithmetic  19.3 us (6%)
  between operations  15.6 us (5%)
    ppermute x13, waiting for transfers between devices, swap_chip(): return lax.ppermute(array, 'ctx', [(i, i ^ 2) for i in range(4)])  64.3 us
    pallas_call x17, Pallas kernels, run(): call(meta, *inputs, *[array for entry in weights for array in entry[0]],...  63.4 us
    ppermute x21, starting transfers between devices, to_shard(): lax.ppermute(array, 'shard', [(i, (i + shift) % n) for i in range(n)])  38.9 us
    ppermute x21, waiting for transfers between devices, to_shard(): lax.ppermute(array, 'shard', [(i, (i + shift) % n) for i in range(n)])  21 us
    ppermute x8, waiting for transfers between devices, swap_tp(): return lax.ppermute(array, 'tp', [(0, 1), (1, 0)])  17.4 us
    unnamed x173, local copies, waits for them, and re-layouts  16.7 us
    all_to_all x1, starting transfers between devices, at_once(): self.stack = lax.all_to_all(copies, 'shard', 0, 0, tiled=True)  13.4 us
    ppermute x8, starting transfers between devices, swap_tp(): return lax.ppermute(array, 'tp', [(0, 1), (1, 0)])  12.9 us
  transfers between devices with their start and end apart: 66, of which 32 were waited for; matrix products, arithmetic and copies ran while one was open for 8% of the time, Pallas kernels for 15%

profile of v6, /device:TPU:0, one launch (start us, length us, event | category | flops | bytes accessed | tf_op | source)
XLA Modules:
  0.0 329.6 jit_solution(8464816401177393311)
XLA Ops:
  9.3 5.1 %collective-permute-start.5 = (s32[1,9]{1,0:T(1,128)S(1)}, s32[1,9]{1,0:T(1,128)S(1)}, u32[]{:S(2)}, u32[]{:S(2)}) collective-permute-start(s32[1,9]{1,0:T(1,128)S(1)} %copy-done.81), channel_id=1, source_target_pairs={{0,24},{8,0},{16,8},{24,16},{1,25},{9,1},{17,9},{25,17},{2,26},{10... | collective-permute-start | bytes 116 | tf_op jit(solution)/shard_map/ppermute | solution.py:451
  43.8 4.9 %collective-permute-done.10 = bf16[48,1536]{1,0:T(8,128)(2,1)S(1)} collective-permute-done((bf16[48,1536]{1,0:T(8,128)(2,1)S(1)}, bf16[48,1536]{1,0:T(8,128)(2,1)S(1)}, u32[]{:S(2)}, u32[]{:S(2)}) %collective-permute-start.10) | collective-permute-done | bytes 147488 | tf_op jit(solution)/shard_map/ppermute | solution.py:451
  53.0 13.4 %all-to-all-start = ((bf16[4,48,1536]{2,1,0:T(8,128)(2,1)}), bf16[4,48,1536]{2,1,0:T(8,128)(2,1)S(1)}, u32[]{:S(2)}, u32[]{:S(2)}) async-start(bf16[4,48,1536]{2,1,0:T(8,128)(2,1)} %broadcast_in_dim.9), calls=%async_computation | async-start | bytes 1179648 | tf_op jit(solution)/shard_map/all_to_all | solution.py:478
  72.0 4.0 %embed.1 = (f32[128,768]{1,0:T(8,128)S(1)}, f32[8,768]{1,0:T(8,128)S(1)}, bf16[128,768]{1,0:T(8,128)(2,1)S(1)}, bf16[128,384]{1,0:T(8,128)(2,1)S(1)}, bf16[128,768]{1,0:T(8,128)(2,1)}) custom-call(s32[10]{0:T(128)S(1)} %pad_add_fusion.3.meta_ref, bf16[128,768]{1,0:T(8,128)(2,1)S(1)} %copy-done.33, bf16[2,384]{1,0:T(2,128)(2,1)S(1)} %copy-done.49, ...), custom_call_target="tpu_custom_call" | custom-call | flops 226492416 | bytes 3075072 | tf_op jit(solution)/shard_map/embed/pallas_call | solution.py:158
  76.3 11.7 %collective-permute-done.18.refs_2_ = bf16[128,768]{1,0:T(8,128)(2,1)S(1)} collective-permute-done((bf16[128,768]{1,0:T(8,128)(2,1)}, bf16[128,768]{1,0:T(8,128)(2,1)S(1)}, u32[]{:S(2)}, u32[]{:S(2)}) %collective-permute-start.18) | collective-permute-done | bytes 196640 | tf_op jit(solution)/shard_map/ppermute | solution.py:442
  89.1 8.1 %all-to-all-done.refs_9_.refs_6_ = bf16[4,48,1536]{2,1,0:T(8,128)(2,1)S(1)} async-done(((bf16[4,48,1536]{2,1,0:T(8,128)(2,1)}), bf16[4,48,1536]{2,1,0:T(8,128)(2,1)S(1)}, u32[]{:S(2)}, u32[]{:S(2)}) %all-to-all-start) | async-done | bytes 589856 | tf_op jit(solution)/shard_map/all_to_all | solution.py:478
  97.2 3.9 %attend.2 = (bf16[128,768]{1,0:T(8,128)(2,1)S(1)}, bf16[128,384]{1,0:T(8,128)(2,1)S(1)}, f32[8,256]{1,0:T(8,128)S(1)}, bf16[512,768]{1,0:T(8,128)(2,1)S(1)}) custom-call(s32[10]{0:T(128)S(1)} %pad_add_fusion.3.meta_ref, bf16[128,384]{1,0:T(8,128)(2,1)S(1)} %get-tuple-element.149.refs_0_.refs_9_, bf16[128,768]{1,0:T(8,128)(2,1)} %get-tuple-element.143.refs_1_, ...), custom_call_target="tpu_custom_call" | custom-call | flops 176160768 | bytes 2564096 | tf_op jit(solution)/shard_map/attend/pallas_call | solution.py:158
  109.9 10.3 %collective-permute-done.25.refs_10_.refs_7_ = bf16[4,48,1536]{2,1,0:T(8,128)(2,1)S(1)} collective-permute-done((bf16[4,48,1536]{2,1,0:T(8,128)(2,1)S(1)}, bf16[4,48,1536]{2,1,0:T(8,128)(2,1)S(1)}, u32[]{:S(2)}, u32[]{:S(2)}) %collective-permute-start.25) | collective-permute-done | bytes 589856 | tf_op jit(solution)/shard_map/ppermute | solution.py:442
  123.1 4.4 %feed.2 = (f32[128,768]{1,0:T(8,128)S(1)}, bf16[128,768]{1,0:T(8,128)(2,1)S(1)}, bf16[128,1536]{1,0:T(8,128)(2,1)S(1)}, f32[128,1536]{1,0:T(8,128)S(1)}, bf16[128,768]{1,0:T(8,128)(2,1)S(1)}) custom-call(s32[10]{0:T(128)S(1)} %pad_add_fusion.3.meta_ref, f32[128,768]{1,0:T(8,128)S(1)} %copy-done.11, bf16[128,768]{1,0:T(8,128)(2,1)S(1)} %get-tuple-element.150.refs_1_, ...), custom_call_target="tpu_custom_call" | custom-call | flops 603979776 | bytes 7501824 | tf_op jit(solution)/shard_map/feed/pallas_call | solution.py:158
  132.0 4.8 %collective-permute-done.28.refs_2_ = bf16[128,768]{1,0:T(8,128)(2,1)S(1)} collective-permute-done((bf16[128,768]{1,0:T(8,128)(2,1)S(1)}, bf16[128,768]{1,0:T(8,128)(2,1)S(1)}, u32[]{:S(2)}, u32[]{:S(2)}) %collective-permute-start.28) | collective-permute-done | bytes 196640 | tf_op jit(solution)/shard_map/ppermute | solution.py:446
  141.5 5.8 %collective-permute-done.29.refs_2_ = bf16[128,768]{1,0:T(8,128)(2,1)S(1)} collective-permute-done((bf16[128,768]{1,0:T(8,128)(2,1)S(1)}, bf16[128,768]{1,0:T(8,128)(2,1)S(1)}, u32[]{:S(2)}, u32[]{:S(2)}) %collective-permute-start.29) | collective-permute-done | bytes 196640 | tf_op jit(solution)/shard_map/ppermute | solution.py:442
  153.6 5.5 %collective-permute-done.32.refs_2_ = bf16[128,768]{1,0:T(8,128)(2,1)S(1)} collective-permute-done((bf16[128,768]{1,0:T(8,128)(2,1)S(1)}, bf16[128,768]{1,0:T(8,128)(2,1)S(1)}, u32[]{:S(2)}, u32[]{:S(2)}) %collective-permute-start.32) | collective-permute-done | bytes 196640 | tf_op jit(solution)/shard_map/ppermute | solution.py:446
  159.0 5.1 %feed.3 = (f32[128,768]{1,0:T(8,128)S(1)}, bf16[128,768]{1,0:T(8,128)(2,1)S(1)}, bf16[128,1536]{1,0:T(8,128)(2,1)S(1)}, f32[128,1536]{1,0:T(8,128)}, bf16[128,76...) custom-call(s32[10]{0:T(128)S(1)} %pad_add_fusion.3.meta_ref, ...), custom_call_target="tpu_custom_call" | custom-call | flops 1207959552 | bytes 8312832 | tf_op jit(solution)/shard_map/feed/pallas_call | solution.py:158
  164.9 4.6 %feed_grad.1 = bf16[768,3072]{1,0:T(8,128)(2,1)S(1)} custom-call(s32[10]{0:T(128)S(1)} %pad_add_fusion.3.meta_ref, bf16[128,768]{1,0:T(8,128)(2,1)S(1)} %get-tuple-element.166.refs_0_, bf16[128,1536]{1,0:T(8,128)(2,1)S(1)} %get-tuple-element.167.refs_1_, bf16[128,768]{1,0:T(8,128)(2,1)S(1)} %copy-done.9, bf16[128,1536]{1,0:T(8,128)(2,1)S(1)} %get-tuple-element.168.refs_3_), custom_call_target="tpu_custom_call" | custom-call | flops 603979776 | bytes 4718592 | tf_op jit(solution)/shard_map/feed_grad/pallas_call | solution.py:158
  173.3 4.8 %collective-permute-done.34.refs_2_ = bf16[128,768]{1,0:T(8,128)(2,1)S(1)} collective-permute-done((bf16[128,768]{1,0:T(8,128)(2,1)}, bf16[128,768]{1,0:T(8,128)(2,1)S(1)}, u32[]{:S(2)}, u32[]{:S(2)}) %collective-permute-start.34) | collective-permute-done | bytes 196640 | tf_op jit(solution)/shard_map/ppermute | solution.py:446
  180.3 4.3 %attend_back.2 = (f32[128,768]{1,0:T(8,128)S(1)}, bf16[128,768]{1,0:T(8,128)(2,1)S(1)}, bf16[128,384]{1,0:T(8,128)(2,1)S(1)}, f32[8,768]{1,0:T(8,128)S(1)}, bf16...) custom-call(s32[10]{0:T(128)S(1)} %pad_add_fusion.3.meta_ref, bf16[128,768]{1,0:T(8,128)(2,1)S(1)} %copy-done.9, ...), custom_call_target="tpu_custom_call" | custom-call | flops 327155712 | bytes 2678784 | tf_op jit(solution)/shard_map/attend_back/pallas_call | solution.py:158
  186.9 6.7 %collective-permute-done.36.refs_3_ = bf16[128,768]{1,0:T(8,128)(2,1)S(1)} collective-permute-done((bf16[128,768]{1,0:T(8,128)(2,1)S(1)}, bf16[128,768]{1,0:T(8,128)(2,1)S(1)}, u32[]{:S(2)}, u32[]{:S(2)}) %collective-permute-start.36) | collective-permute-done | bytes 196640 | tf_op jit(solution)/shard_map/ppermute | solution.py:442
  202.5 5.5 %feed_back.1 = (f32[128,768]{1,0:T(8,128)S(1)}, bf16[128,768]{1,0:T(8,128)(2,1)S(1)}, bf16[128,1536]{1,0:T(8,128)(2,1)S(1)}, bf16[128,768]{1,0:T(8,128)(2,1)S(1)}, f32[8,768]{1,0:T(8,128)S(1)}) custom-call(s32[10]{0:T(128)S(1)} %pad_add_fusion.3.meta_ref, bf16[128,768]{1,0:T(8,128)(2,1)S(1)} %get-tuple-element.182.refs_0_, ...), custom_call_target="tpu_custom_call" | custom-call | flops 603979776 | bytes 6316032 | tf_op jit(solution)/shard_map/feed_back/pallas_call | solution.py:158
  216.7 4.6 %attend_back.3 = (f32[128,768]{1,0:T(8,128)S(1)}, bf16[128,768]{1,0:T(8,128)(2,1)S(1)}, bf16[128,384]{1,0:T(8,128)(2,1)S(1)}, f32[8,768]{1,0:T(8,128)S(1)}, bf16...) custom-call(s32[10]{0:T(128)S(1)} %pad_add_fusion.3.meta_ref, f32[128,768]{1,0:T(8,128)S(1)} %get-tuple-element.192.refs_0_, ...), custom_call_target="tpu_custom_call" | custom-call | flops 327155712 | bytes 2875392 | tf_op jit(solution)/shard_map/attend_back/pallas_call | solution.py:158
  234.1 4.2 %attn_grad.3 = (bf16[2,4,48,1536]{3,2,1,0:T(8,128)(2,1)S(1)}, bf16[2,4,48,1536]{3,2,1,0:T(8,128)(2,1)}) custom-call(s32[10]{0:T(128)S(1)} %pad_add_fusion.3.meta_ref, bf16[128,768]{1,0:T(8,128)(2,1)S(1)} %copy-done.54, bf16[128,1152]{1,0:T(8,128)(2,1)S(1)} %get-tuple-element.211.refs_1_, bf16[128,768]{1,0:T(8,128)(2,1)S(1)} %get-tuple-element.212.refs_2_, ...), custom_call_target="tpu_custom_call" | custom-call | flops 301989888 | bytes 2359296 | tf_op jit(solution)/shard_map/attn_grad/pallas_call | solution.py:158
  249.4 4.5 %all-to-all-start.1 = ((bf16[4,48,1536]{2,1,0:T(8,128)(2,1)}), bf16[4,48,1536]{2,1,0:T(8,128)(2,1)}, u32[]{:S(2)}, u32[]{:S(2)}) async-start(bf16[4,48,1536]{2,1,0:T(8,128)(2,1)} %fusion.1), calls=%async_computation.2 | async-start | bytes 1179648 | tf_op jit(solution)/shard_map/all_to_all | solution.py:582
  253.9 5.5 %collective-permute-done.45 = bf16[4,48,1536]{2,1,0:T(8,128)(2,1)S(1)} collective-permute-done((bf16[4,48,1536]{2,1,0:T(8,128)(2,1)}, bf16[4,48,1536]{2,1,0:T(8,128)(2,1)S(1)}, u32[]{:S(2)}, u32[]{:S(2)}) %collective-permute-start.45) | collective-permute-done | bytes 589856 | tf_op jit(solution)/shard_map/ppermute | solution.py:442
  275.9 9.3 %collective-permute-done.48 = bf16[4,48,1536]{2,1,0:T(8,128)(2,1)} collective-permute-done((bf16[4,48,1536]{2,1,0:T(8,128)(2,1)S(1)}, bf16[4,48,1536]{2,1,0:T(8,128)(2,1)}, u32[]{:S(2)}, u32[]{:S(2)}) %collective-permute-start.48) | collective-permute-done | bytes 589856 | tf_op jit(solution)/shard_map/ppermute | solution.py:442
  307.3 9.0 %collective-permute-done.54 = bf16[48,1536]{1,0:T(8,128)(2,1)S(1)} collective-permute-done((bf16[48,1536]{1,0:T(8,128)(2,1)S(1)}, bf16[48,1536]{1,0:T(8,128)(2,1)S(1)}, u32[]{:S(2)}, u32[]{:S(2)}) %collective-permute-start.54) | collective-permute-done | bytes 147488 | tf_op jit(solution)/shard_map/ppermute | solution.py:451
  (370 shorter events, 164.1 us)
Async XLA Ops:
  7.2 129.6 %all-gather.2.cloned.1.call-start = ((), (), s32[]{:S(2)}) async-start(), calls=%async_computation.4 | async-start | bytes 7520256 | tf_op jit(solution)/shard_map/all_gather | solution.py:621
  15.4 18.2 %collective-permute-start.2 = (bf16[48,1536]{1,0:T(8,128)(2,1)S(1)}, bf16[48,1536]{1,0:T(8,128)(2,1)S(1)}, u32[]{:S(2)}, u32[]{:S(2)}) collective-permute-start(bf16[48,1536]{1,0:T(8,128)(2,1)S(1)} %pad_maximum_fusion.6), channel_id=1, source_target_pairs={{0,24},{8,0},{16,8},{24,16},{1,25},{9,1},{17,9},{25,17},{2,26},{10... | collective-permute-start | bytes 442376 | tf_op jit(solution)/shard_map/ppermute | solution.py:451
  18.2 15.3 %collective-permute-start.1 = (bf16[48,1536]{1,0:T(8,128)(2,1)S(1)}, bf16[48,1536]{1,0:T(8,128)(2,1)S(1)}, u32[]{:S(2)}, u32[]{:S(2)}) collective-permute-start(bf16[48,1536]{1,0:T(8,128)(2,1)S(1)} %pad_maximum_fusion.6), channel_id=1, source_target_pairs={{0,16},{8,24},{16,0},{24,8},{1,17},{9,25},{17,1},{25,9},{2,18},{10... | collective-permute-start | bytes 442376 | tf_op jit(solution)/shard_map/ppermute | solution.py:451
  33.7 17.9 %collective-permute-start.12 = (bf16[4,48,1536]{2,1,0:T(8,128)(2,1)S(1)}, bf16[4,48,1536]{2,1,0:T(8,128)(2,1)S(1)}, u32[]{:S(2)}, u32[]{:S(2)}) collective-permute-start(bf16[4,48,1536]{2,1,0:T(8,128)(2,1)S(1)} %pad_maximum_fusion.refs_3_.refs_5_.refs_4_), channel_id=1, source_target_pairs={{0,4},{2,6},{4,0},{6,2},{1,5},{3,7},{5,1},{7,3},{8,12},{10,14},{12... | collective-permute-start | bytes 1769480 | tf_op jit(solution)/shard_map/ppermute | solution.py:442
  51.7 20.3 %collective-permute-start.13 = (bf16[4,48,1536]{2,1,0:T(8,128)(2,1)S(1)}, bf16[4,48,1536]{2,1,0:T(8,128)(2,1)S(1)}, u32[]{:S(2)}, u32[]{:S(2)}) collective-permute-start(bf16[4,48,1536]{2,1,0:T(8,128)(2,1)S(1)} %pad_maximum_fusion.refs_3_.refs_5_.refs_4_), channel_id=1, source_target_pairs={{0,2},{2,0},{4,6},{6,4},{1,3},{3,1},{5,7},{7,5},{8,10},{10,8},{12,... | collective-permute-start | bytes 1769480 | tf_op jit(solution)/shard_map/ppermute | solution.py:438
  51.7 20.3 %collective-permute-start.14 = (bf16[4,48,1536]{2,1,0:T(8,128)(2,1)S(1)}, bf16[4,48,1536]{2,1,0:T(8,128)(2,1)S(1)}, u32[]{:S(2)}, u32[]{:S(2)}) collective-permute-start(bf16[4,48,1536]{2,1,0:T(8,128)(2,1)S(1)} %collective-permute-done.12.refs_4_.refs_6_.refs_5_), channel_id=1, source_target_pairs={{0,2},{2,0},{4,6},{6,4},{1,3},{3,1},{5,7},{7,5},{8,10},{10,8},{12,... | collective-permute-start | bytes 1769480 | tf_op jit(solution)/shard_map/ppermute | solution.py:438
  53.0 44.1 %all-to-all-start = ((bf16[4,48,1536]{2,1,0:T(8,128)(2,1)}), bf16[4,48,1536]{2,1,0:T(8,128)(2,1)S(1)}, u32[]{:S(2)}, u32[]{:S(2)}) async-start(bf16[4,48,1536]{2,1,0:T(8,128)(2,1)} %broadcast_in_dim.9), calls=%async_computation | async-start | bytes 1179648 | tf_op jit(solution)/shard_map/all_to_all | solution.py:478
  66.4 200.2 %reduce-scatter.2.cloned.1.call-start = ((), (), s32[]{:S(2)}) async-start(), calls=%async_computation.5 | async-start | bytes 5013504 | tf_op jit(solution)/shard_map/reduce_scatter | solution.py:556
  76.3 20.9 %collective-permute-start.19 = (bf16[128,768]{1,0:T(8,128)(2,1)}, bf16[128,768]{1,0:T(8,128)(2,1)S(1)}, u32[]{:S(2)}, u32[]{:S(2)}) collective-permute-start(bf16[128,768]{1,0:T(8,128)(2,1)} %get-tuple-element.143.refs_1_), channel_id=1, source_target_pairs={{0,2},{2,0},{4,6},{6,4},{1,3},{3,1},{5,7},{7,5},{8,10},{10,8},{12,... | collective-permute-start | bytes 589832 | tf_op jit(solution)/shard_map/ppermute | solution.py:438
  88.9 19.0 %collective-permute-start.22 = (bf16[4,48,1536]{2,1,0:T(8,128)(2,1)}, bf16[4,48,1536]{2,1,0:T(8,128)(2,1)}, u32[]{:S(2)}, u32[]{:S(2)}) collective-permute-start(bf16[4,48,1536]{2,1,0:T(8,128)(2,1)} %pad_maximum_fusion.1.refs_5_.refs_2_), channel_id=1, source_target_pairs={{0,4},{2,6},{4,0},{6,2},{1,5},{3,7},{5,1},{7,3},{8,12},{10,14},{12... | collective-permute-start | bytes 1769480 | tf_op jit(solution)/shard_map/ppermute | solution.py:442
  103.2 17.0 %collective-permute-start.25 = (bf16[4,48,1536]{2,1,0:T(8,128)(2,1)S(1)}, bf16[4,48,1536]{2,1,0:T(8,128)(2,1)S(1)}, u32[]{:S(2)}, u32[]{:S(2)}) collective-permute-start(bf16[4,48,1536]{2,1,0:T(8,128)(2,1)S(1)} %all-to-all-done.refs_9_.refs_6_), channel_id=1, source_target_pairs={{0,4},{2,6},{4,0},{6,2},{1,5},{3,7},{5,1},{7,3},{8,12},{10,14},{12... | collective-permute-start | bytes 1769480 | tf_op jit(solution)/shard_map/ppermute | solution.py:442
  202.5 21.2 %collective-permute-start.39 = (bf16[2,4,48,1536]{3,2,1,0:T(8,128)(2,1)S(1)}, bf16[2,4,48,1536]{3,2,1,0:T(8,128)(2,1)S(1)}, u32[]{:S(2)}, u32[]{:S(2)}) collective-permute-start(bf16[2,4,48,1536]{3,2,1,0:T(8,128)(2,1)S(1)} %get-tuple-element.198), channel_id=1, source_target_pairs={{0,2},{2,0},{4,6},{6,4},{1,3},{3,1},{5,7},{7,5},{8,10},{10,8},{12,... | collective-permute-start | bytes 3538952 | tf_op jit(solution)/shard_map/ppermute | solution.py:438
  224.7 22.2 %collective-permute-start.44 = (bf16[4,48,1536]{2,1,0:T(8,128)(2,1)}, bf16[4,48,1536]{2,1,0:T(8,128)(2,1)}, u32[]{:S(2)}, u32[]{:S(2)}) collective-permute-start(bf16[4,48,1536]{2,1,0:T(8,128)(2,1)} %fusion.2), channel_id=1, source_target_pairs={{0,4},{2,6},{4,0},{6,2},{1,5},{3,7},{5,1},{7,3},{8,12},{10,14},{12... | collective-permute-start | bytes 1769480 | tf_op jit(solution)/shard_map/ppermute | solution.py:442
  239.4 24.3 %collective-permute-start.47 = (bf16[2,4,48,1536]{3,2,1,0:T(8,128)(2,1)}, bf16[2,4,48,1536]{3,2,1,0:T(8,128)(2,1)}, u32[]{:S(2)}, u32[]{:S(2)}) collective-permute-start(bf16[2,4,48,1536]{3,2,1,0:T(8,128)(2,1)} %get-tuple-element.230), channel_id=1, source_target_pairs={{0,2},{2,0},{4,6},{6,4},{1,3},{3,1},{5,7},{7,5},{8,10},{10,8},{12,... | collective-permute-start | bytes 3538952 | tf_op jit(solution)/shard_map/ppermute | solution.py:438
  240.0 19.4 %collective-permute-start.45 = (bf16[4,48,1536]{2,1,0:T(8,128)(2,1)}, bf16[4,48,1536]{2,1,0:T(8,128)(2,1)S(1)}, u32[]{:S(2)}, u32[]{:S(2)}) collective-permute-start(bf16[4,48,1536]{2,1,0:T(8,128)(2,1)} %fusion.3), channel_id=1, source_target_pairs={{0,4},{2,6},{4,0},{6,2},{1,5},{3,7},{5,1},{7,3},{8,12},{10,14},{12... | collective-permute-start | bytes 1769480 | tf_op jit(solution)/shard_map/ppermute | solution.py:442
  240.4 21.5 %collective-permute-start.33 = (bf16[128,768]{1,0:T(8,128)(2,1)}, bf16[128,768]{1,0:T(8,128)(2,1)S(1)}, u32[]{:S(2)}, u32[]{:S(2)}) collective-permute-start(bf16[128,768]{1,0:T(8,128)(2,1)} %copy-done.34), channel_id=1, source_target_pairs={{0,1},{1,0},{2,3},{3,2},{4,5},{5,4},{6,7},{7,6},{8,9},{9,8},{10,11... | collective-permute-start | bytes 589832 | tf_op jit(solution)/shard_map/ppermute | solution.py:446
  241.8 30.3 %collective-permute-start.49 = (bf16[4,48,1536]{2,1,0:T(8,128)(2,1)}, bf16[4,48,1536]{2,1,0:T(8,128)(2,1)}, u32[]{:S(2)}, u32[]{:S(2)}) collective-permute-start(bf16[4,48,1536]{2,1,0:T(8,128)(2,1)} %fusion.4), channel_id=1, source_target_pairs={{0,4},{2,6},{4,0},{6,2},{1,5},{3,7},{5,1},{7,3},{8,12},{10,14},{12... | collective-permute-start | bytes 1769480 | tf_op jit(solution)/shard_map/ppermute | solution.py:442
  249.4 46.4 %all-to-all-start.1 = ((bf16[4,48,1536]{2,1,0:T(8,128)(2,1)}), bf16[4,48,1536]{2,1,0:T(8,128)(2,1)}, u32[]{:S(2)}, u32[]{:S(2)}) async-start(bf16[4,48,1536]{2,1,0:T(8,128)(2,1)} %fusion.1), calls=%async_computation.2 | async-start | bytes 1179648 | tf_op jit(solution)/shard_map/all_to_all | solution.py:582
  263.2 23.5 %collective-permute-start.57 = (bf16[32,768]{1,0:T(8,128)(2,1)S(1)}, bf16[32,768]{1,0:T(8,128)(2,1)S(1)}, u32[]{:S(2)}, u32[]{:S(2)}) collective-permute-start(bf16[32,768]{1,0:T(8,128)(2,1)S(1)} %add_convert_fusion.8), channel_id=1, source_target_pairs={{0,4},{2,6},{4,0},{6,2},{1,5},{3,7},{5,1},{7,3},{8,12},{10,14},{12... | collective-permute-start | bytes 147464 | tf_op jit(solution)/shard_map/ppermute | solution.py:442
  264.9 20.2 %collective-permute-start.48 = (bf16[4,48,1536]{2,1,0:T(8,128)(2,1)S(1)}, bf16[4,48,1536]{2,1,0:T(8,128)(2,1)}, u32[]{:S(2)}, u32[]{:S(2)}) collective-permute-start(bf16[4,48,1536]{2,1,0:T(8,128)(2,1)S(1)} %fusion.5), channel_id=1, source_target_pairs={{0,4},{2,6},{4,0},{6,2},{1,5},{3,7},{5,1},{7,3},{8,12},{10,14},{12... | collective-permute-start | bytes 1769480 | tf_op jit(solution)/shard_map/ppermute | solution.py:442
  268.1 17.0 %collective-permute-start.52 = (bf16[48,1536]{1,0:T(8,128)(2,1)S(1)}, bf16[48,1536]{1,0:T(8,128)(2,1)S(1)}, u32[]{:S(2)}, u32[]{:S(2)}) collective-permute-start(bf16[48,1536]{1,0:T(8,128)(2,1)S(1)} %get-tuple-element.274), channel_id=1, source_target_pairs={{0,24},{8,0},{16,8},{24,16},{1,25},{9,1},{17,9},{25,17},{2,26},{10... | collective-permute-start | bytes 442376 | tf_op jit(solution)/shard_map/ppermute | solution.py:451
  291.1 16.2 %collective-permute-start.55 = (bf16[48,1536]{1,0:T(8,128)(2,1)S(1)}, bf16[48,1536]{1,0:T(8,128)(2,1)S(1)}, u32[]{:S(2)}, u32[]{:S(2)}) collective-permute-start(bf16[48,1536]{1,0:T(8,128)(2,1)S(1)} %get-tuple-element.270), channel_id=1, source_target_pairs={{0,24},{8,0},{16,8},{24,16},{1,25},{9,1},{17,9},{25,17},{2,26},{10... | collective-permute-start | bytes 442376 | tf_op jit(solution)/shard_map/ppermute | solution.py:451
  293.8 22.5 %collective-permute-start.54 = (bf16[48,1536]{1,0:T(8,128)(2,1)S(1)}, bf16[48,1536]{1,0:T(8,128)(2,1)S(1)}, u32[]{:S(2)}, u32[]{:S(2)}) collective-permute-start(bf16[48,1536]{1,0:T(8,128)(2,1)S(1)} %get-tuple-element.271), channel_id=1, source_target_pairs={{0,16},{8,24},{16,0},{24,8},{1,17},{9,25},{17,1},{25,9},{2,18},{10... | collective-permute-start | bytes 442376 | tf_op jit(solution)/shard_map/ppermute | solution.py:451
  295.8 25.6 %all-to-all-start.2 = ((bf16[4,48,1536]{2,1,0:T(8,128)(2,1)}), bf16[4,48,1536]{2,1,0:T(8,128)(2,1)S(1)}, u32[]{:S(2)}, u32[]{:S(2)}) async-start(bf16[4,48,1536]{2,1,0:T(8,128)(2,1)} %fusion), calls=%async_computation.3 | async-start | bytes 1179648 | tf_op jit(solution)/shard_map/all_to_all | solution.py:582
  (125 other events, 1139.9 us)
Sparse Core Ops, SparseCore 0:
  33.8 79.2 all-gather.1
  171.9 78.7 reduce-scatter.1
